TPU v7x, 512 devices: a whole 4x4x16 slice. The times are simulated.
512 devices in a mesh: row: 64 (over y_lo, z, core), col: 8 (over x, y_hi).
Axes of the slice: x: 4, y: 4 (y_hi: 2, y_lo: 2; y = y_hi * 2 + y_lo), z: 16, core: 2. Of those that a mesh axis runs over, the one named last changes fastest.
Arguments:
- sensitivity: float32 [16384, 16384], P('row', 'col'), as said below
- injections: bfloat16 [16384, 2048], P('col', 'row'), may hold values from -6 to 6
- from_node: int32 [64], replicated, may hold values from 0 to 16383, as said below
- to_node: int32 [64], replicated, may hold values from 1 to 16382, as said below
- switch_flags: int32 [64], replicated, may hold values 0 or 1
- impedance: float32 [64], replicated, may hold values from 0.5 to 2
Outputs:
- voltages: float32 [16384, 2048], P('row', 'col')
Inputs may be any that keep to these rules, and one draw needn't show every extreme that they name: from_node and to_node together hold 128 distinct nodes; from_node holds nodes 0 and 16383. to_node holds no node of from_node, and no node twice; it holds nodes 1 and 16382. sensitivity is symmetric with diagonal entries of 0.5 to 1.5.
All inputs are finite; a program needn't handle non-finite values.
Results may differ from a plain program's by a relative error of at most 0.0008.
Values may be sent and summed in bfloat16 or wider, within the bound.
No kernel may reach another device: no remote copies, remote signals or barrier semaphores. Data moves between devices by JAX's collectives and lax.ppermute only.
A program may use at most 64 MiB of HBM per device.

v0:
```python
import jax
import jax.numpy as jnp
from jax import lax
from jax.sharding import PartitionSpec as P


def incidence_of(node_ids, from_node, to_node):
    plus = (node_ids[:, None] == from_node[None, :]).astype(jnp.float32)
    minus = (node_ids[:, None] == to_node[None, :]).astype(jnp.float32)
    return plus - minus


def on_device(sensitivity, injections, from_node, to_node, switch_flags, impedance):
    high = lax.Precision.HIGHEST
    row_count = sensitivity.shape[0]
    col_count = sensitivity.shape[1]
    row_base = lax.axis_index("row") * row_count
    col_base = lax.axis_index("col") * col_count
    col_select = incidence_of(col_base + jnp.arange(col_count, dtype=jnp.int32), from_node, to_node)
    row_select = incidence_of(row_base + jnp.arange(row_count, dtype=jnp.int32), from_node, to_node)
    branch_part = jnp.dot(
        sensitivity, col_select, precision=high, preferred_element_type=jnp.float32
    )
    columns = lax.psum(branch_part.astype(jnp.bfloat16), "col").astype(jnp.float32)
    cap_part = jnp.dot(row_select.T, columns, precision=high, preferred_element_type=jnp.float32)
    reach_diag = jnp.diag(impedance * (1.0 + 3.0 * switch_flags.astype(jnp.float32)))
    loads = lax.all_gather(injections, "row", axis=1, tiled=True).astype(jnp.float32)
    partial_terms = jnp.dot(sensitivity, loads, precision=high, preferred_element_type=jnp.float32)
    summed = lax.psum_scatter(partial_terms, "col", scatter_dimension=1, tiled=True)
    ends_part = jnp.dot(row_select.T, summed, precision=high, preferred_element_type=jnp.float32)
    cap_sum = lax.psum(cap_part, "row")
    ends = lax.psum(ends_part, "row")
    factor = jnp.linalg.cholesky(cap_sum + reach_diag)
    weights = jax.scipy.linalg.cho_solve((factor, True), ends)
    return summed - jnp.dot(columns, weights, precision=high, preferred_element_type=jnp.float32)


def solution(mesh):
    placed = (P("row", "col"), P("col", "row"), P(), P(), P(), P())
    return jax.shard_map(
        on_device, mesh=mesh, in_specs=placed, out_specs=P("row", "col"), check_vma=False
    )
```

profile of v0, /device:TPU:1, one launch (start us, length us, event | category | flops | bytes accessed | tf_op | source)
XLA Modules:
  0.0 772.7 jit_solution(15811575903335097937)
XLA Ops:
  6.5 0.0 copy-start
  6.5 0.0 all-gather.2.cloned.1.call-start
  6.5 0.7 all-gather.2.cloned.1.call-update
  7.3 0.0 reduce-scatter.2.cloned.1.call-start
  7.3 136.8 %all-gather.2.cloned.1.call-done = bf16[2048,2048]{0,1:T(8,128)(2,1)} async-done(((bf16[2048,32]{0,1:T(8,128)(2,1)}), bf16[2048,2048]{0,1:T(8,128)(2,1)}) %all-gather.2.cloned.1.call-update) | async-done | bytes 8388624 | tf_op jit(solution)/shard_map/all_gather | solution.py:27
  144.1 0.0 copy-done
  144.1 10.1 %fusion.27 = f32[256,2048]{1,0:T(8,128)} fusion(f32[256,2048]{1,0:T(8,128)S(1)} %copy-done, bf16[2048,2048]{0,1:T(8,128)(2,1)} %all-gather.2.cloned.1.call-done), kind=kOutput, calls=%fused_computation.40 | convolution fusion | flops 12884901888 | bytes 12582912 | tf_op jit(solution)/shard_map/dot_general | solution.py:28
  154.2 0.0 copy-start.1
  154.3 0.0 copy-start.2
  154.3 0.0 reduce-scatter.2.cloned.1.call-update
  154.3 0.0 all-reduce.2.cloned.1.call-start
  154.4 0.5 copy-done.1
  154.9 0.0 copy-done.2
  154.9 2.5 fusion
  157.4 34.1 %psum.21 = bf16[256,64]{0,1:T(8,128)(2,1)S(1)} all-reduce(bf16[256,64]{0,1:T(8,128)(2,1)S(1)} %fusion), channel_id=1, replica_groups=mesh['row'=64,'col'=8] {'col'}, use_global_device_ids=true, to_apply=%region_1.2 | all-reduce | flops 16384 | bytes 65536 | tf_op jit(solution)/shard_map/psum | solution.py:24
  191.5 0.3 fusion.10
  191.9 210.6 %psum.22 = f32[64,64]{1,0:T(8,128)S(1)} all-reduce(f32[64,64]{1,0:T(8,128)S(1)} %fusion.10), channel_id=1, replica_groups=mesh['row'=64,'col'=8] {'row'}, use_global_device_ids=true, to_apply=%region_2.3 | all-reduce | flops 4096 | bytes 32768 | tf_op jit(solution)/shard_map/psum | solution.py:31
  402.4 0.0 copy-done.3
  402.4 0.0 copy-done.4
  402.4 0.1 select_add_fusion
  402.5 0.1 copy.7
  402.6 0.1 fusion.26
  402.7 5.9 cholesky.16
  408.6 0.7 compare_reduce_fusion
  409.3 2.0 fusion.9
  411.3 0.0 all-reduce.2.cloned.1.call-update
  411.3 0.7 fusion.21
  412.0 4.9 custom-call.10
  416.9 346.0 %all-reduce.2.cloned.1.call-done = f32[64,256]{1,0:T(8,128)} async-done(((f32[64,256]{1,0:T(8,128)}), f32[64,256]{1,0:T(8,128)}) %all-reduce.2.cloned.1.call-update) | async-done | bytes 65552 | tf_op jit(solution)/shard_map/psum | solution.py:32
  762.9 1.1 fusion.24
  764.0 0.2 fusion.22
  764.2 2.0 convolution_subtract_fusion
  (7 shorter events, 0.0 us)
Async XLA Ops:
  6.5 137.6 %copy-start = (f32[256,2048]{1,0:T(8,128)S(1)}, f32[256,2048]{1,0:T(8,128)}, u32[]{:S(2)}) copy-start(f32[256,2048]{1,0:T(8,128)} %param.6) | copy-start | bytes 6291460
  6.5 137.6 %all-gather.2.cloned.1.call-start = ((), (), s32[]{:S(2)}) async-start(), calls=%async_computation.1 | async-start | bytes 8519680 | tf_op jit(solution)/shard_map/all_gather | solution.py:27
  7.3 402.0 %reduce-scatter.2.cloned.1.call-start = ((), (), s32[]{:S(2)}) async-start(), calls=%async_computation.2 | async-start | bytes 2359296 | tf_op jit(solution)/shard_map/reduce_scatter | solution.py:29
  154.2 0.7 copy-start.1
  154.3 0.7 copy-start.2
  154.3 248.2 %copy-start.3 = (f32[64]{0:T(128)S(1)}, f32[64]{0:T(128)}, u32[]{:S(2)}) copy-start(f32[64]{0:T(128)} %param.11) | copy-start | bytes 772
  154.3 248.2 %copy-start.4 = (s32[64]{0:T(128)S(1)}, s32[64]{0:T(128)}, u32[]{:S(2)}) copy-start(s32[64]{0:T(128)} %param.10) | copy-start | bytes 772
  154.3 608.6 %all-reduce.2.cloned.1.call-start = ((), (), s32[]{:S(2)}) async-start(), calls=%async_computation.3 | async-start | bytes 131072 | tf_op jit(solution)/shard_map/psum | solution.py:32
Sparse Core Ops, SparseCore 0:
  9.5 134.5 all-gather.1
  154.4 85.2 reduce-scatter.1
  411.5 351.4 all-reduce.1
where the time goes:
time: 773 us
  waiting for transfers between devices  484 us (63%)
  blocking collectives  245 us (32%)
  matrix products  18.2 us (2%)
  between operations  13.2 us (2%)
  other arithmetic  12.4 us (2%)
    psum x1, waiting for transfers between devices, on_device(): ends = lax.psum(ends_part, 'row')  346 us
    psum x1, blocking collectives, on_device(): cap_sum = lax.psum(cap_part, 'row')  211 us
    all_gather x1, waiting for transfers between devices, on_device(): lax.all_gather(injections, 'row', axis=1, tiled=True).astype(jnp.float32)  137 us
    psum x1, blocking collectives, on_device(): lax.psum(branch_part.astype(jnp.bfloat16), 'col').astype(jnp.float32)  34.1 us
  transfers between devices with their start and end apart: 3, of which 2 were waited for; matrix products, arithmetic and copies ran while one was open for 2% of the time, Pallas kernels for 0%

commit v1 on v0

v1 whole, which is shorter than its diff:
```python
import jax
import jax.numpy as jnp
from jax import lax
from jax.sharding import PartitionSpec as P

HIGH = lax.Precision.HIGHEST
F32 = jnp.float32
BF16 = jnp.bfloat16

Y, Z, CORES = 2, 16, 2
COLS = 8
BR = 64


def row_of(y, z, core):
    return y * Z * CORES + z * CORES + core


ROWS = [(y, z, core) for y in range(Y) for z in range(Z) for core in range(CORES)]
OTHER_CORE = [(row_of(y, z, k), row_of(y, z, 1 - k)) for y, z, k in ROWS]
OTHER_Y = [(row_of(y, z, k), row_of(1 - y, z, k)) for y, z, k in ROWS]
ALONG_Z = [[row_of(y, z, k) for z in range(Z)] for y in range(Y) for k in range(CORES)]
TO_COLUMN = [
    ((8 * a + b) * COLS + c, (8 * b + c) * COLS + a)
    for a in range(8) for b in range(8) for c in range(8)
]


def incidence_of(node_ids, from_node, to_node):
    plus = (node_ids[:, None] == from_node[None, :]).astype(BF16)
    minus = (node_ids[:, None] == to_node[None, :]).astype(BF16)
    return plus - minus


def split(values):
    high = lax.reduce_precision(values, 8, 7)
    return high.astype(BF16), (values - high).astype(BF16)


def in_order(position, mine, other):
    return jnp.where(position == 0, jnp.stack([mine, other]), jnp.stack([other, mine]))


def nt(left, right):
    return lax.dot_general(left, right, (((1,), (1,)), ((), ())), preferred_element_type=F32)


def on_device(sensitivity, injections, from_node, to_node, switch_flags, impedance):
    row_count, col_count = sensitivity.shape
    row = lax.axis_index("row")
    col = lax.axis_index("col")
    y, core = row // (Z * CORES), row % CORES
    slots = injections.shape[1]

    loads = injections.T
    other_loads = lax.ppermute(loads, "row", OTHER_Y)
    pair = in_order(y, loads, other_loads)
    gathered = lax.all_gather(pair, "row", axis_index_groups=ALONG_Z, axis=0)

    other_rows = lax.ppermute(sensitivity, "row", OTHER_CORE)

    high, low = split(sensitivity)
    col_select = incidence_of(col * col_count + jnp.arange(col_count, dtype=jnp.int32), from_node, to_node)
    row_select = incidence_of(row * row_count + jnp.arange(row_count, dtype=jnp.int32), from_node, to_node)
    part = nt(col_select.T, high) + nt(col_select.T, low)
    parts = lax.all_to_all(jnp.broadcast_to(part[None], (COLS,) + part.shape), "col", 0, 0, tiled=True)
    columns_t = jnp.sum(parts, axis=0)

    width = row_count // COLS
    piece = lax.dynamic_slice_in_dim(columns_t.T, col * width, width, 0)
    piece = jnp.concatenate([piece[: width // 2], piece[width // 2:]], axis=1)
    piece = lax.ppermute(piece, ("row", "col"), TO_COLUMN)
    cap_part = jnp.dot(columns_t, row_select.astype(F32), precision=HIGH, preferred_element_type=F32)
    cap_part = jnp.concatenate([cap_part[: BR // 2], cap_part[BR // 2:]], axis=1)
    mine = jnp.concatenate([piece, cap_part], axis=0)
    other = lax.ppermute(mine, "row", OTHER_Y)
    h = width // 2
    both = jnp.concatenate(
        [in_order(y, mine[:h], other[:h]).reshape(Y * h, 2 * BR), mine[h:] + other[h:]], axis=0
    )
    line = lax.all_gather(both, "row", axis_index_groups=ALONG_Z, axis=0)
    other_line = lax.ppermute(line, "row", OTHER_CORE)
    capacity = jnp.sum(line[:, Y * h:] + other_line[:, Y * h:], axis=0)
    capacity = jnp.concatenate([capacity[:, :BR], capacity[:, BR:]], axis=0)
    ends = in_order(core, line[:, : Y * h], other_line[:, : Y * h])
    ends = ends.reshape(CORES, Z, Y, h, 2, BR).transpose(2, 1, 0, 4, 3, 5).reshape(col_count, BR)

    other_columns_t = lax.ppermute(columns_t, "row", OTHER_CORE)
    both_columns_t = jnp.concatenate([columns_t, other_columns_t], axis=1)
    reach = impedance * (1.0 + 3.0 * switch_flags.astype(F32))
    factor = jnp.linalg.cholesky(capacity + jnp.diag(reach))
    solved = jax.scipy.linalg.cho_solve((factor, True), both_columns_t)

    correction = lax.dot_general(
        solved, ends, (((0,), (1,)), ((), ())), precision=HIGH, preferred_element_type=F32
    )
    after = jnp.concatenate([sensitivity, other_rows], axis=0) - correction
    after_high, after_low = split(after)

    zs = Z * Y // COLS
    sums = []
    for side in range(Y):
        part_loads = gathered[:, side].reshape(Z * slots, col_count)
        sums.append(nt(part_loads, after_high) + nt(part_loads, after_low))
    sums = jnp.stack(sums).reshape(COLS, zs * slots, CORES * row_count)
    arrived = lax.all_to_all(sums, "col", 0, 0, tiled=True)
    total = jnp.sum(arrived, axis=0)
    keep, give = total[:, :row_count], total[:, row_count:]
    taken = lax.ppermute(give, "row", OTHER_CORE)
    result = in_order(core, keep, taken).reshape(CORES, zs, slots, row_count)
    return result.transpose(3, 1, 0, 2).reshape(row_count, zs * CORES * slots)


def solution(mesh):
    placed = (P("row", "col"), P("col", "row"), P(), P(), P(), P())
    return jax.shard_map(
        on_device, mesh=mesh, in_specs=placed, out_specs=P("row", "col"), check_vma=False
    )
```

time: 773 us -> 187 us (0.24)
  waiting for transfers between devices: 484 us -> 14.2 us
  blocking collectives: 245 us -> 71.9 us
  starting transfers between devices: 0.08 us -> 44.2 us
    psum x1 -> x0, waiting for transfers between devices: 346 us -> none  [on_device(): ends = lax.psum(ends_part, 'row')]
    psum x2 -> x0, blocking collectives: 245 us -> none  [the longest x1 211 us: on_device(): cap_sum = lax.psum(cap_part, 'row')]
    all_gather x1, waiting for transfers between devices: 137 us -> 0.01 us  [on_device(): gathered = lax.all_gather(pair, 'row', axis_index_groups=ALONG_Z, axis=0)]
    all_gather x0 -> x1, blocking collectives: none -> 40.2 us  [on_device(): line = lax.all_gather(both, 'row', axis_index_groups=ALONG_Z, axis=0)]
    ppermute x0 -> x7, starting transfers between devices: none -> 36.8 us  [the longest x1 12.1 us: on_device(): piece = lax.ppermute(piece, ('row', 'col'), TO_COLUMN)]
    all_to_all x0 -> x1, blocking collectives: none -> 31.7 us  [on_device(): arrived = lax.all_to_all(sums, 'col', 0, 0, tiled=True)]
    all_to_all x0 -> x1, waiting for transfers between devices: none -> 8.58 us  [on_device(): lax.all_to_all(jnp.broadcast_to(part[None], (COLS,) + part.shape), 'col',...]
    dot_general x5 -> x8, matrix products: 16.9 us -> 15.6 us  [the longest x6 8.7 us: nt(): lax.dot_general(left, right, (((1,), (1,)), ((), ())), preferred_element_...]
  transfers between devices with their start and end apart: 3 -> 9, of which waited for: 2 -> 5; matrix products, arithmetic and copies ran while one was open for 2% -> 16% of each run, Pallas kernels for 0% -> 0%
where the time goes in v1:
time: 187 us; the launch traced here: 186 us
  blocking collectives  71.9 us (38%)
  starting transfers between devices  44.2 us (24%)
  other arithmetic  18.2 us (10%)
  matrix products  16.2 us (9%)
  waiting for transfers between devices  14.2 us (8%)
  between operations  13.8 us (7%)
  local copies, waits for them, and re-layouts  7.6 us (4%)
    all_gather x1, blocking collectives, on_device(): line = lax.all_gather(both, 'row', axis_index_groups=ALONG_Z, axis=0)  40.2 us
    all_to_all x1, blocking collectives, on_device(): arrived = lax.all_to_all(sums, 'col', 0, 0, tiled=True)  31.7 us
    ppermute x1, starting transfers between devices, on_device(): piece = lax.ppermute(piece, ('row', 'col'), TO_COLUMN)  12.1 us
    ppermute x1, starting transfers between devices, on_device(): other_line = lax.ppermute(line, 'row', OTHER_CORE)  9.07 us
    dot_general x6, matrix products, nt(): lax.dot_general(left, right, (((1,), (1,)), ((), ())), preferred_element_...  8.7 us
    all_to_all x1, waiting for transfers between devices, on_device(): lax.all_to_all(jnp.broadcast_to(part[None], (COLS,) + part.shape), 'col',...  8.58 us
    all_to_all x1, starting transfers between devices, on_device(): lax.all_to_all(jnp.broadcast_to(part[None], (COLS,) + part.shape), 'col',...  7.35 us
    dot_general x1, matrix products, on_device(): lax.dot_general(solved, ends, (((0,), (1,)), ((), ())), precision=HIGH, p...  6.68 us
  transfers between devices with their start and end apart: 9, of which 5 were waited for; matrix products, arithmetic and copies ran while one was open for 16% of the time, Pallas kernels for 0%

profile of v1, /device:TPU:1, one launch (start us, length us, event | category | flops | bytes accessed | tf_op | source)
XLA Modules:
  0.0 186.1 jit_solution(3574581481206083017)
XLA Ops:
  6.5 4.2 %collective-permute-start = (bf16[32,2048]{1,0:T(8,128)(2,1)}, bf16[32,2048]{1,0:T(8,128)(2,1)S(1)}, u32[]{:S(2)}, u32[]{:S(2)}) collective-permute-start(bf16[32,2048]{1,0:T(8,128)(2,1)} %bitcast.58), channel_id=1, source_target_pairs={{0,256},{8,264},{16,272},{24,280},{32,288},{40,296},{48,304},{56,3... | collective-permute-start | bytes 393224 | tf_op jit(solution)/shard_map/ppermute | solution.py:56
  10.7 2.5 %collective-permute-done = bf16[32,2048]{1,0:T(8,128)(2,1)S(1)} collective-permute-done((bf16[32,2048]{1,0:T(8,128)(2,1)}, bf16[32,2048]{1,0:T(8,128)(2,1)S(1)}, u32[]{:S(2)}, u32[]{:S(2)}) %collective-permute-start) | collective-permute-done | bytes 131104 | tf_op jit(solution)/shard_map/ppermute | solution.py:56
  13.3 1.7 maximum_select_fusion.1
  15.0 2.5 %fusion.5 = f32[64,256]{1,0:T(8,128)S(1)} fusion(f32[256,2048]{1,0:T(8,128)} %param.6, s32[64]{0:T(128)} %param.9, s32[64]{0:T(128)} %param.8, s32[2048]{0:T(1024)S(1)} %iota_add_fusion), kind=kOutput, calls=%fused_computation.13 | convolution fusion | flops 68812800 | bytes 2171392 | tf_op jit(solution)/shard_map/dot_general | solution.py:45
  17.6 0.9 convolution_add_fusion.2
  18.5 0.8 broadcast_in_dim.16
  19.3 7.4 %all-to-all-start = ((f32[8,64,256]{2,1,0:T(8,128)}), f32[8,64,256]{2,1,0:T(8,128)S(1)}, u32[]{:S(2)}, u32[]{:S(2)}) async-start(f32[8,64,256]{2,1,0:T(8,128)} %broadcast_in_dim.16), calls=%async_computation | async-start | bytes 1048576 | tf_op jit(solution)/shard_map/all_to_all | solution.py:66
  26.7 8.6 %all-to-all-done = f32[8,64,256]{2,1,0:T(8,128)S(1)} async-done(((f32[8,64,256]{2,1,0:T(8,128)}), f32[8,64,256]{2,1,0:T(8,128)S(1)}, u32[]{:S(2)}, u32[]{:S(2)}) %all-to-all-start) | async-done | bytes 524320 | tf_op jit(solution)/shard_map/all_to_all | solution.py:66
  35.5 12.1 %collective-permute-start.2 = (f32[16,128]{1,0:T(8,128)S(1)}, f32[16,128]{1,0:T(8,128)S(1)}, u32[]{:S(2)}, u32[]{:S(2)}) collective-permute-start(f32[16,128]{1,0:T(8,128)S(1)} %pad_maximum_fusion.2), channel_id=1, source_target_pairs={{0,0},{1,8},{2,16},{3,24},{4,32},{5,40},{6,48},{7,56},{8,64},{9,72... | collective-permute-start | bytes 24584 | tf_op jit(solution)/shard_map/ppermute | solution.py:72
  48.5 3.9 %collective-permute-start.3 = (f32[48,128]{1,0:T(8,128)S(1)}, f32[48,128]{1,0:T(8,128)S(1)}, u32[]{:S(2)}, u32[]{:S(2)}) collective-permute-start(f32[48,128]{1,0:T(8,128)S(1)} %maximum_maximum_fusion), channel_id=1, source_target_pairs={{0,256},{8,264},{16,272},{24,280},{32,288},{40,296},{48,304},{56,3... | collective-permute-start | bytes 73736 | tf_op jit(solution)/shard_map/ppermute | solution.py:76
  52.4 1.6 collective-permute-done.3
  54.1 40.2 %all-gather = f32[1024,128]{1,0:T(8,128)S(1)} all-gather(f32[64,128]{1,0:T(8,128)S(1)} %pad_maximum_fusion.1), channel_id=2, replica_groups={{0,16,32,48,64,80,96,112,128,144,160,176,192,208,224,240},{8,24,40,56,7..., dimensions={0}, use_global_device_ids=true | all-gather | bytes 557056 | tf_op jit(solution)/shard_map/all_gather | solution.py:81
  94.3 9.1 %collective-permute-start.4 = (f32[16,64,128]{2,1,0:T(8,128)S(1)}, f32[16,64,128]{2,1,0:T(8,128)}, u32[]{:S(2)}, u32[]{:S(2)}) collective-permute-start(f32[16,64,128]{2,1,0:T(8,128)S(1)} %bitcast.50), channel_id=1, source_target_pairs={{0,8},{8,0},{16,24},{24,16},{32,40},{40,32},{48,56},{56,48},{64,72... | collective-permute-start | bytes 1572872 | tf_op jit(solution)/shard_map/ppermute | solution.py:82
  103.4 1.9 %collective-permute-start.1 = (f32[256,2048]{1,0:T(8,128)S(1)}, f32[256,2048]{1,0:T(8,128)}, u32[]{:S(2)}, u32[]{:S(2)}) collective-permute-start(f32[256,2048]{1,0:T(8,128)S(1)} %copy-done), channel_id=1, source_target_pairs={{0,8},{8,0},{16,24},{24,16},{32,40},{40,32},{48,56},{56,48},{64,72... | collective-permute-start | bytes 6291464 | tf_op jit(solution)/shard_map/ppermute | solution.py:60
  105.4 2.6 %collective-permute-start.5 = (f32[64,256]{1,0:T(8,128)S(1)}, f32[64,256]{1,0:T(8,128)S(1)}, u32[]{:S(2)}, u32[]{:S(2)}) collective-permute-start(f32[64,256]{1,0:T(8,128)S(1)} %reduce_sum.27), channel_id=1, source_target_pairs={{0,8},{8,0},{16,24},{24,16},{32,40},{40,32},{48,56},{56,48},{64,72... | collective-permute-start | bytes 196616 | tf_op jit(solution)/shard_map/ppermute | solution.py:88
  108.0 1.1 fusion.35
  109.4 5.8 %cholesky.16 = f32[64,64]{1,0:T(8,128)S(1)} custom-call(f32[64,64]{1,0:T(8,128)S(1)} %fusion.32), custom_call_target="Cholesky" | custom-call | tf_op jit(solution)/shard_map/jit(cholesky)/cholesky | solution.py:91
  115.2 1.1 stack.73
  116.4 1.1 stack.74
  117.5 0.6 compare_reduce_fusion
  118.7 2.7 %fusion.6 = f32[2,16,2,2,16,64]{5,3,4,0,1,2:T(2,128)S(1)} fusion(f32[1,16,2,16,2,64]{5,4,3,2,1,0:T(2,128)} %stack.74, f32[1,16,2,16,2,64]{5,4,3,2,1,0:T(2,128)} %stack.73, pred[]{:T(512)S(6)} %eq.27), kind=kLoop, calls=%fused_computation.15 | loop fusion | flops 393216 | bytes 1048577 | tf_op jit(solution)/shard_map/transpose | solution.py:86
  121.3 4.9 %custom-call.10 = f32[1,64,64]{1,2,0:T(8,128)S(1)} custom-call(f32[1,64,64]{2,1,0:T(8,128)S(1)} %fusion.28), custom_call_target="InvertDiagBlocksLowerTriangular" | custom-call | tf_op jit(solution)/shard_map/jit(_cho_solve)/triangular_solve | solution.py:92
  127.0 6.7 %reduce-precision_convert_fusion = (bf16[512,2048]{1,0:T(8,128)(2,1)}, bf16[512,2048]{1,0:T(8,128)(2,1)}) fusion(f32[256,2048]{1,0:T(8,128)} %collective-permute-done.1, f32[256,2048]{1,0:T(8,128)S(1)} %copy-done, f32[64,512]{1,0:T(8,128)S(1)} %fusion.29, f32[2048,64]{1,0:T(8,128)S(1)} %bitcast.49), kind=kOutput, calls=%fused_computation.1 | convolution fusion | flops 811597824 | bytes 9043968 | tf_op jit(solution)/shard_map/dot_general | solution.py:94
  133.6 2.9 %fusion.34 = (bf16[16,1,32,2048]{3,2,1,0:T(8,128)(2,1)S(1)}, bf16[16,1,32,2048]{3,2,1,0:T(8,128)(2,1)S(1)}) fusion(bf16[16,2,32,2048]{3,2,1,0:T(8,128)(2,1)} %all-gather.3.cloned.1.call-done), kind=kLoop, calls=%fused_computation.64 | loop fusion | bytes 8388608 | tf_op jit(solution)/shard_map/slice | solution.py:103
  136.5 1.3 fusion.41
  137.8 1.3 fusion.40
  139.4 1.4 fusion.2
  140.8 1.4 fusion.3
  142.4 31.7 %all_to_all.10 = f32[8,128,512]{2,1,0:T(8,128)S(1)} all-to-all(f32[8,128,512]{2,1,0:T(8,128)S(1)} %bitcast.48), channel_id=1, replica_groups=mesh['row'=64,'col'=8] {'col'}, dimensions={0} | all-to-all | bytes 4194304 | tf_op jit(solution)/shard_map/all_to_all | solution.py:106
  174.3 3.1 %collective-permute-start.6 = (f32[128,256]{1,0:T(8,128)S(1)}, f32[128,256]{1,0:T(8,128)S(1)}, u32[]{:S(2)}, u32[]{:S(2)}) collective-permute-start(f32[128,256]{1,0:T(8,128)S(1)} %get-tuple-element.13), channel_id=1, source_target_pairs={{0,8},{8,0},{16,24},{24,16},{32,40},{40,32},{48,56},{56,48},{64,72... | collective-permute-start | bytes 393224 | tf_op jit(solution)/shard_map/ppermute | solution.py:109
  177.4 1.0 collective-permute-done.6
  178.4 0.8 copy.23
  (50 shorter events, 3.5 us)
Async XLA Ops:
  6.5 11.0 %copy-start = (f32[256,2048]{1,0:T(8,128)S(1)}, f32[256,2048]{1,0:T(8,128)}, u32[]{:S(2)}) copy-start(f32[256,2048]{1,0:T(8,128)} %param.6) | copy-start | bytes 6291460
  6.5 11.0 %copy-start.3 = (s32[64]{0:T(128)S(1)}, s32[64]{0:T(128)}, u32[]{:S(2)}) copy-start(s32[64]{0:T(128)} %param.9) | copy-start | bytes 772
  6.5 11.0 %copy-start.4 = (s32[64]{0:T(128)S(1)}, s32[64]{0:T(128)}, u32[]{:S(2)}) copy-start(s32[64]{0:T(128)} %param.8) | copy-start | bytes 772
  6.5 127.1 %all-gather.3.cloned.1.call-start = ((), (), s32[]{:S(2)}) async-start(), calls=%async_computation.2 | async-start | bytes 4456448 | tf_op jit(solution)/shard_map/all_gather | solution.py:58
  6.5 6.7 %collective-permute-start = (bf16[32,2048]{1,0:T(8,128)(2,1)}, bf16[32,2048]{1,0:T(8,128)(2,1)S(1)}, u32[]{:S(2)}, u32[]{:S(2)}) collective-permute-start(bf16[32,2048]{1,0:T(8,128)(2,1)} %bitcast.58), channel_id=1, source_target_pairs={{0,256},{8,264},{16,272},{24,280},{32,288},{40,296},{48,304},{56,3... | collective-permute-start | bytes 393224 | tf_op jit(solution)/shard_map/ppermute | solution.py:56
  18.5 86.9 %copy-start.5 = (f32[64]{0:T(128)S(1)}, f32[64]{0:T(128)}, u32[]{:S(2)}) copy-start(f32[64]{0:T(128)} %param.11) | copy-start | bytes 772
  18.5 86.9 %copy-start.6 = (s32[64]{0:T(128)S(1)}, s32[64]{0:T(128)}, u32[]{:S(2)}) copy-start(s32[64]{0:T(128)} %param.10) | copy-start | bytes 772
  19.3 15.9 %all-to-all-start = ((f32[8,64,256]{2,1,0:T(8,128)}), f32[8,64,256]{2,1,0:T(8,128)S(1)}, u32[]{:S(2)}, u32[]{:S(2)}) async-start(f32[8,64,256]{2,1,0:T(8,128)} %broadcast_in_dim.16), calls=%async_computation | async-start | bytes 1048576 | tf_op jit(solution)/shard_map/all_to_all | solution.py:66
  35.5 12.9 %collective-permute-start.2 = (f32[16,128]{1,0:T(8,128)S(1)}, f32[16,128]{1,0:T(8,128)S(1)}, u32[]{:S(2)}, u32[]{:S(2)}) collective-permute-start(f32[16,128]{1,0:T(8,128)S(1)} %pad_maximum_fusion.2), channel_id=1, source_target_pairs={{0,0},{1,8},{2,16},{3,24},{4,32},{5,40},{6,48},{7,56},{8,64},{9,72... | collective-permute-start | bytes 24584 | tf_op jit(solution)/shard_map/ppermute | solution.py:72
  48.5 5.5 %collective-permute-start.3 = (f32[48,128]{1,0:T(8,128)S(1)}, f32[48,128]{1,0:T(8,128)S(1)}, u32[]{:S(2)}, u32[]{:S(2)}) collective-permute-start(f32[48,128]{1,0:T(8,128)S(1)} %maximum_maximum_fusion), channel_id=1, source_target_pairs={{0,256},{8,264},{16,272},{24,280},{32,288},{40,296},{48,304},{56,3... | collective-permute-start | bytes 73736 | tf_op jit(solution)/shard_map/ppermute | solution.py:76
  94.3 13.7 %collective-permute-start.4 = (f32[16,64,128]{2,1,0:T(8,128)S(1)}, f32[16,64,128]{2,1,0:T(8,128)}, u32[]{:S(2)}, u32[]{:S(2)}) collective-permute-start(f32[16,64,128]{2,1,0:T(8,128)S(1)} %bitcast.50), channel_id=1, source_target_pairs={{0,8},{8,0},{16,24},{24,16},{32,40},{40,32},{48,56},{56,48},{64,72... | collective-permute-start | bytes 1572872 | tf_op jit(solution)/shard_map/ppermute | solution.py:82
  103.4 23.5 %collective-permute-start.1 = (f32[256,2048]{1,0:T(8,128)S(1)}, f32[256,2048]{1,0:T(8,128)}, u32[]{:S(2)}, u32[]{:S(2)}) collective-permute-start(f32[256,2048]{1,0:T(8,128)S(1)} %copy-done), channel_id=1, source_target_pairs={{0,8},{8,0},{16,24},{24,16},{32,40},{40,32},{48,56},{56,48},{64,72... | collective-permute-start | bytes 6291464 | tf_op jit(solution)/shard_map/ppermute | solution.py:60
  105.4 21.0 %collective-permute-start.5 = (f32[64,256]{1,0:T(8,128)S(1)}, f32[64,256]{1,0:T(8,128)S(1)}, u32[]{:S(2)}, u32[]{:S(2)}) collective-permute-start(f32[64,256]{1,0:T(8,128)S(1)} %reduce_sum.27), channel_id=1, source_target_pairs={{0,8},{8,0},{16,24},{24,16},{32,40},{40,32},{48,56},{56,48},{64,72... | collective-permute-start | bytes 196616 | tf_op jit(solution)/shard_map/ppermute | solution.py:88
  133.6 2.9 %copy-start.2 = (bf16[512,2048]{1,0:T(8,128)(2,1)S(1)}, bf16[512,2048]{1,0:T(8,128)(2,1)}, u32[]{:S(2)}) copy-start(bf16[512,2048]{1,0:T(8,128)(2,1)} %get-tuple-element.6) | copy-start | bytes 6291460
  137.8 1.6 copy-start.1
  174.3 4.0 %collective-permute-start.6 = (f32[128,256]{1,0:T(8,128)S(1)}, f32[128,256]{1,0:T(8,128)S(1)}, u32[]{:S(2)}, u32[]{:S(2)}) collective-permute-start(f32[128,256]{1,0:T(8,128)S(1)} %get-tuple-element.13), channel_id=1, source_target_pairs={{0,8},{8,0},{16,24},{24,16},{32,40},{40,32},{48,56},{56,48},{64,72... | collective-permute-start | bytes 393224 | tf_op jit(solution)/shard_map/ppermute | solution.py:109
Sparse Core Ops, SparseCore 0:
  15.1 80.0 all-gather.2

commit v2 on v1

--- a/solution.py
+++ b/solution.py
@@ -85,30 +85,39 @@
     ends = in_order(core, line[:, : Y * h], other_line[:, : Y * h])
     ends = ends.reshape(CORES, Z, Y, h, 2, BR).transpose(2, 1, 0, 4, 3, 5).reshape(col_count, BR)
 
-    other_columns_t = lax.ppermute(columns_t, "row", OTHER_CORE)
-    both_columns_t = jnp.concatenate([columns_t, other_columns_t], axis=1)
+    other_high, other_low = split(other_rows)
+    both_high = jnp.concatenate([high, other_high], axis=0)
+    both_low = jnp.concatenate([low, other_low], axis=0)
+    ends = jnp.concatenate(split(ends), axis=1)
+    zs = Z * Y // COLS
+    count = zs * slots
+    sums, end_sums = [], []
+    for side in range(Y):
+        part_loads = gathered[:, side].reshape(Z * slots, col_count)
+        sums.append(nt(part_loads, both_high) + nt(part_loads, both_low))
+        end_part = jnp.dot(part_loads, ends, preferred_element_type=F32)
+        end_sums.append(end_part[:, :BR] + end_part[:, BR:])
+    sums = jnp.stack(sums).reshape(COLS, count, CORES * row_count)
+    fold = CORES * row_count // BR
+    end_sums = jnp.stack(end_sums).reshape(COLS, fold, count // fold, BR)
+    end_sums = end_sums.transpose(0, 2, 1, 3).reshape(COLS, count // fold, fold * BR)
+    arrived = lax.all_to_all(jnp.concatenate([sums, end_sums], axis=1), "col", 0, 0, tiled=True)
+
     reach = impedance * (1.0 + 3.0 * switch_flags.astype(F32))
     factor = jnp.linalg.cholesky(capacity + jnp.diag(reach))
-    solved = jax.scipy.linalg.cho_solve((factor, True), both_columns_t)
+    solved = jax.scipy.linalg.cho_solve((factor, True), columns_t)
 
-    correction = lax.dot_general(
-        solved, ends, (((0,), (1,)), ((), ())), precision=HIGH, preferred_element_type=F32
+    total = jnp.sum(arrived, axis=0)
+    end_total = total[count:].reshape(count // fold, fold, BR).transpose(1, 0, 2).reshape(count, BR)
+    mine = jnp.concatenate([total[:count, :row_count], end_total], axis=1)
+    give = jnp.concatenate([total[:count, row_count:], end_total], axis=1)
+    taken = lax.ppermute(give, "row", OTHER_CORE)
+    result = in_order(core, mine, taken).reshape(CORES, zs, slots, row_count + BR)
+    result = result.transpose(1, 0, 2, 3).reshape(CORES * count, row_count + BR)
+    drop = lax.dot_general(
+        solved, result[:, row_count:], (((0,), (1,)), ((), ())), precision=HIGH, preferred_element_type=F32
     )
-    after = jnp.concatenate([sensitivity, other_rows], axis=0) - correction
-    after_high, after_low = split(after)
-
-    zs = Z * Y // COLS
-    sums = []
-    for side in range(Y):
-        part_loads = gathered[:, side].reshape(Z * slots, col_count)
-        sums.append(nt(part_loads, after_high) + nt(part_loads, after_low))
-    sums = jnp.stack(sums).reshape(COLS, zs * slots, CORES * row_count)
-    arrived = lax.all_to_all(sums, "col", 0, 0, tiled=True)
-    total = jnp.sum(arrived, axis=0)
-    keep, give = total[:, :row_count], total[:, row_count:]
-    taken = lax.ppermute(give, "row", OTHER_CORE)
-    result = in_order(core, keep, taken).reshape(CORES, zs, slots, row_count)
-    return result.transpose(3, 1, 0, 2).reshape(row_count, zs * CORES * slots)
+    return result[:, :row_count].T - drop
 
 
 def solution(mesh):

time: 187 us -> 179 us (0.957)
  blocking collectives: 71.9 us -> 42.9 us
  waiting for transfers between devices: 14.2 us -> 35.9 us
  other arithmetic: 18.2 us -> 23.3 us
  matrix products: 16.2 us -> 11.9 us
    all_to_all x1 -> x0, blocking collectives: 31.7 us -> none  [on_device(): arrived = lax.all_to_all(sums, 'col', 0, 0, tiled=True)]
    all_to_all x0 -> x1, waiting for transfers between devices: none -> 21.8 us  [on_device(): lax.all_to_all(jnp.concatenate([sums, end_sums], axis=1), 'col', 0, 0, ti...]
    convert_element_type x0 -> x3, other arithmetic: none -> 5.19 us  [split(): return (high.astype(BF16), (values - high).astype(BF16))]
    all_to_all x0 -> x1, starting transfers between devices: none -> 5.09 us  [on_device(): lax.all_to_all(jnp.concatenate([sums, end_sums], axis=1), 'col', 0, 0, ti...]
    dot_general x1 -> x3, matrix products: 6.68 us -> 3.25 us  [the longest x2 2.12 us: on_device(): end_part = jnp.dot(part_loads, ends, preferred_element_type=F32)]
    ppermute x1, starting transfers between devices: 9.07 us -> 5.98 us  [on_device(): other_line = lax.ppermute(line, 'row', OTHER_CORE)]
    all_gather x1, blocking collectives: 40.2 us -> 42.9 us  [on_device(): line = lax.all_gather(both, 'row', axis_index_groups=ALONG_Z, axis=0)]
    ppermute x1 -> x0, starting transfers between devices: 2.59 us -> none  [on_device(): other_columns_t = lax.ppermute(columns_t, 'row', OTHER_CORE)]
  transfers between devices with their start and end apart: 9 -> 9, of which waited for: 5 -> 6; matrix products, arithmetic and copies ran while one was open for 16% -> 13% of each run, Pallas kernels for 0% -> 0%
where the time goes in v2:
time: 179 us
  starting transfers between devices  43.7 us (24%)
  blocking collectives  42.9 us (24%)
  waiting for transfers between devices  35.9 us (20%)
  other arithmetic  23.3 us (13%)
  between operations  13.9 us (8%)
  matrix products  11.9 us (7%)
  local copies, waits for them, and re-layouts  6.79 us (4%)
    all_gather x1, blocking collectives, on_device(): line = lax.all_gather(both, 'row', axis_index_groups=ALONG_Z, axis=0)  42.9 us
    all_to_all x1, waiting for transfers between devices, on_device(): lax.all_to_all(jnp.concatenate([sums, end_sums], axis=1), 'col', 0, 0, ti...  21.8 us
    ppermute x1, starting transfers between devices, on_device(): piece = lax.ppermute(piece, ('row', 'col'), TO_COLUMN)  12.1 us
    all_to_all x1, waiting for transfers between devices, on_device(): lax.all_to_all(jnp.broadcast_to(part[None], (COLS,) + part.shape), 'col',...  8.58 us
    dot_general x6, matrix products, nt(): lax.dot_general(left, right, (((1,), (1,)), ((), ())), preferred_element_...  7.97 us
    all_to_all x1, starting transfers between devices, on_device(): lax.all_to_all(jnp.broadcast_to(part[None], (COLS,) + part.shape), 'col',...  7.36 us
    another operation x3, other arithmetic, on_device(): factor = jnp.linalg.cholesky(capacity + jnp.diag(reach))  6.52 us
    ppermute x1, starting transfers between devices, on_device(): other_line = lax.ppermute(line, 'row', OTHER_CORE)  5.98 us
  transfers between devices with their start and end apart: 9, of which 6 were waited for; matrix products, arithmetic and copies ran while one was open for 13% of the time, Pallas kernels for 0%

profile of v2, /device:TPU:1, one launch (start us, length us, event | category | flops | bytes accessed | tf_op | source)
XLA Modules:
  0.0 178.5 jit_solution(15182007479961784607)
XLA Ops:
  6.5 4.0 %collective-permute-start = (bf16[32,2048]{1,0:T(8,128)(2,1)}, bf16[32,2048]{1,0:T(8,128)(2,1)S(1)}, u32[]{:S(2)}, u32[]{:S(2)}) collective-permute-start(bf16[32,2048]{1,0:T(8,128)(2,1)} %bitcast.82), channel_id=1, source_target_pairs={{0,256},{8,264},{16,272},{24,280},{32,288},{40,296},{48,304},{56,3... | collective-permute-start | bytes 393224 | tf_op jit(solution)/shard_map/ppermute | solution.py:56
  10.6 2.5 %collective-permute-done = bf16[32,2048]{1,0:T(8,128)(2,1)S(1)} collective-permute-done((bf16[32,2048]{1,0:T(8,128)(2,1)}, bf16[32,2048]{1,0:T(8,128)(2,1)S(1)}, u32[]{:S(2)}, u32[]{:S(2)}) %collective-permute-start) | collective-permute-done | bytes 131104 | tf_op jit(solution)/shard_map/ppermute | solution.py:56
  13.1 1.7 maximum_select_fusion.2
  14.9 2.0 %fusion = (bf16[256,2048]{1,0:T(8,128)(2,1)S(1)}, bf16[256,2048]{1,0:T(8,128)(2,1)S(1)}) fusion(f32[256,2048]{1,0:T(8,128)} %param.6), kind=kLoop, calls=%fused_computation.5 | loop fusion | flops 2097152 | bytes 4194304 | tf_op jit(solution)/shard_map/convert_element_type | solution.py:37
  16.9 0.9 fusion.14
  18.3 0.9 convolution_add_fusion
  19.1 0.8 broadcast_in_dim.16
  20.0 7.4 %all-to-all-start = ((f32[8,64,256]{2,1,0:T(8,128)}), f32[8,64,256]{2,1,0:T(8,128)S(1)}, u32[]{:S(2)}, u32[]{:S(2)}) async-start(f32[8,64,256]{2,1,0:T(8,128)} %broadcast_in_dim.16), calls=%async_computation | async-start | bytes 1048576 | tf_op jit(solution)/shard_map/all_to_all | solution.py:66
  27.3 8.6 %all-to-all-done = f32[8,64,256]{2,1,0:T(8,128)S(1)} async-done(((f32[8,64,256]{2,1,0:T(8,128)}), f32[8,64,256]{2,1,0:T(8,128)S(1)}, u32[]{:S(2)}, u32[]{:S(2)}) %all-to-all-start) | async-done | bytes 524320 | tf_op jit(solution)/shard_map/all_to_all | solution.py:66
  36.2 12.1 %collective-permute-start.2 = (f32[16,128]{1,0:T(8,128)S(1)}, f32[16,128]{1,0:T(8,128)S(1)}, u32[]{:S(2)}, u32[]{:S(2)}) collective-permute-start(f32[16,128]{1,0:T(8,128)S(1)} %pad_maximum_fusion.22), channel_id=1, source_target_pairs={{0,0},{1,8},{2,16},{3,24},{4,32},{5,40},{6,48},{7,56},{8,64},{9,72... | collective-permute-start | bytes 24584 | tf_op jit(solution)/shard_map/ppermute | solution.py:72
  49.2 3.9 %collective-permute-start.3 = (f32[48,128]{1,0:T(8,128)S(1)}, f32[48,128]{1,0:T(8,128)S(1)}, u32[]{:S(2)}, u32[]{:S(2)}) collective-permute-start(f32[48,128]{1,0:T(8,128)S(1)} %maximum_maximum_fusion), channel_id=1, source_target_pairs={{0,256},{8,264},{16,272},{24,280},{32,288},{40,296},{48,304},{56,3... | collective-permute-start | bytes 73736 | tf_op jit(solution)/shard_map/ppermute | solution.py:76
  53.1 1.9 %collective-permute-start.1 = (f32[256,2048]{1,0:T(8,128)S(1)}, f32[256,2048]{1,0:T(8,128)}, u32[]{:S(2)}, u32[]{:S(2)}) collective-permute-start(f32[256,2048]{1,0:T(8,128)S(1)} %copy-done), channel_id=1, source_target_pairs={{0,8},{8,0},{16,24},{24,16},{32,40},{40,32},{48,56},{56,48},{64,72... | collective-permute-start | bytes 6291464 | tf_op jit(solution)/shard_map/ppermute | solution.py:60
  55.1 42.9 %all-gather = f32[1024,128]{1,0:T(8,128)S(1)} all-gather(f32[64,128]{1,0:T(8,128)S(1)} %pad_maximum_fusion.21), channel_id=2, replica_groups={{0,16,32,48,64,80,96,112,128,144,160,176,192,208,224,240},{8,24,40,56,7..., dimensions={0}, use_global_device_ids=true | all-gather | bytes 557056 | tf_op jit(solution)/shard_map/all_gather | solution.py:81
  98.1 6.0 %collective-permute-start.4 = (f32[16,64,128]{2,1,0:T(8,128)S(1)}, f32[16,64,128]{2,1,0:T(8,128)}, u32[]{:S(2)}, u32[]{:S(2)}) collective-permute-start(f32[16,64,128]{2,1,0:T(8,128)S(1)} %bitcast.73), channel_id=1, source_target_pairs={{0,8},{8,0},{16,24},{24,16},{32,40},{40,32},{48,56},{56,48},{64,72... | collective-permute-start | bytes 1572872 | tf_op jit(solution)/shard_map/ppermute | solution.py:82
  104.1 1.6 collective-permute-done.4
  105.7 1.1 fusion.48
  108.4 3.0 %reduce-precision_convert_fusion = (bf16[256,2048]{1,0:T(8,128)(2,1)S(1)}, bf16[256,2048]{1,0:T(8,128)(2,1)}) fusion(f32[256,2048]{1,0:T(8,128)} %collective-permute-done.1), kind=kLoop, calls=%fused_computation.1 | loop fusion | flops 2097152 | bytes 4194304 | tf_op jit(solution)/shard_map/convert_element_type | solution.py:37
  111.4 2.9 %fusion.47 = (bf16[16,1,32,2048]{3,2,1,0:T(8,128)(2,1)S(1)}, bf16[16,1,32,2048]{3,2,1,0:T(8,128)(2,1)S(1)}) fusion(bf16[16,2,32,2048]{3,2,1,0:T(8,128)(2,1)} %all-gather.3.cloned.1.call-done), kind=kLoop, calls=%fused_computation.86 | loop fusion | bytes 8388608 | tf_op jit(solution)/shard_map/slice | solution.py:96
  114.3 1.3 fusion.3
  115.6 1.3 fusion.2
  116.9 1.1 fusion.28
  118.0 1.1 fusion.27
  119.2 1.3 fusion.7
  120.5 2.3 %fusion.9 = f32[1,512,512]{2,1,0:T(8,128)} fusion(f32[512,512]{1,0:T(8,128)S(1)} %fusion.2, bf16[512,2048]{1,0:T(8,128)(2,1)S(1)} %bitcast.69, bf16[256,2048]{1,0:T(8,128)(2,1)S(1)} %get-tuple-element.7, bf16[256,2048]{1,0:T(8,128)(2,1)S(1)} %copy-done.2), kind=kOutput, calls=%fused_computation.19 | convolution fusion | flops 1078198272 | bytes 6291456 | tf_op jit(solution)/shard_map/dot_general | solution.py:45
  124.3 1.7 pad_maximum_fusion
  126.0 5.1 %all-to-all-start.1 = ((f32[8,144,512]{2,1,0:T(8,128)}), f32[8,144,512]{2,1,0:T(8,128)S(1)}, u32[]{:S(2)}, u32[]{:S(2)}) async-start(f32[8,144,512]{2,1,0:T(8,128)} %pad_maximum_fusion), calls=%async_computation.1 | async-start | bytes 4718592 | tf_op jit(solution)/shard_map/all_to_all | solution.py:104
  131.3 5.8 %cholesky.16 = f32[64,64]{1,0:T(8,128)S(1)} custom-call(f32[64,64]{1,0:T(8,128)S(1)} %fusion.40), custom_call_target="Cholesky" | custom-call | tf_op jit(solution)/shard_map/jit(cholesky)/cholesky | solution.py:107
  138.5 4.9 %custom-call.10 = f32[1,64,64]{1,2,0:T(8,128)S(1)} custom-call(f32[1,64,64]{2,1,0:T(8,128)S(1)} %fusion.35), custom_call_target="InvertDiagBlocksLowerTriangular" | custom-call | tf_op jit(solution)/shard_map/jit(_cho_solve)/triangular_solve | solution.py:108
  143.7 21.8 %all-to-all-done.1 = f32[8,144,512]{2,1,0:T(8,128)S(1)} async-done(((f32[8,144,512]{2,1,0:T(8,128)}), f32[8,144,512]{2,1,0:T(8,128)S(1)}, u32[]{:S(2)}, u32[]{:S(2)}) %all-to-all-start.1) | async-done | bytes 2359328 | tf_op jit(solution)/shard_map/all_to_all | solution.py:104
  165.9 3.4 %collective-permute-start.5 = (f32[128,320]{1,0:T(8,128)S(1)}, f32[128,320]{1,0:T(8,128)S(1)}, u32[]{:S(2)}, u32[]{:S(2)}) collective-permute-start(f32[128,320]{1,0:T(8,128)S(1)} %pad_maximum_fusion.18), channel_id=1, source_target_pairs={{0,8},{8,0},{16,24},{24,16},{32,40},{40,32},{48,56},{56,48},{64,72... | collective-permute-start | bytes 491528 | tf_op jit(solution)/shard_map/ppermute | solution.py:114
  169.5 0.8 collective-permute-done.5
  170.5 1.1 convolution_subtract_fusion
  (73 shorter events, 7.4 us)
Async XLA Ops:
  6.5 104.9 %all-gather.3.cloned.1.call-start = ((), (), s32[]{:S(2)}) async-start(), calls=%async_computation.2 | async-start | bytes 4456448 | tf_op jit(solution)/shard_map/all_gather | solution.py:58
  6.5 6.6 %collective-permute-start = (bf16[32,2048]{1,0:T(8,128)(2,1)}, bf16[32,2048]{1,0:T(8,128)(2,1)S(1)}, u32[]{:S(2)}, u32[]{:S(2)}) collective-permute-start(bf16[32,2048]{1,0:T(8,128)(2,1)} %bitcast.82), channel_id=1, source_target_pairs={{0,256},{8,264},{16,272},{24,280},{32,288},{40,296},{48,304},{56,3... | collective-permute-start | bytes 393224 | tf_op jit(solution)/shard_map/ppermute | solution.py:56
  14.9 2.0 %copy-start.7 = (s32[64]{0:T(128)S(1)}, s32[64]{0:T(128)}, u32[]{:S(2)}) copy-start(s32[64]{0:T(128)} %param.9) | copy-start | bytes 772
  14.9 2.0 %copy-start.8 = (s32[64]{0:T(128)S(1)}, s32[64]{0:T(128)}, u32[]{:S(2)}) copy-start(s32[64]{0:T(128)} %param.8) | copy-start | bytes 772
  16.9 1.0 copy-start.1
  16.9 1.4 copy-start.3
  18.3 34.8 %copy-start = (f32[256,2048]{1,0:T(8,128)S(1)}, f32[256,2048]{1,0:T(8,128)}, u32[]{:S(2)}) copy-start(f32[256,2048]{1,0:T(8,128)} %param.6) | copy-start | bytes 6291460
  20.0 15.9 %all-to-all-start = ((f32[8,64,256]{2,1,0:T(8,128)}), f32[8,64,256]{2,1,0:T(8,128)S(1)}, u32[]{:S(2)}, u32[]{:S(2)}) async-start(f32[8,64,256]{2,1,0:T(8,128)} %broadcast_in_dim.16), calls=%async_computation | async-start | bytes 1048576 | tf_op jit(solution)/shard_map/all_to_all | solution.py:66
  36.2 12.9 %collective-permute-start.2 = (f32[16,128]{1,0:T(8,128)S(1)}, f32[16,128]{1,0:T(8,128)S(1)}, u32[]{:S(2)}, u32[]{:S(2)}) collective-permute-start(f32[16,128]{1,0:T(8,128)S(1)} %pad_maximum_fusion.22), channel_id=1, source_target_pairs={{0,0},{1,8},{2,16},{3,24},{4,32},{5,40},{6,48},{7,56},{8,64},{9,72... | collective-permute-start | bytes 24584 | tf_op jit(solution)/shard_map/ppermute | solution.py:72
  49.2 5.8 %collective-permute-start.3 = (f32[48,128]{1,0:T(8,128)S(1)}, f32[48,128]{1,0:T(8,128)S(1)}, u32[]{:S(2)}, u32[]{:S(2)}) collective-permute-start(f32[48,128]{1,0:T(8,128)S(1)} %maximum_maximum_fusion), channel_id=1, source_target_pairs={{0,256},{8,264},{16,272},{24,280},{32,288},{40,296},{48,304},{56,3... | collective-permute-start | bytes 73736 | tf_op jit(solution)/shard_map/ppermute | solution.py:76
  53.1 55.3 %collective-permute-start.1 = (f32[256,2048]{1,0:T(8,128)S(1)}, f32[256,2048]{1,0:T(8,128)}, u32[]{:S(2)}, u32[]{:S(2)}) collective-permute-start(f32[256,2048]{1,0:T(8,128)S(1)} %copy-done), channel_id=1, source_target_pairs={{0,8},{8,0},{16,24},{24,16},{32,40},{40,32},{48,56},{56,48},{64,72... | collective-permute-start | bytes 6291464 | tf_op jit(solution)/shard_map/ppermute | solution.py:60
  98.1 7.6 %collective-permute-start.4 = (f32[16,64,128]{2,1,0:T(8,128)S(1)}, f32[16,64,128]{2,1,0:T(8,128)}, u32[]{:S(2)}, u32[]{:S(2)}) collective-permute-start(f32[16,64,128]{2,1,0:T(8,128)S(1)} %bitcast.73), channel_id=1, source_target_pairs={{0,8},{8,0},{16,24},{24,16},{32,40},{40,32},{48,56},{56,48},{64,72... | collective-permute-start | bytes 1572872 | tf_op jit(solution)/shard_map/ppermute | solution.py:82
  111.4 2.9 %copy-start.4 = (bf16[256,2048]{1,0:T(8,128)(2,1)S(1)}, bf16[256,2048]{1,0:T(8,128)(2,1)}, u32[]{:S(2)}) copy-start(bf16[256,2048]{1,0:T(8,128)(2,1)} %copy-done.3) | copy-start | bytes 3145732
  111.4 2.9 %copy-start.6 = (bf16[256,2048]{1,0:T(8,128)(2,1)S(1)}, bf16[256,2048]{1,0:T(8,128)(2,1)}, u32[]{:S(2)}) copy-start(bf16[256,2048]{1,0:T(8,128)(2,1)} %get-tuple-element.8) | copy-start | bytes 3145732
  118.0 1.2 copy-start.2
  122.9 1.2 copy-start.5
  126.0 5.1 %copy-start.9 = (f32[64]{0:T(128)S(1)}, f32[64]{0:T(128)}, u32[]{:S(2)}) copy-start(f32[64]{0:T(128)} %param.11) | copy-start | bytes 772
  126.0 5.1 %copy-start.10 = (s32[64]{0:T(128)S(1)}, s32[64]{0:T(128)}, u32[]{:S(2)}) copy-start(s32[64]{0:T(128)} %param.10) | copy-start | bytes 772
  126.0 39.5 %all-to-all-start.1 = ((f32[8,144,512]{2,1,0:T(8,128)}), f32[8,144,512]{2,1,0:T(8,128)S(1)}, u32[]{:S(2)}, u32[]{:S(2)}) async-start(f32[8,144,512]{2,1,0:T(8,128)} %pad_maximum_fusion), calls=%async_computation.1 | async-start | bytes 4718592 | tf_op jit(solution)/shard_map/all_to_all | solution.py:104
  165.9 4.4 %collective-permute-start.5 = (f32[128,320]{1,0:T(8,128)S(1)}, f32[128,320]{1,0:T(8,128)S(1)}, u32[]{:S(2)}, u32[]{:S(2)}) collective-permute-start(f32[128,320]{1,0:T(8,128)S(1)} %pad_maximum_fusion.18), channel_id=1, source_target_pairs={{0,8},{8,0},{16,24},{24,16},{32,40},{40,32},{48,56},{56,48},{64,72... | collective-permute-start | bytes 491528 | tf_op jit(solution)/shard_map/ppermute | solution.py:114
Sparse Core Ops, SparseCore 0:
  15.0 80.6 all-gather.2

commit v3 on v2

--- a/solution.py
+++ b/solution.py
@@ -19,6 +19,7 @@
 ROWS = [(y, z, core) for y in range(Y) for z in range(Z) for core in range(CORES)]
 OTHER_CORE = [(row_of(y, z, k), row_of(y, z, 1 - k)) for y, z, k in ROWS]
 OTHER_Y = [(row_of(y, z, k), row_of(1 - y, z, k)) for y, z, k in ROWS]
+ALONG_Z_CORE = [[row_of(y, z, k) for z in range(Z) for k in range(CORES)] for y in range(Y)]
 ALONG_Z = [[row_of(y, z, k) for z in range(Z)] for y in range(Y) for k in range(CORES)]
 TO_COLUMN = [
     ((8 * a + b) * COLS + c, (8 * b + c) * COLS + a)
@@ -54,15 +55,16 @@
 
     loads = injections.T
     other_loads = lax.ppermute(loads, "row", OTHER_Y)
-    pair = in_order(y, loads, other_loads)
-    gathered = lax.all_gather(pair, "row", axis_index_groups=ALONG_Z, axis=0)
-
-    other_rows = lax.ppermute(sensitivity, "row", OTHER_CORE)
 
     high, low = split(sensitivity)
     col_select = incidence_of(col * col_count + jnp.arange(col_count, dtype=jnp.int32), from_node, to_node)
     row_select = incidence_of(row * row_count + jnp.arange(row_count, dtype=jnp.int32), from_node, to_node)
     part = nt(col_select.T, high) + nt(col_select.T, low)
+    part, other_loads = lax.optimization_barrier((part, other_loads))
+
+    pair = in_order(y, loads, other_loads)
+    gathered = lax.all_gather(pair, "row", axis_index_groups=ALONG_Z_CORE, axis=0)
+
     parts = lax.all_to_all(jnp.broadcast_to(part[None], (COLS,) + part.shape), "col", 0, 0, tiled=True)
     columns_t = jnp.sum(parts, axis=0)
 
@@ -85,23 +87,23 @@
     ends = in_order(core, line[:, : Y * h], other_line[:, : Y * h])
     ends = ends.reshape(CORES, Z, Y, h, 2, BR).transpose(2, 1, 0, 4, 3, 5).reshape(col_count, BR)
 
-    other_high, other_low = split(other_rows)
-    both_high = jnp.concatenate([high, other_high], axis=0)
-    both_low = jnp.concatenate([low, other_low], axis=0)
     ends = jnp.concatenate(split(ends), axis=1)
+    everything = gathered.reshape(Z * CORES * Y * slots, col_count)
+    sums = nt(everything, high) + nt(everything, low)
+    end_sums = jnp.dot(everything, ends, preferred_element_type=F32)
+    end_sums = end_sums[:, :BR] + end_sums[:, BR:]
     zs = Z * Y // COLS
-    count = zs * slots
-    sums, end_sums = [], []
-    for side in range(Y):
-        part_loads = gathered[:, side].reshape(Z * slots, col_count)
-        sums.append(nt(part_loads, both_high) + nt(part_loads, both_low))
-        end_part = jnp.dot(part_loads, ends, preferred_element_type=F32)
-        end_sums.append(end_part[:, :BR] + end_part[:, BR:])
-    sums = jnp.stack(sums).reshape(COLS, count, CORES * row_count)
-    fold = CORES * row_count // BR
-    end_sums = jnp.stack(end_sums).reshape(COLS, fold, count // fold, BR)
+    count = zs * CORES * slots
+
+    def by_block(values):
+        values = values.reshape(Z // zs, zs * CORES, Y, slots, values.shape[1]).transpose(2, 0, 1, 3, 4)
+        return values.reshape(COLS, count, values.shape[4])
+
+    fold = row_count // BR
+    end_sums = by_block(end_sums).reshape(COLS, fold, count // fold, BR)
     end_sums = end_sums.transpose(0, 2, 1, 3).reshape(COLS, count // fold, fold * BR)
-    arrived = lax.all_to_all(jnp.concatenate([sums, end_sums], axis=1), "col", 0, 0, tiled=True)
+    packed = jnp.concatenate([by_block(sums), end_sums], axis=1)
+    arrived = lax.all_to_all(packed, "col", 0, 0, tiled=True)
 
     reach = impedance * (1.0 + 3.0 * switch_flags.astype(F32))
     factor = jnp.linalg.cholesky(capacity + jnp.diag(reach))
@@ -109,15 +111,10 @@
 
     total = jnp.sum(arrived, axis=0)
     end_total = total[count:].reshape(count // fold, fold, BR).transpose(1, 0, 2).reshape(count, BR)
-    mine = jnp.concatenate([total[:count, :row_count], end_total], axis=1)
-    give = jnp.concatenate([total[:count, row_count:], end_total], axis=1)
-    taken = lax.ppermute(give, "row", OTHER_CORE)
-    result = in_order(core, mine, taken).reshape(CORES, zs, slots, row_count + BR)
-    result = result.transpose(1, 0, 2, 3).reshape(CORES * count, row_count + BR)
     drop = lax.dot_general(
-        solved, result[:, row_count:], (((0,), (1,)), ((), ())), precision=HIGH, preferred_element_type=F32
+        solved, end_total, (((0,), (1,)), ((), ())), precision=HIGH, preferred_element_type=F32
     )
-    return result[:, :row_count].T - drop
+    return total[:count].T - drop
 
 
 def solution(mesh):

time: 179 us -> 180 us (level)
  matrix products: 11.9 us -> 21.9 us
  other arithmetic: 23.3 us -> 17.8 us
  starting transfers between devices: 43.7 us -> 40.8 us
  blocking collectives: 42.9 us -> 40.5 us
    dot_general x6 -> x4, matrix products: 7.97 us -> 17.1 us  [nt(): lax.dot_general(left, right, (((1,), (1,)), ((), ())), preferred_element_...]
    ppermute x2 -> x0, starting transfers between devices: 5.27 us -> none  [the longest x1 3.35 us: on_device(): taken = lax.ppermute(give, 'row', OTHER_CORE)]
    convert_element_type x3 -> x1, other arithmetic: 5.19 us -> 0.17 us  [split(): return (high.astype(BF16), (values - high).astype(BF16))]
    all_to_all x1, waiting for transfers between devices: 21.8 us -> 25.1 us  [on_device(): arrived = lax.all_to_all(packed, 'col', 0, 0, tiled=True)]
    slice x3 -> x1, local copies, waits for them, and re-layouts: 2.91 us -> 0.02 us  [on_device(): return total[:count].T - drop]
    ppermute x1, starting transfers between devices: 5.98 us -> 8.77 us  [on_device(): other_line = lax.ppermute(line, 'row', OTHER_CORE)]
    ppermute x1, waiting for transfers between devices: 2.53 us -> 0.01 us  [on_device(): other_loads = lax.ppermute(loads, 'row', OTHER_Y)]
    all_gather x1, blocking collectives: 42.9 us -> 40.5 us  [on_device(): line = lax.all_gather(both, 'row', axis_index_groups=ALONG_Z, axis=0)]
  transfers between devices with their start and end apart: 9 -> 7, of which waited for: 6 -> 5; matrix products, arithmetic and copies ran while one was open for 13% -> 11% of each run, Pallas kernels for 0% -> 0%
where the time goes in v3:
time: 180 us; the launch traced here: 179 us
  starting transfers between devices  40.8 us (23%)
  blocking collectives  40.5 us (22%)
  waiting for transfers between devices  37.3 us (21%)
  matrix products  21.9 us (12%)
  other arithmetic  17.8 us (10%)
  between operations  13.8 us (8%)
  local copies, waits for them, and re-layouts  7.04 us (4%)
    all_gather x1, blocking collectives, on_device(): line = lax.all_gather(both, 'row', axis_index_groups=ALONG_Z, axis=0)  40.5 us
    all_to_all x1, waiting for transfers between devices, on_device(): arrived = lax.all_to_all(packed, 'col', 0, 0, tiled=True)  25.1 us
    dot_general x4, matrix products, nt(): lax.dot_general(left, right, (((1,), (1,)), ((), ())), preferred_element_...  17.1 us
    ppermute x1, starting transfers between devices, on_device(): piece = lax.ppermute(piece, ('row', 'col'), TO_COLUMN)  12.1 us
    ppermute x1, starting transfers between devices, on_device(): other_line = lax.ppermute(line, 'row', OTHER_CORE)  8.77 us
    all_to_all x1, waiting for transfers between devices, on_device(): lax.all_to_all(jnp.broadcast_to(part[None], (COLS,) + part.shape), 'col',...  8.59 us
    another operation x3, other arithmetic, on_device(): factor = jnp.linalg.cholesky(capacity + jnp.diag(reach))  6.52 us
    all_to_all x1, starting transfers between devices, on_device(): lax.all_to_all(jnp.broadcast_to(part[None], (COLS,) + part.shape), 'col',...  6.4 us
  transfers between devices with their start and end apart: 7, of which 5 were waited for; matrix products, arithmetic and copies ran while one was open for 11% of the time, Pallas kernels for 0%

profile of v3, /device:TPU:1, one launch (start us, length us, event | category | flops | bytes accessed | tf_op | source)
XLA Modules:
  0.0 179.1 jit_solution(13149594700741083166)
XLA Ops:
  6.5 4.2 %collective-permute-start = (bf16[32,2048]{1,0:T(8,128)(2,1)}, bf16[32,2048]{1,0:T(8,128)(2,1)S(1)}, u32[]{:S(2)}, u32[]{:S(2)}) collective-permute-start(bf16[32,2048]{1,0:T(8,128)(2,1)} %bitcast.62), channel_id=1, source_target_pairs={{0,256},{8,264},{16,272},{24,280},{32,288},{40,296},{48,304},{56,3... | collective-permute-start | bytes 393224 | tf_op jit(solution)/shard_map/ppermute | solution.py:57
  10.7 2.5 %fusion.5 = f32[64,256]{1,0:T(8,128)S(1)} fusion(s32[64]{0:T(128)} %param.9, s32[64]{0:T(128)} %param.8, s32[2048]{0:T(1024)S(1)} %iota_add_fusion, f32[256,2048]{1,0:T(8,128)} %param.6), kind=kOutput, calls=%fused_computation.15 | convolution fusion | flops 68812800 | bytes 2171392 | tf_op jit(solution)/shard_map/dot_general | solution.py:46
  13.3 0.9 convolution_add_fusion.1
  14.3 0.7 maximum_select_fusion.1
  15.0 0.9 broadcast_in_dim.16
  15.9 6.4 %all-to-all-start = ((f32[8,64,256]{2,1,0:T(8,128)}), f32[8,64,256]{2,1,0:T(8,128)S(1)}, u32[]{:S(2)}, u32[]{:S(2)}) async-start(f32[8,64,256]{2,1,0:T(8,128)} %broadcast_in_dim.16), calls=%async_computation | async-start | bytes 1048576 | tf_op jit(solution)/shard_map/all_to_all | solution.py:68
  22.3 8.6 %all-to-all-done = f32[8,64,256]{2,1,0:T(8,128)S(1)} async-done(((f32[8,64,256]{2,1,0:T(8,128)}), f32[8,64,256]{2,1,0:T(8,128)S(1)}, u32[]{:S(2)}, u32[]{:S(2)}) %all-to-all-start) | async-done | bytes 524320 | tf_op jit(solution)/shard_map/all_to_all | solution.py:68
  31.1 12.1 %collective-permute-start.1 = (f32[16,128]{1,0:T(8,128)S(1)}, f32[16,128]{1,0:T(8,128)S(1)}, u32[]{:S(2)}, u32[]{:S(2)}) collective-permute-start(f32[16,128]{1,0:T(8,128)S(1)} %pad_maximum_fusion.2), channel_id=1, source_target_pairs={{0,0},{1,8},{2,16},{3,24},{4,32},{5,40},{6,48},{7,56},{8,64},{9,72... | collective-permute-start | bytes 24584 | tf_op jit(solution)/shard_map/ppermute | solution.py:74
  43.5 0.5 collective-permute-done.1
  44.1 3.9 %collective-permute-start.2 = (f32[48,128]{1,0:T(8,128)S(1)}, f32[48,128]{1,0:T(8,128)S(1)}, u32[]{:S(2)}, u32[]{:S(2)}) collective-permute-start(f32[48,128]{1,0:T(8,128)S(1)} %maximum_maximum_fusion), channel_id=1, source_target_pairs={{0,256},{8,264},{16,272},{24,280},{32,288},{40,296},{48,304},{56,3... | collective-permute-start | bytes 73736 | tf_op jit(solution)/shard_map/ppermute | solution.py:78
  48.0 1.6 collective-permute-done.2
  49.7 40.5 %all-gather = f32[1024,128]{1,0:T(8,128)S(1)} all-gather(f32[64,128]{1,0:T(8,128)S(1)} %pad_maximum_fusion.1), channel_id=2, replica_groups={{0,16,32,48,64,80,96,112,128,144,160,176,192,208,224,240},{8,24,40,56,7..., dimensions={0}, use_global_device_ids=true | all-gather | bytes 557056 | tf_op jit(solution)/shard_map/all_gather | solution.py:83
  90.2 8.8 %collective-permute-start.3 = (f32[16,64,128]{2,1,0:T(8,128)S(1)}, f32[16,64,128]{2,1,0:T(8,128)}, u32[]{:S(2)}, u32[]{:S(2)}) collective-permute-start(f32[16,64,128]{2,1,0:T(8,128)S(1)} %bitcast.58), channel_id=1, source_target_pairs={{0,8},{8,0},{16,24},{24,16},{32,40},{40,32},{48,56},{56,48},{64,72... | collective-permute-start | bytes 1572872 | tf_op jit(solution)/shard_map/ppermute | solution.py:84
  99.0 1.5 collective-permute-done.3
  100.4 1.1 fusion.34
  102.2 0.6 fusion.2
  103.1 7.3 %fusion.17 = f32[2048,256]{1,0:T(8,128)} fusion(bf16[2048,2048]{1,0:T(8,128)(2,1)} %bitcast.50, f32[256,2048]{1,0:T(8,128)S(1)} %copy-done), kind=kOutput, calls=%fused_computation.27 | convolution fusion | flops 2148532224 | bytes 12582912 | tf_op jit(solution)/shard_map/dot_general | solution.py:46
  110.4 3.0 %fusion.7 = f32[2048,128]{0,1:T(8,128)S(1)} fusion(bf16[2048,2048]{1,0:T(8,128)(2,1)S(1)} %bitcast.54, bf16[2048,64]{1,0:T(8,128)(2,1)S(1)} %get-tuple-element.10, bf16[2048,64]{1,0:T(8,128)(2,1)S(1)} %get-tuple-element.9), kind=kOutput, calls=%fused_computation.17 | convolution fusion | flops 1074790400 | bytes 9961472 | tf_op jit(solution)/shard_map/dot_general | solution.py:93
  113.4 0.9 slice_add_fusion
  114.3 1.4 copy.32
  115.8 0.7 copy.34
  116.5 1.4 reshape.127
  117.9 6.4 %convolution_add_fusion = f32[2048,256]{1,0:T(8,128)S(1)} fusion(f32[2048,256]{1,0:T(8,128)} %fusion.17, bf16[2048,2048]{1,0:T(8,128)(2,1)} %bitcast.51, f32[256,2048]{1,0:T(8,128)S(1)} %copy-done), kind=kOutput, calls=%fused_computation.3 | convolution fusion | flops 2149580800 | bytes 14680064 | tf_op jit(solution)/shard_map/dot_general | solution.py:46
  124.4 0.9 copy-done.1
  125.3 1.7 pad_maximum_fusion
  127.0 5.4 %all-to-all-start.1 = ((f32[8,320,256]{2,1,0:T(8,128)}), f32[8,320,256]{2,1,0:T(8,128)S(1)}, u32[]{:S(2)}, u32[]{:S(2)}) async-start(f32[8,320,256]{2,1,0:T(8,128)} %pad_maximum_fusion), calls=%async_computation.1 | async-start | bytes 5242880 | tf_op jit(solution)/shard_map/all_to_all | solution.py:106
  132.7 5.8 %cholesky.16 = f32[64,64]{1,0:T(8,128)S(1)} custom-call(f32[64,64]{1,0:T(8,128)S(1)} %fusion.32), custom_call_target="Cholesky" | custom-call | tf_op jit(solution)/shard_map/jit(cholesky)/cholesky | solution.py:109
  138.6 0.6 compare_reduce_fusion
  139.2 0.7 fusion.27
  139.9 4.9 %custom-call.10 = f32[1,64,64]{1,2,0:T(8,128)S(1)} custom-call(f32[1,64,64]{2,1,0:T(8,128)S(1)} %fusion.27), custom_call_target="InvertDiagBlocksLowerTriangular" | custom-call | tf_op jit(solution)/shard_map/jit(_cho_solve)/triangular_solve | solution.py:110
  145.3 25.1 %all-to-all-done.1 = f32[8,320,256]{2,1,0:T(8,128)S(1)} async-done(((f32[8,320,256]{2,1,0:T(8,128)}), f32[8,320,256]{2,1,0:T(8,128)S(1)}, u32[]{:S(2)}, u32[]{:S(2)}) %all-to-all-start.1) | async-done | bytes 2621472 | tf_op jit(solution)/shard_map/all_to_all | solution.py:106
  171.1 1.1 convolution_subtract_fusion
  (57 shorter events, 3.3 us)
Async XLA Ops:
  6.5 6.8 %copy-start = (f32[256,2048]{1,0:T(8,128)S(1)}, f32[256,2048]{1,0:T(8,128)}, u32[]{:S(2)}) copy-start(f32[256,2048]{1,0:T(8,128)} %param.6) | copy-start | bytes 6291460
  6.5 6.8 %copy-start.3 = (s32[64]{0:T(128)S(1)}, s32[64]{0:T(128)}, u32[]{:S(2)}) copy-start(s32[64]{0:T(128)} %param.9) | copy-start | bytes 772
  6.5 6.8 %copy-start.4 = (s32[64]{0:T(128)S(1)}, s32[64]{0:T(128)}, u32[]{:S(2)}) copy-start(s32[64]{0:T(128)} %param.8) | copy-start | bytes 772
  6.5 96.6 %all-gather.3.cloned.1.call-start = ((), (), s32[]{:S(2)}) async-start(), calls=%async_computation.2 | async-start | bytes 8650752 | tf_op jit(solution)/shard_map/all_gather | solution.py:66
  6.5 7.7 %collective-permute-start = (bf16[32,2048]{1,0:T(8,128)(2,1)}, bf16[32,2048]{1,0:T(8,128)(2,1)S(1)}, u32[]{:S(2)}, u32[]{:S(2)}) collective-permute-start(bf16[32,2048]{1,0:T(8,128)(2,1)} %bitcast.62), channel_id=1, source_target_pairs={{0,256},{8,264},{16,272},{24,280},{32,288},{40,296},{48,304},{56,3... | collective-permute-start | bytes 393224 | tf_op jit(solution)/shard_map/ppermute | solution.py:57
  10.7 3.5 %copy-start.2 = (bf16[2048,32]{0,1:T(8,128)(2,1)S(1)}, bf16[2048,32]{0,1:T(8,128)(2,1)}, u32[]{:S(2)}) copy-start(bf16[2048,32]{0,1:T(8,128)(2,1)} %param.7) | copy-start | bytes 393220
  15.9 15.0 %all-to-all-start = ((f32[8,64,256]{2,1,0:T(8,128)}), f32[8,64,256]{2,1,0:T(8,128)S(1)}, u32[]{:S(2)}, u32[]{:S(2)}) async-start(f32[8,64,256]{2,1,0:T(8,128)} %broadcast_in_dim.16), calls=%async_computation | async-start | bytes 1048576 | tf_op jit(solution)/shard_map/all_to_all | solution.py:68
  31.1 12.9 %collective-permute-start.1 = (f32[16,128]{1,0:T(8,128)S(1)}, f32[16,128]{1,0:T(8,128)S(1)}, u32[]{:S(2)}, u32[]{:S(2)}) collective-permute-start(f32[16,128]{1,0:T(8,128)S(1)} %pad_maximum_fusion.2), channel_id=1, source_target_pairs={{0,0},{1,8},{2,16},{3,24},{4,32},{5,40},{6,48},{7,56},{8,64},{9,72... | collective-permute-start | bytes 24584 | tf_op jit(solution)/shard_map/ppermute | solution.py:74
  44.1 5.5 %collective-permute-start.2 = (f32[48,128]{1,0:T(8,128)S(1)}, f32[48,128]{1,0:T(8,128)S(1)}, u32[]{:S(2)}, u32[]{:S(2)}) collective-permute-start(f32[48,128]{1,0:T(8,128)S(1)} %maximum_maximum_fusion), channel_id=1, source_target_pairs={{0,256},{8,264},{16,272},{24,280},{32,288},{40,296},{48,304},{56,3... | collective-permute-start | bytes 73736 | tf_op jit(solution)/shard_map/ppermute | solution.py:78
  90.2 10.2 %collective-permute-start.3 = (f32[16,64,128]{2,1,0:T(8,128)S(1)}, f32[16,64,128]{2,1,0:T(8,128)}, u32[]{:S(2)}, u32[]{:S(2)}) collective-permute-start(f32[16,64,128]{2,1,0:T(8,128)S(1)} %bitcast.58), channel_id=1, source_target_pairs={{0,8},{8,0},{16,24},{24,16},{32,40},{40,32},{48,56},{56,48},{64,72... | collective-permute-start | bytes 1572872 | tf_op jit(solution)/shard_map/ppermute | solution.py:84
  103.1 7.3 %slice-start = ((s8[8388608]{0:T(1024)(128)(4,1)}), s8[4194304]{0:T(1024)(128)(4,1)S(1)}, s32[]{:S(2)}) async-start(s8[8388608]{0:T(1024)(128)(4,1)} %bitcast.52), calls=%async_computation.3 | async-start | bytes 8388608
  103.1 7.3 %slice-start.1 = ((s8[8388608]{0:T(1024)(128)(4,1)}), s8[4194304]{0:T(1024)(128)(4,1)S(1)}, s32[]{:S(2)}) async-start(s8[8388608]{0:T(1024)(128)(4,1)} %bitcast.52), calls=%async_computation.4 | async-start | bytes 8388608
  124.3 1.0 copy-start.1
  127.0 5.4 %copy-start.5 = (f32[64]{0:T(128)S(1)}, f32[64]{0:T(128)}, u32[]{:S(2)}) copy-start(f32[64]{0:T(128)} %param.11) | copy-start | bytes 772
  127.0 5.5 %copy-start.6 = (s32[64]{0:T(128)S(1)}, s32[64]{0:T(128)}, u32[]{:S(2)}) copy-start(s32[64]{0:T(128)} %param.10) | copy-start | bytes 772
  127.0 43.4 %all-to-all-start.1 = ((f32[8,320,256]{2,1,0:T(8,128)}), f32[8,320,256]{2,1,0:T(8,128)S(1)}, u32[]{:S(2)}, u32[]{:S(2)}) async-start(f32[8,320,256]{2,1,0:T(8,128)} %pad_maximum_fusion), calls=%async_computation.1 | async-start | bytes 5242880 | tf_op jit(solution)/shard_map/all_to_all | solution.py:106
Sparse Core Ops, SparseCore 0:
  15.1 87.2 all-gather.2

commit v4 on v3

--- a/solution.py
+++ b/solution.py
@@ -1,6 +1,8 @@
 import jax
 import jax.numpy as jnp
 from jax import lax
+from jax.experimental import pallas as pl
+from jax.experimental.pallas import tpu as pltpu
 from jax.sharding import PartitionSpec as P
 
 HIGH = lax.Precision.HIGHEST
@@ -46,6 +48,37 @@
     return lax.dot_general(left, right, (((1,), (1,)), ((), ())), preferred_element_type=F32)
 
 
+def products(loads, weights, ends):
+    blocks, lines, sides, slots, nodes = loads.shape
+    rows = weights.shape[1] // 2
+    count = lines * slots
+    fold = rows // BR
+
+    def body(loads_ref, weights_ref, ends_ref, out_ref):
+        tile = loads_ref[...].reshape(count, nodes)
+        sums = jnp.dot(tile, weights_ref[...], preferred_element_type=F32)
+        out_ref[0, :count] = sums[:, :rows] + sums[:, rows:]
+        end_sums = jnp.dot(tile, ends_ref[...], preferred_element_type=F32)
+        end_sums = end_sums[:, :BR] + end_sums[:, BR:]
+        step = count // fold
+        folded = [end_sums[i * step:(i + 1) * step] for i in range(fold)]
+        out_ref[0, count:] = jnp.concatenate(folded, axis=1)
+
+    height = count + count // fold
+    return pl.pallas_call(
+        body,
+        grid=(sides, blocks),
+        in_specs=[
+            pl.BlockSpec((1, lines, 1, slots, nodes), lambda side, block: (block, 0, side, 0, 0)),
+            pl.BlockSpec(weights.shape, lambda side, block: (0, 0)),
+            pl.BlockSpec(ends.shape, lambda side, block: (0, 0)),
+        ],
+        out_specs=pl.BlockSpec((1, height, rows), lambda side, block: (side * blocks + block, 0, 0)),
+        out_shape=jax.ShapeDtypeStruct((sides * blocks, height, rows), F32),
+        compiler_params=pltpu.CompilerParams(vmem_limit_bytes=32 * 1024 * 1024),
+    )(loads, weights, ends)
+
+
 def on_device(sensitivity, injections, from_node, to_node, switch_flags, impedance):
     row_count, col_count = sensitivity.shape
     row = lax.axis_index("row")
@@ -61,6 +94,7 @@
     row_select = incidence_of(row * row_count + jnp.arange(row_count, dtype=jnp.int32), from_node, to_node)
     part = nt(col_select.T, high) + nt(col_select.T, low)
     part, other_loads = lax.optimization_barrier((part, other_loads))
+    weights = jnp.concatenate([high.T, low.T], axis=1)
 
     pair = in_order(y, loads, other_loads)
     gathered = lax.all_gather(pair, "row", axis_index_groups=ALONG_Z_CORE, axis=0)
@@ -87,22 +121,14 @@
     ends = in_order(core, line[:, : Y * h], other_line[:, : Y * h])
     ends = ends.reshape(CORES, Z, Y, h, 2, BR).transpose(2, 1, 0, 4, 3, 5).reshape(col_count, BR)
 
-    ends = jnp.concatenate(split(ends), axis=1)
-    everything = gathered.reshape(Z * CORES * Y * slots, col_count)
-    sums = nt(everything, high) + nt(everything, low)
-    end_sums = jnp.dot(everything, ends, preferred_element_type=F32)
-    end_sums = end_sums[:, :BR] + end_sums[:, BR:]
     zs = Z * Y // COLS
     count = zs * CORES * slots
-
-    def by_block(values):
-        values = values.reshape(Z // zs, zs * CORES, Y, slots, values.shape[1]).transpose(2, 0, 1, 3, 4)
-        return values.reshape(COLS, count, values.shape[4])
-
     fold = row_count // BR
-    end_sums = by_block(end_sums).reshape(COLS, fold, count // fold, BR)
-    end_sums = end_sums.transpose(0, 2, 1, 3).reshape(COLS, count // fold, fold * BR)
-    packed = jnp.concatenate([by_block(sums), end_sums], axis=1)
+    packed = products(
+        gathered.reshape(Z // zs, zs * CORES, Y, slots, col_count),
+        weights,
+        jnp.concatenate(split(ends), axis=1),
+    )
     arrived = lax.all_to_all(packed, "col", 0, 0, tiled=True)
 
     reach = impedance * (1.0 + 3.0 * switch_flags.astype(F32))

time: 180 us -> 174 us (0.967)
  matrix products: 21.9 us -> 3.12 us
  Pallas kernels: 0 us -> 10.4 us
    dot_general x4 -> x2, matrix products: 17.1 us -> 1.28 us  [nt(): lax.dot_general(left, right, (((1,), (1,)), ((), ())), preferred_element_...]
    pallas_call x0 -> x1, Pallas kernels: none -> 10.4 us  [products(): pl.pallas_call(body, grid=(sides, blocks), in_specs=[pl.BlockSpec((1, lin...]
    unnamed x20 -> x15, local copies, waits for them, and re-layouts: 1.12 us -> 5.53 us
    dot_general x1 -> x0, matrix products: 2.98 us -> none  [on_device(): end_sums = jnp.dot(everything, ends, preferred_element_type=F32)]
  transfers between devices with their start and end apart: 7 -> 7, of which waited for: 5 -> 4; matrix products, arithmetic and copies ran while one was open for 11% -> 14% of each run, Pallas kernels for 0% -> 0%
where the time goes in v4:
time: 174 us; the launch traced here: 173 us
  blocking collectives  42.3 us (24%)
  starting transfers between devices  40.7 us (23%)
  waiting for transfers between devices  36.2 us (21%)
  other arithmetic  18.5 us (11%)
  between operations  13.7 us (8%)
  Pallas kernels  10.4 us (6%)
  local copies, waits for them, and re-layouts  7.76 us (4%)
  matrix products  3.12 us (2%)
    all_gather x1, blocking collectives, on_device(): line = lax.all_gather(both, 'row', axis_index_groups=ALONG_Z, axis=0)  42.3 us
    all_to_all x1, waiting for transfers between devices, on_device(): arrived = lax.all_to_all(packed, 'col', 0, 0, tiled=True)  25.4 us
    ppermute x1, starting transfers between devices, on_device(): piece = lax.ppermute(piece, ('row', 'col'), TO_COLUMN)  12.1 us
    pallas_call x1, Pallas kernels, products(): pl.pallas_call(body, grid=(sides, blocks), in_specs=[pl.BlockSpec((1, lin...  10.4 us
    ppermute x1, starting transfers between devices, on_device(): other_line = lax.ppermute(line, 'row', OTHER_CORE)  9.94 us
    all_to_all x1, waiting for transfers between devices, on_device(): lax.all_to_all(jnp.broadcast_to(part[None], (COLS,) + part.shape), 'col',...  8.59 us
    all_to_all x1, starting transfers between devices, on_device(): lax.all_to_all(jnp.broadcast_to(part[None], (COLS,) + part.shape), 'col',...  6.58 us
    another operation x3, other arithmetic, on_device(): factor = jnp.linalg.cholesky(capacity + jnp.diag(reach))  6.52 us
  transfers between devices with their start and end apart: 7, of which 4 were waited for; matrix products, arithmetic and copies ran while one was open for 14% of the time, Pallas kernels for 0%

profile of v4, /device:TPU:1, one launch (start us, length us, event | category | flops | bytes accessed | tf_op | source)
XLA Modules:
  0.0 172.7 jit_solution(15824154356364864359)
XLA Ops:
  6.5 4.0 %collective-permute-start = (bf16[32,2048]{1,0:T(8,128)(2,1)}, bf16[32,2048]{1,0:T(8,128)(2,1)S(1)}, u32[]{:S(2)}, u32[]{:S(2)}) collective-permute-start(bf16[32,2048]{1,0:T(8,128)(2,1)} %bitcast.43), channel_id=1, source_target_pairs={{0,256},{8,264},{16,272},{24,280},{32,288},{40,296},{48,304},{56,3... | collective-permute-start | bytes 393224 | tf_op jit(solution)/shard_map/ppermute | solution.py:90
  10.6 1.9 %copy.21 = f32[256,2048]{0,1:T(8,128)S(1)} copy(f32[256,2048]{1,0:T(8,128)} %param.6) | data formatting | bytes 4194304 | tf_op args[0]
  12.6 0.6 fusion.5
  13.2 0.6 convolution_add_fusion
  13.9 0.7 maximum_select_fusion.1
  14.7 0.9 broadcast_in_dim.16
  15.5 6.6 %all-to-all-start = ((f32[8,64,256]{2,1,0:T(8,128)}), f32[8,64,256]{2,1,0:T(8,128)S(1)}, u32[]{:S(2)}, u32[]{:S(2)}) async-start(f32[8,64,256]{2,1,0:T(8,128)} %broadcast_in_dim.16), calls=%async_computation | async-start | bytes 1048576 | tf_op jit(solution)/shard_map/all_to_all | solution.py:102
  22.1 8.6 %all-to-all-done = f32[8,64,256]{2,1,0:T(8,128)S(1)} async-done(((f32[8,64,256]{2,1,0:T(8,128)}), f32[8,64,256]{2,1,0:T(8,128)S(1)}, u32[]{:S(2)}, u32[]{:S(2)}) %all-to-all-start) | async-done | bytes 524320 | tf_op jit(solution)/shard_map/all_to_all | solution.py:102
  31.0 12.1 %collective-permute-start.1 = (f32[16,128]{1,0:T(8,128)S(1)}, f32[16,128]{1,0:T(8,128)S(1)}, u32[]{:S(2)}, u32[]{:S(2)}) collective-permute-start(f32[16,128]{1,0:T(8,128)S(1)} %pad_maximum_fusion.3), channel_id=1, source_target_pairs={{0,0},{1,8},{2,16},{3,24},{4,32},{5,40},{6,48},{7,56},{8,64},{9,72... | collective-permute-start | bytes 24584 | tf_op jit(solution)/shard_map/ppermute | solution.py:108
  43.1 0.3 fusion.18
  43.4 0.5 collective-permute-done.1
  44.0 3.9 %collective-permute-start.2 = (f32[48,128]{1,0:T(8,128)S(1)}, f32[48,128]{1,0:T(8,128)S(1)}, u32[]{:S(2)}, u32[]{:S(2)}) collective-permute-start(f32[48,128]{1,0:T(8,128)S(1)} %maximum_maximum_fusion), channel_id=1, source_target_pairs={{0,256},{8,264},{16,272},{24,280},{32,288},{40,296},{48,304},{56,3... | collective-permute-start | bytes 73736 | tf_op jit(solution)/shard_map/ppermute | solution.py:112
  47.9 1.6 collective-permute-done.2
  49.6 42.3 %all-gather = f32[1024,128]{1,0:T(8,128)} all-gather(f32[64,128]{1,0:T(8,128)S(1)} %pad_maximum_fusion.2), channel_id=2, replica_groups={{0,16,32,48,64,80,96,112,128,144,160,176,192,208,224,240},{8,24,40,56,7..., dimensions={0}, use_global_device_ids=true | all-gather | bytes 557056 | tf_op jit(solution)/shard_map/all_gather | solution.py:117
  91.8 9.9 %collective-permute-start.3 = (f32[16,64,128]{2,1,0:T(8,128)}, f32[16,64,128]{2,1,0:T(8,128)}, u32[]{:S(2)}, u32[]{:S(2)}) collective-permute-start(f32[16,64,128]{2,1,0:T(8,128)} %bitcast.11), channel_id=1, source_target_pairs={{0,8},{8,0},{16,24},{24,16},{32,40},{40,32},{48,56},{56,48},{64,72... | collective-permute-start | bytes 1572872 | tf_op jit(solution)/shard_map/ppermute | solution.py:118
  101.8 1.4 fusion.13
  103.1 1.4 pad_maximum_fusion.weights_ref
  104.5 1.3 fusion.29
  105.8 0.3 stack.50
  106.1 0.3 stack.51
  106.5 0.6 fusion.2
  107.4 0.3 pad_maximum_fusion.1.ends_ref
  107.7 3.4 %copy-done = bf16[32,2,32,2048]{3,2,1,0:T(8,128)(2,1)S(1)} copy-done((bf16[32,2,32,2048]{3,2,1,0:T(8,128)(2,1)S(1)}, bf16[32,2,32,2048]{3,2,1,0:T(8,128)(2,1)}, u32[]{:S(2)}) %copy-start) | copy-done | bytes 8388632
  111.1 10.4 %shard_map.64 = f32[8,320,256]{2,1,0:T(8,128)} custom-call(bf16[4,8,2,32,2048]{4,3,2,1,0:T(8,128)(2,1)S(1)} %bitcast.41, bf16[2048,512]{1,0:T(8,128)(2,1)S(1)} %pad_maximum_fusion.weights_ref, bf16[2048,128]{1,0:T(8,128)(2,1)S(1)} %pad_maximum_fusion.1.ends_ref), custom_call_target="tpu_custom_call" | custom-call | tf_op jit(solution)/shard_map/pallas_call | solution.py:68
  121.5 4.2 %all-to-all-start.1 = ((f32[8,320,256]{2,1,0:T(8,128)}), f32[8,320,256]{2,1,0:T(8,128)S(1)}, u32[]{:S(2)}, u32[]{:S(2)}) async-start(f32[8,320,256]{2,1,0:T(8,128)} %shard_map.64), calls=%async_computation.1 | async-start | bytes 5242880 | tf_op jit(solution)/shard_map/all_to_all | solution.py:132
  126.0 5.8 %cholesky.16 = f32[64,64]{1,0:T(8,128)S(1)} custom-call(f32[64,64]{1,0:T(8,128)S(1)} %fusion.28), custom_call_target="Cholesky" | custom-call | tf_op jit(solution)/shard_map/jit(cholesky)/cholesky | solution.py:135
  131.9 0.6 compare_reduce_fusion
  132.5 0.7 fusion.23
  133.2 4.9 %custom-call.10 = f32[1,64,64]{1,2,0:T(8,128)S(1)} custom-call(f32[1,64,64]{2,1,0:T(8,128)S(1)} %fusion.23), custom_call_target="InvertDiagBlocksLowerTriangular" | custom-call | tf_op jit(solution)/shard_map/jit(_cho_solve)/triangular_solve | solution.py:136
  138.1 0.3 fusion.26
  138.5 25.4 %all-to-all-done.1 = f32[8,320,256]{2,1,0:T(8,128)S(1)} async-done(((f32[8,320,256]{2,1,0:T(8,128)}), f32[8,320,256]{2,1,0:T(8,128)S(1)}, u32[]{:S(2)}, u32[]{:S(2)}) %all-to-all-start.1) | async-done | bytes 2621472 | tf_op jit(solution)/shard_map/all_to_all | solution.py:132
  164.7 1.1 convolution_subtract_fusion
  (45 shorter events, 1.9 us)
Async XLA Ops:
  6.5 101.2 %all-gather.3.cloned.1.call-start = ((), (), s32[]{:S(2)}) async-start(), calls=%async_computation.2 | async-start | bytes 8650752 | tf_op jit(solution)/shard_map/all_gather | solution.py:100
  6.5 7.4 %collective-permute-start = (bf16[32,2048]{1,0:T(8,128)(2,1)}, bf16[32,2048]{1,0:T(8,128)(2,1)S(1)}, u32[]{:S(2)}, u32[]{:S(2)}) collective-permute-start(bf16[32,2048]{1,0:T(8,128)(2,1)} %bitcast.43), channel_id=1, source_target_pairs={{0,256},{8,264},{16,272},{24,280},{32,288},{40,296},{48,304},{56,3... | collective-permute-start | bytes 393224 | tf_op jit(solution)/shard_map/ppermute | solution.py:90
  10.6 2.0 %copy-start.2 = (s32[64]{0:T(128)S(1)}, s32[64]{0:T(128)}, u32[]{:S(2)}) copy-start(s32[64]{0:T(128)} %param.9) | copy-start | bytes 772
  10.6 2.0 %copy-start.3 = (s32[64]{0:T(128)S(1)}, s32[64]{0:T(128)}, u32[]{:S(2)}) copy-start(s32[64]{0:T(128)} %param.8) | copy-start | bytes 772
  12.6 1.3 copy-start.1
  15.5 15.2 %all-to-all-start = ((f32[8,64,256]{2,1,0:T(8,128)}), f32[8,64,256]{2,1,0:T(8,128)S(1)}, u32[]{:S(2)}, u32[]{:S(2)}) async-start(f32[8,64,256]{2,1,0:T(8,128)} %broadcast_in_dim.16), calls=%async_computation | async-start | bytes 1048576 | tf_op jit(solution)/shard_map/all_to_all | solution.py:102
  31.0 12.9 %collective-permute-start.1 = (f32[16,128]{1,0:T(8,128)S(1)}, f32[16,128]{1,0:T(8,128)S(1)}, u32[]{:S(2)}, u32[]{:S(2)}) collective-permute-start(f32[16,128]{1,0:T(8,128)S(1)} %pad_maximum_fusion.3), channel_id=1, source_target_pairs={{0,0},{1,8},{2,16},{3,24},{4,32},{5,40},{6,48},{7,56},{8,64},{9,72... | collective-permute-start | bytes 24584 | tf_op jit(solution)/shard_map/ppermute | solution.py:108
  44.0 5.5 %collective-permute-start.2 = (f32[48,128]{1,0:T(8,128)S(1)}, f32[48,128]{1,0:T(8,128)S(1)}, u32[]{:S(2)}, u32[]{:S(2)}) collective-permute-start(f32[48,128]{1,0:T(8,128)S(1)} %maximum_maximum_fusion), channel_id=1, source_target_pairs={{0,256},{8,264},{16,272},{24,280},{32,288},{40,296},{48,304},{56,3... | collective-permute-start | bytes 73736 | tf_op jit(solution)/shard_map/ppermute | solution.py:112
  91.8 12.7 %collective-permute-start.3 = (f32[16,64,128]{2,1,0:T(8,128)}, f32[16,64,128]{2,1,0:T(8,128)}, u32[]{:S(2)}, u32[]{:S(2)}) collective-permute-start(f32[16,64,128]{2,1,0:T(8,128)} %bitcast.11), channel_id=1, source_target_pairs={{0,8},{8,0},{16,24},{24,16},{32,40},{40,32},{48,56},{56,48},{64,72... | collective-permute-start | bytes 1572872 | tf_op jit(solution)/shard_map/ppermute | solution.py:118
  107.7 3.4 %copy-start = (bf16[32,2,32,2048]{3,2,1,0:T(8,128)(2,1)S(1)}, bf16[32,2,32,2048]{3,2,1,0:T(8,128)(2,1)}, u32[]{:S(2)}) copy-start(bf16[32,2,32,2048]{3,2,1,0:T(8,128)(2,1)} %all-gather.3.cloned.1.call-done) | copy-start | bytes 25165828
  121.5 4.2 %copy-start.4 = (f32[64]{0:T(128)S(1)}, f32[64]{0:T(128)}, u32[]{:S(2)}) copy-start(f32[64]{0:T(128)} %param.11) | copy-start | bytes 772
  121.5 4.2 %copy-start.5 = (s32[64]{0:T(128)S(1)}, s32[64]{0:T(128)}, u32[]{:S(2)}) copy-start(s32[64]{0:T(128)} %param.10) | copy-start | bytes 772
  121.5 42.5 %all-to-all-start.1 = ((f32[8,320,256]{2,1,0:T(8,128)}), f32[8,320,256]{2,1,0:T(8,128)S(1)}, u32[]{:S(2)}, u32[]{:S(2)}) async-start(f32[8,320,256]{2,1,0:T(8,128)} %shard_map.64), calls=%async_computation.1 | async-start | bytes 5242880 | tf_op jit(solution)/shard_map/all_to_all | solution.py:132
Sparse Core Ops, SparseCore 0:
  14.8 88.1 all-gather.2

commit v5 on v4

--- a/solution.py
+++ b/solution.py
@@ -54,28 +54,33 @@
     count = lines * slots
     fold = rows // BR
 
+    taken = 2
+
     def body(loads_ref, weights_ref, ends_ref, out_ref):
-        tile = loads_ref[...].reshape(count, nodes)
+        tile = loads_ref[...].reshape(taken * count, nodes)
         sums = jnp.dot(tile, weights_ref[...], preferred_element_type=F32)
-        out_ref[0, :count] = sums[:, :rows] + sums[:, rows:]
+        sums = sums[:, :rows] + sums[:, rows:]
         end_sums = jnp.dot(tile, ends_ref[...], preferred_element_type=F32)
         end_sums = end_sums[:, :BR] + end_sums[:, BR:]
         step = count // fold
-        folded = [end_sums[i * step:(i + 1) * step] for i in range(fold)]
-        out_ref[0, count:] = jnp.concatenate(folded, axis=1)
+        for block in range(taken):
+            at = block * count
+            out_ref[block, :count] = sums[at:at + count]
+            folded = [end_sums[at + i * step:at + (i + 1) * step] for i in range(fold)]
+            out_ref[block, count:] = jnp.concatenate(folded, axis=1)
 
     height = count + count // fold
     return pl.pallas_call(
         body,
-        grid=(sides, blocks),
+        grid=(sides, blocks // taken),
         in_specs=[
-            pl.BlockSpec((1, lines, 1, slots, nodes), lambda side, block: (block, 0, side, 0, 0)),
+            pl.BlockSpec((taken, lines, 1, slots, nodes), lambda side, block: (block, 0, side, 0, 0)),
             pl.BlockSpec(weights.shape, lambda side, block: (0, 0)),
             pl.BlockSpec(ends.shape, lambda side, block: (0, 0)),
         ],
-        out_specs=pl.BlockSpec((1, height, rows), lambda side, block: (side * blocks + block, 0, 0)),
+        out_specs=pl.BlockSpec((taken, height, rows), lambda side, block: (side * (blocks // taken) + block, 0, 0)),
         out_shape=jax.ShapeDtypeStruct((sides * blocks, height, rows), F32),
-        compiler_params=pltpu.CompilerParams(vmem_limit_bytes=32 * 1024 * 1024),
+        compiler_params=pltpu.CompilerParams(vmem_limit_bytes=56 * 1024 * 1024),
     )(loads, weights, ends)
 
 
@@ -93,6 +98,8 @@
     col_select = incidence_of(col * col_count + jnp.arange(col_count, dtype=jnp.int32), from_node, to_node)
     row_select = incidence_of(row * row_count + jnp.arange(row_count, dtype=jnp.int32), from_node, to_node)
     part = nt(col_select.T, high) + nt(col_select.T, low)
+    reach_of_rows = jnp.sum(jnp.abs(sensitivity), axis=1)
+    part = jnp.concatenate([part, jnp.broadcast_to(reach_of_rows[None], (8, row_count))], axis=0)
     part, other_loads = lax.optimization_barrier((part, other_loads))
     weights = jnp.concatenate([high.T, low.T], axis=1)
 
@@ -100,7 +107,9 @@
     gathered = lax.all_gather(pair, "row", axis_index_groups=ALONG_Z_CORE, axis=0)
 
     parts = lax.all_to_all(jnp.broadcast_to(part[None], (COLS,) + part.shape), "col", 0, 0, tiled=True)
-    columns_t = jnp.sum(parts, axis=0)
+    parts = jnp.sum(parts, axis=0)
+    parts, weights = lax.optimization_barrier((parts, weights))
+    columns_t, row_bound = parts[:BR], parts[BR:]
 
     width = row_count // COLS
     piece = lax.dynamic_slice_in_dim(columns_t.T, col * width, width, 0)
@@ -108,7 +117,8 @@
     piece = lax.ppermute(piece, ("row", "col"), TO_COLUMN)
     cap_part = jnp.dot(columns_t, row_select.astype(F32), precision=HIGH, preferred_element_type=F32)
     cap_part = jnp.concatenate([cap_part[: BR // 2], cap_part[BR // 2:]], axis=1)
-    mine = jnp.concatenate([piece, cap_part], axis=0)
+    end_bound = jnp.dot(row_bound, jnp.abs(row_select.astype(F32)), precision=HIGH, preferred_element_type=F32)
+    mine = jnp.concatenate([piece, cap_part, jnp.concatenate([end_bound, end_bound], axis=1)], axis=0)
     other = lax.ppermute(mine, "row", OTHER_Y)
     h = width // 2
     both = jnp.concatenate(
@@ -117,7 +127,8 @@
     line = lax.all_gather(both, "row", axis_index_groups=ALONG_Z, axis=0)
     other_line = lax.ppermute(line, "row", OTHER_CORE)
     capacity = jnp.sum(line[:, Y * h:] + other_line[:, Y * h:], axis=0)
-    capacity = jnp.concatenate([capacity[:, :BR], capacity[:, BR:]], axis=0)
+    end_bound = capacity[BR // 2, :BR]
+    capacity = jnp.concatenate([capacity[: BR // 2, :BR], capacity[: BR // 2, BR:]], axis=0)
     ends = in_order(core, line[:, : Y * h], other_line[:, : Y * h])
     ends = ends.reshape(CORES, Z, Y, h, 2, BR).transpose(2, 1, 0, 4, 3, 5).reshape(col_count, BR)
 
@@ -129,13 +140,18 @@
         weights,
         jnp.concatenate(split(ends), axis=1),
     )
-    arrived = lax.all_to_all(packed, "col", 0, 0, tiled=True)
+    bound = jnp.concatenate([
+        jnp.broadcast_to(row_bound[:1], (count, row_count)),
+        jnp.broadcast_to(jnp.concatenate([end_bound] * fold)[None], (count // fold, row_count)),
+    ])
+    bound = jnp.maximum(bound, 1e-30) / 8192.0
+    arrived = lax.all_to_all((packed / bound).astype(jnp.float16), "col", 0, 0, tiled=True)
 
     reach = impedance * (1.0 + 3.0 * switch_flags.astype(F32))
     factor = jnp.linalg.cholesky(capacity + jnp.diag(reach))
     solved = jax.scipy.linalg.cho_solve((factor, True), columns_t)
 
-    total = jnp.sum(arrived, axis=0)
+    total = jnp.sum(arrived.astype(F32), axis=0) * bound
     end_total = total[count:].reshape(count // fold, fold, BR).transpose(1, 0, 2).reshape(count, BR)
     drop = lax.dot_general(
         solved, end_total, (((0,), (1,)), ((), ())), precision=HIGH, preferred_element_type=F32

time: 174 us -> 154 us (0.89)
  waiting for transfers between devices: 36.2 us -> 15 us
  other arithmetic: 18.5 us -> 24 us
  local copies, waits for them, and re-layouts: 7.76 us -> 5.22 us
    all_to_all x1, waiting for transfers between devices: 25.4 us -> 6.95 us  [on_device(): lax.all_to_all((packed / bound).astype(jnp.float16), 'col', 0, 0, tiled=T...]
    all_to_all x1, waiting for transfers between devices: 8.59 us -> 5.02 us  [on_device(): lax.all_to_all(jnp.broadcast_to(part[None], (COLS,) + part.shape), 'col',...]
    unnamed x15, local copies, waits for them, and re-layouts: 5.53 us -> 2.24 us
    convert_element_type x0 -> x1, other arithmetic: none -> 3.12 us  [on_device(): (packed / bound).astype(jnp.float16)]
    ppermute x1, starting transfers between devices: 9.94 us -> 7.88 us  [on_device(): other_line = lax.ppermute(line, 'row', OTHER_CORE)]
  transfers between devices with their start and end apart: 7 -> 7, of which waited for: 4 -> 5; matrix products, arithmetic and copies ran while one was open for 14% -> 17% of each run, Pallas kernels for 0% -> 0%
where the time goes in v5:
time: 154 us
  blocking collectives  41.8 us (27%)
  starting transfers between devices  39.4 us (26%)
  other arithmetic  24 us (16%)
  waiting for transfers between devices  15 us (10%)
  between operations  13.8 us (9%)
  Pallas kernels  11 us (7%)
  local copies, waits for them, and re-layouts  5.22 us (3%)
  matrix products  3.5 us (2%)
    all_gather x1, blocking collectives, on_device(): line = lax.all_gather(both, 'row', axis_index_groups=ALONG_Z, axis=0)  41.8 us
    ppermute x1, starting transfers between devices, on_device(): piece = lax.ppermute(piece, ('row', 'col'), TO_COLUMN)  12.3 us
    pallas_call x1, Pallas kernels, products(): pl.pallas_call(body, grid=(sides, blocks // taken), in_specs=[pl.BlockSpe...  11 us
    ppermute x1, starting transfers between devices, on_device(): other_line = lax.ppermute(line, 'row', OTHER_CORE)  7.88 us
    all_to_all x1, waiting for transfers between devices, on_device(): lax.all_to_all((packed / bound).astype(jnp.float16), 'col', 0, 0, tiled=T...  6.95 us
    another operation x3, other arithmetic, on_device(): factor = jnp.linalg.cholesky(capacity + jnp.diag(reach))  6.52 us
    all_to_all x1, starting transfers between devices, on_device(): lax.all_to_all(jnp.broadcast_to(part[None], (COLS,) + part.shape), 'col',...  6.36 us
    another operation x2, other arithmetic, on_device(): solved = jax.scipy.linalg.cho_solve((factor, True), columns_t)  5.55 us
  transfers between devices with their start and end apart: 7, of which 5 were waited for; matrix products, arithmetic and copies ran while one was open for 17% of the time, Pallas kernels for 0%

profile of v5, /device:TPU:1, one launch (start us, length us, event | category | flops | bytes accessed | tf_op | source)
XLA Modules:
  0.0 153.7 jit_solution(10819602158325580260)
XLA Ops:
  6.5 4.0 %collective-permute-start = (bf16[32,2048]{1,0:T(8,128)(2,1)}, bf16[32,2048]{1,0:T(8,128)(2,1)S(1)}, u32[]{:S(2)}, u32[]{:S(2)}) collective-permute-start(bf16[32,2048]{1,0:T(8,128)(2,1)} %bitcast.57), channel_id=1, source_target_pairs={{0,256},{8,264},{16,272},{24,280},{32,288},{40,296},{48,304},{56,3... | collective-permute-start | bytes 393224 | tf_op jit(solution)/shard_map/ppermute | solution.py:95
  10.6 1.9 %copy.24 = f32[256,2048]{0,1:T(8,128)S(1)} copy(f32[256,2048]{1,0:T(8,128)} %param.6) | data formatting | bytes 4194304 | tf_op args[0]
  12.6 0.6 fusion.5
  13.2 0.6 convolution_add_fusion
  14.5 0.7 maximum_select_fusion.1
  15.2 0.9 broadcast_in_dim.23
  16.1 6.4 %all-to-all-start = ((f32[8,72,256]{2,1,0:T(8,128)}), f32[8,72,256]{2,1,0:T(8,128)}, u32[]{:S(2)}, u32[]{:S(2)}) async-start(f32[8,72,256]{2,1,0:T(8,128)} %broadcast_in_dim.23), calls=%async_computation | async-start | bytes 1179648 | tf_op jit(solution)/shard_map/all_to_all | solution.py:109
  22.4 1.4 fusion.13
  23.8 2.7 %pad_maximum_fusion.weights_ref = bf16[2048,512]{1,0:T(8,128)(2,1)} fusion(bf16[2048,256]{1,0:T(8,128)(2,1)} %get-tuple-element.14, bf16[2048,256]{1,0:T(8,128)(2,1)S(1)} %get-tuple-element.13), kind=kLoop, calls=%fused_computation.5 | loop fusion | flops 4194304 | bytes 4194304 | tf_op jit(solution)/shard_map/concatenate | solution.py:104
  26.5 5.0 %all-to-all-done = f32[8,72,256]{2,1,0:T(8,128)} async-done(((f32[8,72,256]{2,1,0:T(8,128)}), f32[8,72,256]{2,1,0:T(8,128)}, u32[]{:S(2)}, u32[]{:S(2)}) %all-to-all-start) | async-done | bytes 589856 | tf_op jit(solution)/shard_map/all_to_all | solution.py:109
  31.6 1.1 reduce_sum.37
  32.9 12.3 %collective-permute-start.1 = (f32[16,128]{1,0:T(8,128)S(1)}, f32[16,128]{1,0:T(8,128)S(1)}, u32[]{:S(2)}, u32[]{:S(2)}) collective-permute-start(f32[16,128]{1,0:T(8,128)S(1)} %pad_maximum_fusion.4), channel_id=1, source_target_pairs={{0,0},{1,8},{2,16},{3,24},{4,32},{5,40},{6,48},{7,56},{8,64},{9,72... | collective-permute-start | bytes 24584 | tf_op jit(solution)/shard_map/ppermute | solution.py:117
  45.1 0.3 fusion.24
  46.0 4.0 %collective-permute-start.2 = (f32[56,128]{1,0:T(8,128)S(1)}, f32[56,128]{1,0:T(8,128)S(1)}, u32[]{:S(2)}, u32[]{:S(2)}) collective-permute-start(f32[56,128]{1,0:T(8,128)S(1)} %maximum_maximum_fusion.1), channel_id=1, source_target_pairs={{0,256},{8,264},{16,272},{24,280},{32,288},{40,296},{48,304},{56,3... | collective-permute-start | bytes 86024 | tf_op jit(solution)/shard_map/ppermute | solution.py:122
  50.0 1.6 %collective-permute-done.2 = f32[56,128]{1,0:T(8,128)S(1)} collective-permute-done((f32[56,128]{1,0:T(8,128)S(1)}, f32[56,128]{1,0:T(8,128)S(1)}, u32[]{:S(2)}, u32[]{:S(2)}) %collective-permute-start.2) | collective-permute-done | bytes 28704 | tf_op jit(solution)/shard_map/ppermute | solution.py:122
  51.8 41.8 %all-gather = f32[1152,128]{1,0:T(8,128)S(1)} all-gather(f32[72,128]{1,0:T(8,128)S(1)} %pad_maximum_fusion.3), channel_id=2, replica_groups={{0,16,32,48,64,80,96,112,128,144,160,176,192,208,224,240},{8,24,40,56,7..., dimensions={0}, use_global_device_ids=true | all-gather | bytes 626688 | tf_op jit(solution)/shard_map/all_gather | solution.py:127
  93.6 7.9 %collective-permute-start.3 = (f32[16,72,128]{2,1,0:T(8,128)S(1)}, f32[16,72,128]{2,1,0:T(8,128)S(1)}, u32[]{:S(2)}, u32[]{:S(2)}) collective-permute-start(f32[16,72,128]{2,1,0:T(8,128)S(1)} %bitcast.50), channel_id=1, source_target_pairs={{0,8},{8,0},{16,24},{24,16},{32,40},{40,32},{48,56},{56,48},{64,72... | collective-permute-start | bytes 1769480 | tf_op jit(solution)/shard_map/ppermute | solution.py:128
  101.5 0.3 stack.50
  101.9 1.2 collective-permute-done.3
  103.1 0.3 stack.51
  103.4 0.6 fusion.2
  104.4 0.3 slice-done
  105.3 1.1 pad_maximum_fusion.1.ends_ref
  106.5 11.0 %shard_map.64 = f32[8,320,256]{2,1,0:T(8,128)} custom-call(bf16[4,8,2,32,2048]{4,3,2,1,0:T(8,128)(2,1)} %bitcast.49, bf16[2048,512]{1,0:T(8,128)(2,1)} %pad_maximum_fusion.weights_ref, bf16[2048,128]{1,0:T(8,128)(2,1)} %pad_maximum_fusion.1.ends_ref), custom_call_target="tpu_custom_call" | custom-call | tf_op jit(solution)/shard_map/pallas_call | solution.py:73
  117.4 3.1 %divide_convert_fusion = f16[8,320,256]{2,1,0:T(8,128)(2,1)} fusion(f32[8,320,256]{2,1,0:T(8,128)} %shard_map.64, f32[320,256]{1,0:T(8,128)S(1)} %copy.28), kind=kLoop, calls=%fused_computation.3 | loop fusion | flops 1310720 | bytes 4259840 | tf_op jit(solution)/shard_map/convert_element_type | solution.py:148
  120.5 4.8 %all-to-all-start.1 = ((f16[8,320,256]{2,1,0:T(8,128)(2,1)}), f16[8,320,256]{2,1,0:T(8,128)(2,1)S(1)}, u32[]{:S(2)}, u32[]{:S(2)}) async-start(f16[8,320,256]{2,1,0:T(8,128)(2,1)} %divide_convert_fusion), calls=%async_computation.1 | async-start | bytes 2621440 | tf_op jit(solution)/shard_map/all_to_all | solution.py:148
  125.6 5.8 %cholesky.16 = f32[64,64]{1,0:T(8,128)S(1)} custom-call(f32[64,64]{1,0:T(8,128)S(1)} %fusion.37), custom_call_target="Cholesky" | custom-call | tf_op jit(solution)/shard_map/jit(cholesky)/cholesky | solution.py:151
  131.4 0.6 compare_reduce_fusion
  132.1 0.7 fusion.32
  132.8 4.9 %custom-call.10 = f32[1,64,64]{1,2,0:T(8,128)S(1)} custom-call(f32[1,64,64]{2,1,0:T(8,128)S(1)} %fusion.32), custom_call_target="InvertDiagBlocksLowerTriangular" | custom-call | tf_op jit(solution)/shard_map/jit(_cho_solve)/triangular_solve | solution.py:152
  138.2 6.9 %all-to-all-done.1 = f16[8,320,256]{2,1,0:T(8,128)(2,1)S(1)} async-done(((f16[8,320,256]{2,1,0:T(8,128)(2,1)}), f16[8,320,256]{2,1,0:T(8,128)(2,1)S(1)}, u32[]{:S(2)}, u32[]{:S(2)}) %all-to-all-start.1) | async-done | bytes 1310752 | tf_op jit(solution)/shard_map/all_to_all | solution.py:148
  145.8 1.1 convolution_subtract_fusion
  (61 shorter events, 3.6 us)
Async XLA Ops:
  6.5 99.9 %all-gather.3.cloned.1.call-start = ((), (), s32[]{:S(2)}) async-start(), calls=%async_computation.2 | async-start | bytes 8650752 | tf_op jit(solution)/shard_map/all_gather | solution.py:107
  6.5 7.9 %collective-permute-start = (bf16[32,2048]{1,0:T(8,128)(2,1)}, bf16[32,2048]{1,0:T(8,128)(2,1)S(1)}, u32[]{:S(2)}, u32[]{:S(2)}) collective-permute-start(bf16[32,2048]{1,0:T(8,128)(2,1)} %bitcast.57), channel_id=1, source_target_pairs={{0,256},{8,264},{16,272},{24,280},{32,288},{40,296},{48,304},{56,3... | collective-permute-start | bytes 393224 | tf_op jit(solution)/shard_map/ppermute | solution.py:95
  10.6 2.0 %copy-start.3 = (s32[64]{0:T(128)S(1)}, s32[64]{0:T(128)}, u32[]{:S(2)}) copy-start(s32[64]{0:T(128)} %param.9) | copy-start | bytes 772
  10.6 2.0 %copy-start.4 = (s32[64]{0:T(128)S(1)}, s32[64]{0:T(128)}, u32[]{:S(2)}) copy-start(s32[64]{0:T(128)} %param.8) | copy-start | bytes 772
  12.6 1.6 %copy-start = (f32[256,2048]{1,0:T(8,128)S(1)}, f32[256,2048]{1,0:T(8,128)}, u32[]{:S(2)}) copy-start(f32[256,2048]{1,0:T(8,128)} %param.6) | copy-start | bytes 6291460
  13.2 1.2 copy-start.2
  16.1 15.5 %all-to-all-start = ((f32[8,72,256]{2,1,0:T(8,128)}), f32[8,72,256]{2,1,0:T(8,128)}, u32[]{:S(2)}, u32[]{:S(2)}) async-start(f32[8,72,256]{2,1,0:T(8,128)} %broadcast_in_dim.23), calls=%async_computation | async-start | bytes 1179648 | tf_op jit(solution)/shard_map/all_to_all | solution.py:109
  26.5 74.9 %copy-start.5 = (f32[64]{0:T(128)S(1)}, f32[64]{0:T(128)}, u32[]{:S(2)}) copy-start(f32[64]{0:T(128)} %param.11) | copy-start | bytes 772
  26.5 75.0 %copy-start.6 = (s32[64]{0:T(128)S(1)}, s32[64]{0:T(128)}, u32[]{:S(2)}) copy-start(s32[64]{0:T(128)} %param.10) | copy-start | bytes 772
  32.7 70.8 %copy-start.1 = (f32[72,256]{1,0:T(8,128)}, f32[72,256]{1,0:T(8,128)S(1)}, u32[]{:S(2)}) copy-start(f32[72,256]{1,0:T(8,128)S(1)} %reduce_sum.37) | copy-start | bytes 221188
  32.9 13.0 %collective-permute-start.1 = (f32[16,128]{1,0:T(8,128)S(1)}, f32[16,128]{1,0:T(8,128)S(1)}, u32[]{:S(2)}, u32[]{:S(2)}) collective-permute-start(f32[16,128]{1,0:T(8,128)S(1)} %pad_maximum_fusion.4), channel_id=1, source_target_pairs={{0,0},{1,8},{2,16},{3,24},{4,32},{5,40},{6,48},{7,56},{8,64},{9,72... | collective-permute-start | bytes 24584 | tf_op jit(solution)/shard_map/ppermute | solution.py:117
  46.0 5.7 %collective-permute-start.2 = (f32[56,128]{1,0:T(8,128)S(1)}, f32[56,128]{1,0:T(8,128)S(1)}, u32[]{:S(2)}, u32[]{:S(2)}) collective-permute-start(f32[56,128]{1,0:T(8,128)S(1)} %maximum_maximum_fusion.1), channel_id=1, source_target_pairs={{0,256},{8,264},{16,272},{24,280},{32,288},{40,296},{48,304},{56,3... | collective-permute-start | bytes 86024 | tf_op jit(solution)/shard_map/ppermute | solution.py:122
  93.6 9.5 %collective-permute-start.3 = (f32[16,72,128]{2,1,0:T(8,128)S(1)}, f32[16,72,128]{2,1,0:T(8,128)S(1)}, u32[]{:S(2)}, u32[]{:S(2)}) collective-permute-start(f32[16,72,128]{2,1,0:T(8,128)S(1)} %bitcast.50), channel_id=1, source_target_pairs={{0,8},{8,0},{16,24},{24,16},{32,40},{40,32},{48,56},{56,48},{64,72... | collective-permute-start | bytes 1769480 | tf_op jit(solution)/shard_map/ppermute | solution.py:128
  104.1 0.7 slice-start
  120.5 24.6 %all-to-all-start.1 = ((f16[8,320,256]{2,1,0:T(8,128)(2,1)}), f16[8,320,256]{2,1,0:T(8,128)(2,1)S(1)}, u32[]{:S(2)}, u32[]{:S(2)}) async-start(f16[8,320,256]{2,1,0:T(8,128)(2,1)} %divide_convert_fusion), calls=%async_computation.1 | async-start | bytes 2621440 | tf_op jit(solution)/shard_map/all_to_all | solution.py:148
Sparse Core Ops, SparseCore 0:
  15.3 87.9 all-gather.2

commit v6 on v5

v6 whole, which is shorter than its diff:
```python
import jax
import jax.numpy as jnp
from jax import lax
from jax.experimental import pallas as pl
from jax.experimental.pallas import tpu as pltpu
from jax.sharding import PartitionSpec as P

HIGH = lax.Precision.HIGHEST
F32 = jnp.float32
BF16 = jnp.bfloat16

Y, Z, CORES = 2, 16, 2
COLS = 8
BR = 64


def row_of(y, z, core):
    return y * Z * CORES + z * CORES + core


ROWS = [(y, z, core) for y in range(Y) for z in range(Z) for core in range(CORES)]
OTHER_Y = [(row_of(y, z, k), row_of(1 - y, z, k)) for y, z, k in ROWS]
ALONG_Z_CORE = [[row_of(y, z, k) for z in range(Z) for k in range(CORES)] for y in range(Y)]
Q = 4
ACROSS_QUARTERS = [
    [row_of(y, q * Q + i, k) for q in range(Z // Q)] for y in range(Y) for i in range(Q) for k in range(CORES)
]
QUARTERS = [
    [row_of(y, q * Q + i, k) for i in range(Q)] for y in range(Y) for q in range(Z // Q) for k in range(CORES)
]
CHIP_PAIRS = [[row_of(y, z, k) for y in range(Y) for k in range(CORES)] for z in range(Z)]
TO_COLUMN = [
    ((8 * a + b) * COLS + c, (8 * b + c) * COLS + a)
    for a in range(8) for b in range(8) for c in range(8)
]


def incidence_of(node_ids, from_node, to_node):
    plus = (node_ids[:, None] == from_node[None, :]).astype(BF16)
    minus = (node_ids[:, None] == to_node[None, :]).astype(BF16)
    return plus - minus


def split(values):
    high = lax.reduce_precision(values, 8, 7)
    return high.astype(BF16), (values - high).astype(BF16)


def in_order(position, mine, other):
    return jnp.where(position == 0, jnp.stack([mine, other]), jnp.stack([other, mine]))


def nt(left, right):
    return lax.dot_general(left, right, (((1,), (1,)), ((), ())), preferred_element_type=F32)


def gather(values, groups):
    copies = jnp.broadcast_to(values[None], (len(groups[0]),) + values.shape)
    return lax.all_to_all(copies, "row", 0, 0, axis_index_groups=groups, tiled=True)


def products(loads, weights):
    blocks, lines, sides, slots, nodes = loads.shape
    rows = weights.shape[0] // 2
    count = lines * slots
    taken = 2

    def body(loads_ref, weights_ref, out_ref):
        tile = loads_ref[...].reshape(taken * count, nodes)
        sums = nt(tile, weights_ref[...])
        sums = sums[:, :rows] + sums[:, rows:]
        out_ref[...] = sums.reshape(taken, count, rows)

    return pl.pallas_call(
        body,
        grid=(sides, blocks // taken),
        in_specs=[
            pl.BlockSpec((taken, lines, 1, slots, nodes), lambda side, block: (block, 0, side, 0, 0)),
            pl.BlockSpec(weights.shape, lambda side, block: (0, 0)),
        ],
        out_specs=pl.BlockSpec((taken, count, rows), lambda side, block: (side * (blocks // taken) + block, 0, 0)),
        out_shape=jax.ShapeDtypeStruct((sides * blocks, count, rows), F32),
        compiler_params=pltpu.CompilerParams(vmem_limit_bytes=56 * 1024 * 1024),
    )(loads, weights)


def on_device(sensitivity, injections, from_node, to_node, switch_flags, impedance):
    row_count, col_count = sensitivity.shape
    row = lax.axis_index("row")
    col = lax.axis_index("col")
    y, core = row // (Z * CORES), row % CORES
    slots = injections.shape[1]

    loads = injections.T
    other_loads = lax.ppermute(loads, "row", OTHER_Y)

    high, low = split(sensitivity)
    col_select = incidence_of(col * col_count + jnp.arange(col_count, dtype=jnp.int32), from_node, to_node)
    row_select = incidence_of(row * row_count + jnp.arange(row_count, dtype=jnp.int32), from_node, to_node)
    part = nt(col_select.T, high) + nt(col_select.T, low)
    reach_of_rows = jnp.sum(jnp.abs(sensitivity), axis=1)
    part = jnp.concatenate([part, jnp.broadcast_to(reach_of_rows[None], (8, row_count))], axis=0)
    part, other_loads = lax.optimization_barrier((part, other_loads))

    pair = in_order(y, loads, other_loads)
    gathered = lax.all_gather(pair, "row", axis_index_groups=ALONG_Z_CORE, axis=0)

    parts = lax.all_to_all(jnp.broadcast_to(part[None], (COLS,) + part.shape), "col", 0, 0, tiled=True)
    parts = jnp.sum(parts, axis=0)
    columns_t, row_bound = parts[:BR], parts[BR:]

    width = row_count // COLS
    piece = lax.dynamic_slice_in_dim(columns_t.T, col * width, width, 0)
    piece = jnp.concatenate([piece[: width // 2], piece[width // 2:]], axis=1)
    piece = lax.ppermute(piece, ("row", "col"), TO_COLUMN)
    cap_part = jnp.dot(columns_t, row_select.astype(F32), precision=HIGH, preferred_element_type=F32)
    cap_part = jnp.concatenate([cap_part[: BR // 2], cap_part[BR // 2:]], axis=1)
    end_bound = jnp.dot(row_bound, jnp.abs(row_select.astype(F32)), precision=HIGH, preferred_element_type=F32)
    h = width // 2
    mine = jnp.concatenate([piece, cap_part, jnp.concatenate([end_bound, end_bound], axis=1)], axis=0)
    for groups in (ACROSS_QUARTERS, QUARTERS, CHIP_PAIRS):
        got = gather(mine, groups)
        top = mine.shape[0] - BR // 2 - 8
        mine = jnp.concatenate([got[:, :top].reshape(-1, 2 * BR), jnp.sum(got[:, top:], axis=0)], axis=0)
    top = mine.shape[0] - BR // 2 - 8
    ends = mine[:top].reshape(Y, CORES, Q, Z // Q, h, 2, BR)
    ends = ends.transpose(0, 3, 2, 1, 5, 4, 6).reshape(col_count, BR)
    capacity = jnp.concatenate([mine[top:-8, :BR], mine[top:-8, BR:]], axis=0)
    end_bound = mine[-8:, :BR]

    reach = impedance * (1.0 + 3.0 * switch_flags.astype(F32))
    factor = jnp.linalg.cholesky(capacity + jnp.diag(reach))
    solved = jax.scipy.linalg.cho_solve((factor, True), columns_t)
    bound = row_bound + jnp.dot(end_bound, jnp.abs(solved), precision=HIGH, preferred_element_type=F32)
    unit = jnp.maximum(bound[0], 1e-30) / 8192.0
    correction = lax.dot_general(
        solved, ends, (((0,), (1,)), ((), ())), precision=HIGH, preferred_element_type=F32
    )
    weights = jnp.concatenate(split((sensitivity - correction) * (1.0 / unit)[:, None]), axis=0)

    zs = Z * Y // COLS
    count = zs * CORES * slots
    packed = products(gathered.reshape(Z // zs, zs * CORES, Y, slots, col_count), weights)
    arrived = lax.all_to_all(packed.astype(jnp.float16), "col", 0, 0, tiled=True)
    total = jnp.sum(arrived.astype(F32), axis=0) * unit[None]
    return total.T


def solution(mesh):
    placed = (P("row", "col"), P("col", "row"), P(), P(), P(), P())
    return jax.shard_map(
        on_device, mesh=mesh, in_specs=placed, out_specs=P("row", "col"), check_vma=False
    )
```

time: 154 us -> 165 us (1.071)
  blocking collectives: 41.8 us -> 62.7 us
  starting transfers between devices: 39.4 us -> 31 us
  other arithmetic: 24 us -> 16.9 us
  matrix products: 3.5 us -> 6.77 us
  waiting for transfers between devices: 15 us -> 18.1 us
  Pallas kernels: 11 us -> 8.84 us
    all_to_all x0 -> x3, blocking collectives: none -> 62.7 us  [the longest x2 44.9 us: gather(): lax.all_to_all(copies, 'row', 0, 0, axis_index_groups=groups, tiled=True)]
    all_gather x1 -> x0, blocking collectives: 41.8 us -> none  [on_device(): line = lax.all_gather(both, 'row', axis_index_groups=ALONG_Z, axis=0)]
    ppermute x2 -> x0, starting transfers between devices: 11.9 us -> none  [the longest x1 7.88 us: on_device(): other_line = lax.ppermute(line, 'row', OTHER_CORE)]
    all_to_all x1, waiting for transfers between devices: 5.02 us -> 9.05 us  [on_device(): lax.all_to_all(jnp.broadcast_to(part[None], (COLS,) + part.shape), 'col',...]
    all_to_all x1, starting transfers between devices: 4.85 us -> 8.36 us  [gather(): lax.all_to_all(copies, 'row', 0, 0, axis_index_groups=groups, tiled=True)]
    ppermute x2 -> x0, waiting for transfers between devices: 2.85 us -> none  [the longest x1 1.64 us: on_device(): other = lax.ppermute(mine, 'row', OTHER_Y)]
    concatenate x4 -> x3, other arithmetic: 3.93 us -> 1.66 us  [the longest x1 1.64 us: on_device(): jnp.concatenate(split((sensitivity - correction) * (1.0 / unit)[:, None])...]
    unnamed x15 -> x14, local copies, waits for them, and re-layouts: 2.24 us -> 0.1 us
  transfers between devices with their start and end apart: 7 -> 5, of which waited for: 5 -> 3; matrix products, arithmetic and copies ran while one was open for 17% -> 16% of each run, Pallas kernels for 0% -> 0%
where the time goes in v6:
time: 165 us; the launch traced here: 164 us
  blocking collectives  62.7 us (38%)
  starting transfers between devices  31 us (19%)
  waiting for transfers between devices  18.1 us (11%)
  other arithmetic  16.9 us (10%)
  between operations  13.7 us (8%)
  Pallas kernels  8.84 us (5%)
  matrix products  6.77 us (4%)
  local copies, waits for them, and re-layouts  5.69 us (3%)
    all_to_all x2, blocking collectives, gather(): lax.all_to_all(copies, 'row', 0, 0, axis_index_groups=groups, tiled=True)  44.9 us
    all_to_all x1, blocking collectives, on_device(): lax.all_to_all(packed.astype(jnp.float16), 'col', 0, 0, tiled=True)  17.8 us
    ppermute x1, starting transfers between devices, on_device(): piece = lax.ppermute(piece, ('row', 'col'), TO_COLUMN)  12.1 us
    all_to_all x1, waiting for transfers between devices, on_device(): lax.all_to_all(jnp.broadcast_to(part[None], (COLS,) + part.shape), 'col',...  9.05 us
    pallas_call x1, Pallas kernels, products(): pl.pallas_call(body, grid=(sides, blocks // taken), in_specs=[pl.BlockSpe...  8.84 us
    all_to_all x1, waiting for transfers between devices, gather(): lax.all_to_all(copies, 'row', 0, 0, axis_index_groups=groups, tiled=True)  8.83 us
    all_to_all x1, starting transfers between devices, gather(): lax.all_to_all(copies, 'row', 0, 0, axis_index_groups=groups, tiled=True)  8.36 us
    another operation x3, other arithmetic, on_device(): factor = jnp.linalg.cholesky(capacity + jnp.diag(reach))  6.49 us
  transfers between devices with their start and end apart: 5, of which 3 were waited for; matrix products, arithmetic and copies ran while one was open for 16% of the time, Pallas kernels for 0%

profile of v6, /device:TPU:1, one launch (start us, length us, event | category | flops | bytes accessed | tf_op | source)
XLA Modules:
  0.0 163.6 jit_solution(12876152236574739254)
XLA Ops:
  6.5 4.2 %collective-permute-start = (bf16[32,2048]{1,0:T(8,128)(2,1)}, bf16[32,2048]{1,0:T(8,128)(2,1)S(1)}, u32[]{:S(2)}, u32[]{:S(2)}) collective-permute-start(bf16[32,2048]{1,0:T(8,128)(2,1)} %bitcast.32), channel_id=1, source_target_pairs={{0,256},{8,264},{16,272},{24,280},{32,288},{40,296},{48,304},{56,3... | collective-permute-start | bytes 393224 | tf_op jit(solution)/shard_map/ppermute | solution.py:95
  10.7 2.5 %fusion.4 = f32[64,256]{1,0:T(8,128)S(1)} fusion(f32[256,2048]{1,0:T(8,128)} %param.6, s32[64]{0:T(128)} %param.9, s32[64]{0:T(128)} %param.8, s32[2048]{0:T(1024)S(1)} %iota_add_fusion), kind=kOutput, calls=%fused_computation.12 | convolution fusion | flops 68812800 | bytes 2171392 | tf_op jit(solution)/shard_map/dot_general | solution.py:54
  13.3 0.9 convolution_add_fusion
  14.2 0.2 abs_reduce_fusion
  14.5 0.7 maximum_select_fusion
  15.2 0.9 broadcast_in_dim.25
  16.1 6.4 %all-to-all-start = ((f32[8,72,256]{2,1,0:T(8,128)}), f32[8,72,256]{2,1,0:T(8,128)S(1)}, u32[]{:S(2)}, u32[]{:S(2)}) async-start(f32[8,72,256]{2,1,0:T(8,128)} %broadcast_in_dim.25), calls=%async_computation | async-start | bytes 1179648 | tf_op jit(solution)/shard_map/all_to_all | solution.py:108
  22.5 9.1 %all-to-all-done = f32[8,72,256]{2,1,0:T(8,128)S(1)} async-done(((f32[8,72,256]{2,1,0:T(8,128)}), f32[8,72,256]{2,1,0:T(8,128)S(1)}, u32[]{:S(2)}, u32[]{:S(2)}) %all-to-all-start) | async-done | bytes 589856 | tf_op jit(solution)/shard_map/all_to_all | solution.py:108
  31.8 12.1 %collective-permute-start.1 = (f32[16,128]{1,0:T(8,128)S(1)}, f32[16,128]{1,0:T(8,128)S(1)}, u32[]{:S(2)}, u32[]{:S(2)}) collective-permute-start(f32[16,128]{1,0:T(8,128)S(1)} %pad_maximum_fusion.4), channel_id=1, source_target_pairs={{0,0},{1,8},{2,16},{3,24},{4,32},{5,40},{6,48},{7,56},{8,64},{9,72... | collective-permute-start | bytes 24584 | tf_op jit(solution)/shard_map/ppermute | solution.py:115
  43.9 0.3 fusion.19
  44.2 0.3 fusion.14
  44.5 0.2 collective-permute-done.1
  44.8 31.0 %all_to_all.25 = f32[4,56,128]{2,1,0:T(8,128)S(1)} all-to-all(f32[4,56,128]{2,1,0:T(8,128)S(1)} %broadcast_in_dim.26), channel_id=1, replica_groups={{0,64,128,192},{8,72,136,200},{16,80,144,208},{24,88,152,216},{32,96,16..., dimensions={0} | all-to-all | bytes 229376 | tf_op jit(solution)/shard_map/all_to_all | solution.py:59
  75.9 13.9 %all_to_all.26 = f32[4,104,128]{2,1,0:T(8,128)S(1)} all-to-all(f32[4,104,128]{2,1,0:T(8,128)S(1)} %broadcast_in_dim.27), channel_id=1, replica_groups={{0,16,32,48},{8,24,40,56},{64,80,96,112},{72,88,104,120},{128,144,160,1..., dimensions={0} | all-to-all | bytes 425984 | tf_op jit(solution)/shard_map/all_to_all | solution.py:59
  89.8 0.9 broadcast_in_dim.28
  90.7 8.4 %all-to-all-start.3 = ((f32[4,296,128]{2,1,0:T(8,128)}), f32[4,296,128]{2,1,0:T(8,128)S(1)}, u32[]{:S(2)}, u32[]{:S(2)}) async-start(f32[4,296,128]{2,1,0:T(8,128)} %broadcast_in_dim.28), calls=%async_computation.3 | async-start | bytes 1212416 | tf_op jit(solution)/shard_map/all_to_all | solution.py:59
  99.1 8.8 %all-to-all-done.3 = f32[4,296,128]{2,1,0:T(8,128)S(1)} async-done(((f32[4,296,128]{2,1,0:T(8,128)}), f32[4,296,128]{2,1,0:T(8,128)S(1)}, u32[]{:S(2)}, u32[]{:S(2)}) %all-to-all-start.3) | async-done | bytes 606240 | tf_op jit(solution)/shard_map/all_to_all | solution.py:59
  108.2 5.8 %cholesky.16 = f32[64,64]{1,0:T(8,128)S(1)} custom-call(f32[64,64]{1,0:T(8,128)S(1)} %fusion.34), custom_call_target="Cholesky" | custom-call | tf_op jit(solution)/shard_map/jit(cholesky)/cholesky | solution.py:132
  114.1 0.6 compare_reduce_fusion
  114.7 0.6 fusion.29
  115.3 4.9 %custom-call.10 = f32[1,64,64]{1,2,0:T(8,128)S(1)} custom-call(f32[1,64,64]{2,1,0:T(8,128)S(1)} %fusion.29), custom_call_target="InvertDiagBlocksLowerTriangular" | custom-call | tf_op jit(solution)/shard_map/jit(_cho_solve)/triangular_solve | solution.py:133
  120.2 0.9 slice.96
  121.1 1.6 %reshape_reshape.3 = f32[2,2,4,4,16,2,64]{6,5,4,3,2,1,0:T(2,128)S(1)} reshape(f32[4,256,128]{2,1,0:T(8,128)} %slice.96) | data formatting | bytes 1048576 | tf_op jit(solution)/shard_map/reshape;reshape | solution.py:126
  122.8 0.3 fusion.32
  123.1 0.2 fusion.30
  123.3 0.1 fusion.21
  123.5 2.3 %reduce-precision_convert_fusion = (bf16[256,2048]{1,0:T(8,128)(2,1)S(1)}, bf16[256,2048]{1,0:T(8,128)(2,1)S(1)}) fusion(f32[256]{0:T(256)S(1)} %bitcast.38, f32[256,2048]{1,0:T(8,128)S(1)} %copy-done, f32[64,256]{1,0:T(8,128)S(1)} %fusion.30, f32[2048,64]{1,0:T(8,128)S(1)} %bitcast.30), kind=kOutput, calls=%fused_computation.1 | convolution fusion | flops 405798912 | bytes 4785152 | tf_op jit(solution)/shard_map/dot_general | solution.py:136
  125.7 1.6 %pad_maximum_fusion.weights_ref = bf16[512,2048]{1,0:T(8,128)(2,1)} fusion(bf16[256,2048]{1,0:T(8,128)(2,1)S(1)} %get-tuple-element.12, bf16[256,2048]{1,0:T(8,128)(2,1)S(1)} %get-tuple-element.11), kind=kLoop, calls=%fused_computation.8 | loop fusion | flops 4194304 | bytes 4194304 | tf_op jit(solution)/shard_map/concatenate | solution.py:139
  127.4 8.8 %shard_map.64 = f32[8,256,256]{2,1,0:T(8,128)} custom-call(bf16[4,8,2,32,2048]{4,3,2,1,0:T(8,128)(2,1)} %bitcast.28, bf16[512,2048]{1,0:T(8,128)(2,1)} %pad_maximum_fusion.weights_ref), custom_call_target="tpu_custom_call" | custom-call | tf_op jit(solution)/shard_map/pallas_call | solution.py:74
  136.2 1.8 %convert_element_type.47 = f16[8,256,256]{2,1,0:T(8,128)(2,1)S(1)} convert(f32[8,256,256]{2,1,0:T(8,128)} %shard_map.64) | non-fusion elementwise | flops 524288 | bytes 3145728 | tf_op jit(solution)/shard_map/convert_element_type | solution.py:144
  138.0 17.8 %all_to_all.27 = f16[8,256,256]{2,1,0:T(8,128)(2,1)S(1)} all-to-all(f16[8,256,256]{2,1,0:T(8,128)(2,1)S(1)} %convert_element_type.47), channel_id=1, replica_groups=mesh['row'=64,'col'=8] {'col'}, dimensions={0} | all-to-all | bytes 2097152 | tf_op jit(solution)/shard_map/all_to_all | solution.py:144
  155.9 0.8 copy.21
  (48 shorter events, 1.0 us)
Async XLA Ops:
  6.5 6.7 %copy-start.2 = (s32[64]{0:T(128)S(1)}, s32[64]{0:T(128)}, u32[]{:S(2)}) copy-start(s32[64]{0:T(128)} %param.9) | copy-start | bytes 772
  6.5 6.7 %copy-start.3 = (s32[64]{0:T(128)S(1)}, s32[64]{0:T(128)}, u32[]{:S(2)}) copy-start(s32[64]{0:T(128)} %param.8) | copy-start | bytes 772
  6.5 6.7 %copy-start = (f32[256,2048]{1,0:T(8,128)S(1)}, f32[256,2048]{1,0:T(8,128)}, u32[]{:S(2)}) copy-start(f32[256,2048]{1,0:T(8,128)} %param.6) | copy-start | bytes 6291460
  6.5 120.8 %all-gather.2.cloned.1.call-start = ((), (), s32[]{:S(2)}) async-start(), calls=%async_computation.5 | async-start | bytes 8650752 | tf_op jit(solution)/shard_map/all_gather | solution.py:106
  6.5 7.9 %collective-permute-start = (bf16[32,2048]{1,0:T(8,128)(2,1)}, bf16[32,2048]{1,0:T(8,128)(2,1)S(1)}, u32[]{:S(2)}, u32[]{:S(2)}) collective-permute-start(bf16[32,2048]{1,0:T(8,128)(2,1)} %bitcast.32), channel_id=1, source_target_pairs={{0,256},{8,264},{16,272},{24,280},{32,288},{40,296},{48,304},{56,3... | collective-permute-start | bytes 393224 | tf_op jit(solution)/shard_map/ppermute | solution.py:95
  13.3 1.2 copy-start.1
  16.1 15.4 %all-to-all-start = ((f32[8,72,256]{2,1,0:T(8,128)}), f32[8,72,256]{2,1,0:T(8,128)S(1)}, u32[]{:S(2)}, u32[]{:S(2)}) async-start(f32[8,72,256]{2,1,0:T(8,128)} %broadcast_in_dim.25), calls=%async_computation | async-start | bytes 1179648 | tf_op jit(solution)/shard_map/all_to_all | solution.py:108
  31.8 12.9 %collective-permute-start.1 = (f32[16,128]{1,0:T(8,128)S(1)}, f32[16,128]{1,0:T(8,128)S(1)}, u32[]{:S(2)}, u32[]{:S(2)}) collective-permute-start(f32[16,128]{1,0:T(8,128)S(1)} %pad_maximum_fusion.4), channel_id=1, source_target_pairs={{0,0},{1,8},{2,16},{3,24},{4,32},{5,40},{6,48},{7,56},{8,64},{9,72... | collective-permute-start | bytes 24584 | tf_op jit(solution)/shard_map/ppermute | solution.py:115
  44.2 54.9 %copy-start.4 = (f32[64]{0:T(128)S(1)}, f32[64]{0:T(128)}, u32[]{:S(2)}) copy-start(f32[64]{0:T(128)} %param.11) | copy-start | bytes 772
  44.2 54.9 %copy-start.5 = (s32[64]{0:T(128)S(1)}, s32[64]{0:T(128)}, u32[]{:S(2)}) copy-start(s32[64]{0:T(128)} %param.10) | copy-start | bytes 772
  90.7 17.2 %all-to-all-start.3 = ((f32[4,296,128]{2,1,0:T(8,128)}), f32[4,296,128]{2,1,0:T(8,128)S(1)}, u32[]{:S(2)}, u32[]{:S(2)}) async-start(f32[4,296,128]{2,1,0:T(8,128)} %broadcast_in_dim.28), calls=%async_computation.3 | async-start | bytes 1212416 | tf_op jit(solution)/shard_map/all_to_all | solution.py:59
Sparse Core Ops, SparseCore 0:
  15.4 91.2 all-gather.1

commit v7 on v6

v7 whole, which is shorter than its diff:
```python
import jax
import jax.numpy as jnp
from jax import lax
from jax.experimental import pallas as pl
from jax.experimental.pallas import tpu as pltpu
from jax.sharding import PartitionSpec as P

HIGH = lax.Precision.HIGHEST
F32 = jnp.float32
BF16 = jnp.bfloat16

Y, Z, CORES = 2, 16, 2
COLS = 8
BR = 64


def row_of(y, z, core):
    return y * Z * CORES + z * CORES + core


ROWS = [(y, z, core) for y in range(Y) for z in range(Z) for core in range(CORES)]
OTHER_Y = [(row_of(y, z, k), row_of(1 - y, z, k)) for y, z, k in ROWS]
ALONG_Z_CORE = [[row_of(y, z, k) for z in range(Z) for k in range(CORES)] for y in range(Y)]
ALONG_Z = [[row_of(y, z, k) for z in range(Z)] for y in range(Y) for k in range(CORES)]
OTHER_CORE = [(row_of(y, z, k), row_of(y, z, 1 - k)) for y, z, k in ROWS]


def incidence_of(node_ids, from_node, to_node):
    plus = (node_ids[:, None] == from_node[None, :]).astype(BF16)
    minus = (node_ids[:, None] == to_node[None, :]).astype(BF16)
    return plus - minus


def split(values):
    high = lax.reduce_precision(values, 8, 7)
    return high.astype(BF16), (values - high).astype(BF16)


def in_order(position, mine, other):
    return jnp.where(position == 0, jnp.stack([mine, other]), jnp.stack([other, mine]))


def nt(left, right):
    return lax.dot_general(left, right, (((1,), (1,)), ((), ())), preferred_element_type=F32)


def products(loads, high, low):
    blocks, lines, sides, slots, nodes = loads.shape
    rows = high.shape[0]
    count = lines * slots
    taken = 2

    def body(loads_ref, high_ref, low_ref, out_ref):
        tile = loads_ref[...].reshape(taken * count, nodes)
        out_ref[...] = (nt(tile, high_ref[...]) + nt(tile, low_ref[...])).reshape(taken, count, rows)

    return pl.pallas_call(
        body,
        grid=(sides, blocks // taken),
        in_specs=[
            pl.BlockSpec((taken, lines, 1, slots, nodes), lambda side, block: (block, 0, side, 0, 0)),
            pl.BlockSpec(high.shape, lambda side, block: (0, 0)),
            pl.BlockSpec(low.shape, lambda side, block: (0, 0)),
        ],
        out_specs=pl.BlockSpec((taken, count, rows), lambda side, block: (side * (blocks // taken) + block, 0, 0)),
        out_shape=jax.ShapeDtypeStruct((sides * blocks, count, rows), F32),
        compiler_params=pltpu.CompilerParams(vmem_limit_bytes=56 * 1024 * 1024),
    )(loads, high, low)


def solve(matrix, right):
    size = matrix.shape[0]

    def body(matrix_ref, right_ref, out_ref):
        left, right = matrix_ref[...], right_ref[...]
        index = lax.broadcasted_iota(jnp.int32, (size, 1), 0)
        for k in range(size):
            inverse = 1.0 / left[k:k + 1, k:k + 1]
            left_row, right_row = left[k:k + 1] * inverse, right[k:k + 1] * inverse
            column = left[:, k:k + 1]
            here = index == k
            left = jnp.where(here, left_row, left - column * left_row)
            right = jnp.where(here, right_row, right - column * right_row)
        out_ref[...] = right

    return pl.pallas_call(body, out_shape=jax.ShapeDtypeStruct(right.shape, F32))(matrix, right)


def on_device(sensitivity, injections, from_node, to_node, switch_flags, impedance):
    row_count, col_count = sensitivity.shape
    row = lax.axis_index("row")
    col = lax.axis_index("col")
    y, core = row // (Z * CORES), row % CORES
    slots = injections.shape[1]

    loads = injections.T
    other_loads = lax.ppermute(loads, "row", OTHER_Y)

    high, low = split(sensitivity)
    col_select = incidence_of(col * col_count + jnp.arange(col_count, dtype=jnp.int32), from_node, to_node)
    row_select = incidence_of(row * row_count + jnp.arange(row_count, dtype=jnp.int32), from_node, to_node)
    part = nt(col_select.T, high) + nt(col_select.T, low)
    reach_of_rows = jnp.sum(jnp.abs(sensitivity), axis=1)
    part = jnp.concatenate([part, jnp.broadcast_to(reach_of_rows[None], (8, row_count))], axis=0)
    part, other_loads = lax.optimization_barrier((part, other_loads))

    pair = in_order(y, loads, other_loads)
    gathered = lax.all_gather(pair, "row", axis_index_groups=ALONG_Z_CORE, axis=0)

    parts = lax.all_to_all(jnp.broadcast_to(part[None], (COLS,) + part.shape), "col", 0, 0, tiled=True)
    parts = jnp.sum(parts, axis=0)
    columns_t, row_bound = parts[:BR], parts[BR:]

    half = row_count // 2
    first, second = columns_t[:, :half], columns_t[:, half:]
    cap_part = jnp.dot(columns_t, row_select.astype(F32), precision=HIGH, preferred_element_type=F32)
    cap_part = jnp.concatenate([cap_part[: BR // 2], cap_part[BR // 2:]], axis=1)
    end_bound = jnp.dot(row_bound, jnp.abs(row_select.astype(F32)), precision=HIGH, preferred_element_type=F32)
    cap_part = jnp.concatenate([cap_part, jnp.concatenate([end_bound, end_bound], axis=1)], axis=0)
    give = jnp.concatenate([jnp.where(y == 0, second, first), cap_part], axis=0)
    take = lax.ppermute(give, "row", OTHER_Y)
    blocks = COLS // Y
    block = jnp.where(col // blocks == y, jnp.where(y == 0, first, second), take[:BR])
    line = lax.all_gather(
        jnp.concatenate([block, cap_part + take[BR:]], axis=0), "row", axis_index_groups=ALONG_Z, axis=0
    )
    zs = Z // blocks
    ends = lax.dynamic_slice_in_dim(line[:, :BR], (col % blocks) * zs, zs, 0).reshape(zs * BR, half)
    mine = jnp.concatenate([ends, jnp.sum(line[:, BR:], axis=0)], axis=0)
    other = lax.ppermute(mine, "row", OTHER_CORE)
    ends = in_order(core, mine[: zs * BR], other[: zs * BR])
    other_ends = lax.ppermute(ends, "row", OTHER_Y)
    capacity = mine[zs * BR:] + other[zs * BR:]
    end_bound = capacity[BR // 2:, :BR]
    capacity = jnp.concatenate([capacity[: BR // 2, :BR], capacity[: BR // 2, BR:]], axis=0)

    reach = impedance * (1.0 + 3.0 * switch_flags.astype(F32))
    solved = solve(capacity + jnp.diag(reach), columns_t)
    bound = row_bound + jnp.dot(end_bound, jnp.abs(solved), precision=HIGH, preferred_element_type=F32)
    unit = jnp.maximum(bound[0], 1e-30) / 8192.0
    ends = in_order(y, ends, other_ends).reshape(Y, CORES, zs, BR, half)
    ends = ends.transpose(3, 2, 1, 0, 4).reshape(BR, col_count)
    correction = lax.dot_general(
        solved, ends, (((0,), (0,)), ((), ())), precision=HIGH, preferred_element_type=F32
    )
    after_high, after_low = split((sensitivity - correction) * (1.0 / unit)[:, None])

    packed = products(gathered.reshape(blocks, zs * CORES, Y, slots, col_count), after_high, after_low)
    arrived = lax.all_to_all(packed.astype(jnp.float16), "col", 0, 0, tiled=True)
    total = jnp.sum(arrived.astype(F32), axis=0) * unit[None]
    return total.T


def solution(mesh):
    placed = (P("row", "col"), P("col", "row"), P(), P(), P(), P())
    return jax.shard_map(
        on_device, mesh=mesh, in_specs=placed, out_specs=P("row", "col"), check_vma=False
    )
```

time: 165 us -> 147 us (0.89)
  other arithmetic: 16.9 us -> 5.03 us
  starting transfers between devices: 31 us -> 24 us
  Pallas kernels: 8.84 us -> 15.7 us
  waiting for transfers between devices: 18.1 us -> 12 us
  local copies, waits for them, and re-layouts: 5.69 us -> 3.47 us
    all_gather x0 -> x1, blocking collectives: none -> 45 us  [on_device(): lax.all_gather(jnp.concatenate([block, cap_part + take[BR:]], axis=0), 'r...]
    all_to_all x2 -> x0, blocking collectives: 44.9 us -> none  [gather(): lax.all_to_all(copies, 'row', 0, 0, axis_index_groups=groups, tiled=True)]
    another operation x5 -> x0, other arithmetic: 12 us -> none  [the longest x3 6.49 us: on_device(): factor = jnp.linalg.cholesky(capacity + jnp.diag(reach))]
    all_to_all x1 -> x0, waiting for transfers between devices: 8.83 us -> none  [gather(): lax.all_to_all(copies, 'row', 0, 0, axis_index_groups=groups, tiled=True)]
    all_to_all x1 -> x0, starting transfers between devices: 8.36 us -> none  [gather(): lax.all_to_all(copies, 'row', 0, 0, axis_index_groups=groups, tiled=True)]
    pallas_call x0 -> x1, Pallas kernels: none -> 6.9 us  [solve(): pl.pallas_call(body, out_shape=jax.ShapeDtypeStruct(right.shape, F32))]
    ppermute x1 -> x3, waiting for transfers between devices: 0.21 us -> 2.96 us  [the longest x1 2.73 us: on_device(): take = lax.ppermute(give, 'row', OTHER_Y)]
    concatenate x5 -> x3, other arithmetic: 1.82 us -> 0.1 us  [the longest x1 0.08 us: on_device(): give = jnp.concatenate([jnp.where(y == 0, second, first), cap_part], axis=0)]
  transfers between devices with their start and end apart: 5 -> 6, of which waited for: 3 -> 3; matrix products, arithmetic and copies ran while one was open for 16% -> 9% of each run, Pallas kernels for 0% -> 5%
where the time goes in v7:
time: 147 us
  blocking collectives  64.3 us (44%)
  starting transfers between devices  24 us (16%)
  Pallas kernels  15.7 us (11%)
  between operations  13.8 us (9%)
  waiting for transfers between devices  12 us (8%)
  matrix products  8.4 us (6%)
  other arithmetic  5.03 us (3%)
  local copies, waits for them, and re-layouts  3.47 us (2%)
    all_gather x1, blocking collectives, on_device(): lax.all_gather(jnp.concatenate([block, cap_part + take[BR:]], axis=0), 'r...  45 us
    all_to_all x1, blocking collectives, on_device(): lax.all_to_all(packed.astype(jnp.float16), 'col', 0, 0, tiled=True)  19.3 us
    ppermute x1, starting transfers between devices, on_device(): other = lax.ppermute(mine, 'row', OTHER_CORE)  9.47 us
    all_to_all x1, waiting for transfers between devices, on_device(): lax.all_to_all(jnp.broadcast_to(part[None], (COLS,) + part.shape), 'col',...  9.03 us
    pallas_call x1, Pallas kernels, products(): pl.pallas_call(body, grid=(sides, blocks // taken), in_specs=[pl.BlockSpe...  8.78 us
    pallas_call x1, Pallas kernels, solve(): pl.pallas_call(body, out_shape=jax.ShapeDtypeStruct(right.shape, F32))  6.9 us
    all_to_all x1, starting transfers between devices, on_device(): lax.all_to_all(jnp.broadcast_to(part[None], (COLS,) + part.shape), 'col',...  6.35 us
    ppermute x1, starting transfers between devices, on_device(): other_loads = lax.ppermute(loads, 'row', OTHER_Y)  4.16 us
  transfers between devices with their start and end apart: 6, of which 3 were waited for; matrix products, arithmetic and copies ran while one was open for 9% of the time, Pallas kernels for 5%

profile of v7, /device:TPU:1, one launch (start us, length us, event | category | flops | bytes accessed | tf_op | source)
XLA Modules:
  0.0 146.7 jit_solution(15289753725614125854)
XLA Ops:
  6.5 4.2 %collective-permute-start = (bf16[32,2048]{1,0:T(8,128)(2,1)}, bf16[32,2048]{1,0:T(8,128)(2,1)S(1)}, u32[]{:S(2)}, u32[]{:S(2)}) collective-permute-start(bf16[32,2048]{1,0:T(8,128)(2,1)} %bitcast.29), channel_id=1, source_target_pairs={{0,256},{8,264},{16,272},{24,280},{32,288},{40,296},{48,304},{56,3... | collective-permute-start | bytes 393224 | tf_op jit(solution)/shard_map/ppermute | solution.py:97
  10.7 2.5 %fusion.4 = f32[64,256]{1,0:T(8,128)S(1)} fusion(f32[256,2048]{1,0:T(8,128)} %param.6, s32[64]{0:T(128)} %param.9, s32[64]{0:T(128)} %param.8, s32[2048]{0:T(1024)S(1)} %iota_add_fusion), kind=kOutput, calls=%fused_computation.11 | convolution fusion | flops 68812800 | bytes 2171392 | tf_op jit(solution)/shard_map/dot_general | solution.py:44
  13.3 0.9 convolution_add_fusion
  14.2 0.2 abs_reduce_fusion
  14.5 0.7 maximum_select_fusion.1
  15.2 0.9 broadcast_in_dim.18
  16.1 6.4 %all-to-all-start = ((f32[8,72,256]{2,1,0:T(8,128)}), f32[8,72,256]{2,1,0:T(8,128)S(1)}, u32[]{:S(2)}, u32[]{:S(2)}) async-start(f32[8,72,256]{2,1,0:T(8,128)} %broadcast_in_dim.18), calls=%async_computation | async-start | bytes 1179648 | tf_op jit(solution)/shard_map/all_to_all | solution.py:110
  22.5 9.0 %all-to-all-done = f32[8,72,256]{2,1,0:T(8,128)S(1)} async-done(((f32[8,72,256]{2,1,0:T(8,128)}), f32[8,72,256]{2,1,0:T(8,128)S(1)}, u32[]{:S(2)}, u32[]{:S(2)}) %all-to-all-start) | async-done | bytes 589856 | tf_op jit(solution)/shard_map/all_to_all | solution.py:110
  31.6 0.3 fusion.15
  31.9 0.3 fusion.20
  32.2 2.1 %collective-permute-start.1 = (f32[104,128]{1,0:T(8,128)S(1)}, f32[104,128]{1,0:T(8,128)S(1)}, u32[]{:S(2)}, u32[]{:S(2)}) collective-permute-start(f32[104,128]{1,0:T(8,128)S(1)} %maximum_maximum_fusion), channel_id=1, source_target_pairs={{0,256},{8,264},{16,272},{24,280},{32,288},{40,296},{48,304},{56,3... | collective-permute-start | bytes 159752 | tf_op jit(solution)/shard_map/ppermute | solution.py:121
  34.4 2.7 %collective-permute-done.1 = f32[104,128]{1,0:T(8,128)S(1)} collective-permute-done((f32[104,128]{1,0:T(8,128)S(1)}, f32[104,128]{1,0:T(8,128)S(1)}, u32[]{:S(2)}, u32[]{:S(2)}) %collective-permute-start.1) | collective-permute-done | bytes 53280 | tf_op jit(solution)/shard_map/ppermute | solution.py:121
  37.2 45.0 %all-gather = f32[1664,128]{1,0:T(8,128)S(1)} all-gather(f32[104,128]{1,0:T(8,128)S(1)} %pad_maximum_fusion.2), channel_id=2, replica_groups={{0,16,32,48,64,80,96,112,128,144,160,176,192,208,224,240},{8,24,40,56,7..., dimensions={0}, use_global_device_ids=true | all-gather | bytes 905216 | tf_op jit(solution)/shard_map/all_gather | solution.py:124
  82.3 9.5 %collective-permute-start.2 = (f32[296,128]{1,0:T(8,128)S(1)}, f32[296,128]{1,0:T(8,128)S(1)}, u32[]{:S(2)}, u32[]{:S(2)}) collective-permute-start(f32[296,128]{1,0:T(8,128)S(1)} %pad_maximum_fusion), channel_id=1, source_target_pairs={{0,8},{8,0},{16,24},{24,16},{32,40},{40,32},{48,56},{56,48},{64,72... | collective-permute-start | bytes 454664 | tf_op jit(solution)/shard_map/ppermute | solution.py:130
  91.8 0.6 slice.68.right_ref
  92.5 0.1 copy.18
  92.6 0.2 collective-permute-done.2
  92.8 0.1 copy.19
  93.0 1.9 %collective-permute-start.3 = (f32[2,256,128]{2,1,0:T(8,128)S(1)}, f32[2,256,128]{2,1,0:T(8,128)S(1)}, u32[]{:S(2)}, u32[]{:S(2)}) collective-permute-start(f32[2,256,128]{2,1,0:T(8,128)S(1)} %maximum_select_fusion.2), channel_id=1, source_target_pairs={{0,256},{8,264},{16,272},{24,280},{32,288},{40,296},{48,304},{56,3... | collective-permute-start | bytes 786440 | tf_op jit(solution)/shard_map/ppermute | solution.py:132
  95.0 0.7 maximum_add_fusion.matrix_ref
  95.7 6.9 %shard_map.64 = f32[64,256]{1,0:T(8,128)} custom-call(f32[64,64]{1,0:T(8,128)} %maximum_add_fusion.matrix_ref, f32[64,256]{1,0:T(8,128)} %slice.68.right_ref), custom_call_target="tpu_custom_call" | custom-call | tf_op jit(solution)/shard_map/pallas_call | solution.py:86
  102.6 1.1 fusion.22
  103.6 0.4 broadcast_select_fusion
  104.1 0.3 copy.21
  104.4 0.7 fusion.8
  105.1 0.4 reshape.170
  105.6 3.4 %fusion.2 = (bf16[256,2048]{1,0:T(8,128)(2,1)}, bf16[256,2048]{1,0:T(8,128)(2,1)}) fusion(f32[256]{0:T(256)S(1)} %bitcast.33, f32[256,2048]{1,0:T(8,128)S(1)} %copy-done, f32[64,256]{1,0:T(8,128)S(1)} %copy-done.2, f32[64,2048]{1,0:T(8,128)S(1)} %reshape.170), kind=kOutput, calls=%fused_computation.7 | convolution fusion | flops 405798912 | bytes 4785152 | tf_op jit(solution)/shard_map/dot_general | solution.py:143
  109.0 8.8 %shard_map.65 = f32[8,256,256]{2,1,0:T(8,128)} custom-call(bf16[4,8,2,32,2048]{4,3,2,1,0:T(8,128)(2,1)} %bitcast.21, bf16[256,2048]{1,0:T(8,128)(2,1)} %get-tuple-element.12.high_ref, bf16[256,2048]{1,0:T(8,128)(2,1)} %get-tuple-element.11.low_ref), custom_call_target="tpu_custom_call" | custom-call | tf_op jit(solution)/shard_map/pallas_call | solution.py:57
  117.8 1.8 %convert_element_type.47 = f16[8,256,256]{2,1,0:T(8,128)(2,1)S(1)} convert(f32[8,256,256]{2,1,0:T(8,128)} %shard_map.65) | non-fusion elementwise | flops 524288 | bytes 3145728 | tf_op jit(solution)/shard_map/convert_element_type | solution.py:149
  119.6 19.3 %all_to_all.10 = f16[8,256,256]{2,1,0:T(8,128)(2,1)S(1)} all-to-all(f16[8,256,256]{2,1,0:T(8,128)(2,1)S(1)} %convert_element_type.47), channel_id=1, replica_groups=mesh['row'=64,'col'=8] {'col'}, dimensions={0} | all-to-all | bytes 2097152 | tf_op jit(solution)/shard_map/all_to_all | solution.py:149
  138.8 0.1 convert_reduce_fusion
  139.0 0.8 copy.23
  (45 shorter events, 0.6 us)
Async XLA Ops:
  6.5 6.7 %copy-start.4 = (s32[64]{0:T(128)S(1)}, s32[64]{0:T(128)}, u32[]{:S(2)}) copy-start(s32[64]{0:T(128)} %param.9) | copy-start | bytes 772
  6.5 6.7 %copy-start.5 = (s32[64]{0:T(128)S(1)}, s32[64]{0:T(128)}, u32[]{:S(2)}) copy-start(s32[64]{0:T(128)} %param.8) | copy-start | bytes 772
  6.5 6.7 %copy-start = (f32[256,2048]{1,0:T(8,128)S(1)}, f32[256,2048]{1,0:T(8,128)}, u32[]{:S(2)}) copy-start(f32[256,2048]{1,0:T(8,128)} %param.6) | copy-start | bytes 6291460
  6.5 102.5 %all-gather.3.cloned.1.call-start = ((), (), s32[]{:S(2)}) async-start(), calls=%async_computation.2 | async-start | bytes 8650752 | tf_op jit(solution)/shard_map/all_gather | solution.py:108
  6.5 7.9 %collective-permute-start = (bf16[32,2048]{1,0:T(8,128)(2,1)}, bf16[32,2048]{1,0:T(8,128)(2,1)S(1)}, u32[]{:S(2)}, u32[]{:S(2)}) collective-permute-start(bf16[32,2048]{1,0:T(8,128)(2,1)} %bitcast.29), channel_id=1, source_target_pairs={{0,256},{8,264},{16,272},{24,280},{32,288},{40,296},{48,304},{56,3... | collective-permute-start | bytes 393224 | tf_op jit(solution)/shard_map/ppermute | solution.py:97
  13.3 1.2 copy-start.3
  16.1 15.4 %all-to-all-start = ((f32[8,72,256]{2,1,0:T(8,128)}), f32[8,72,256]{2,1,0:T(8,128)S(1)}, u32[]{:S(2)}, u32[]{:S(2)}) async-start(f32[8,72,256]{2,1,0:T(8,128)} %broadcast_in_dim.18), calls=%async_computation | async-start | bytes 1179648 | tf_op jit(solution)/shard_map/all_to_all | solution.py:110
  22.5 69.3 %copy-start.6 = (f32[64]{0:T(128)S(1)}, f32[64]{0:T(128)}, u32[]{:S(2)}) copy-start(f32[64]{0:T(128)} %param.11) | copy-start | bytes 772
  22.5 69.3 %copy-start.7 = (s32[64]{0:T(128)S(1)}, s32[64]{0:T(128)}, u32[]{:S(2)}) copy-start(s32[64]{0:T(128)} %param.10) | copy-start | bytes 772
  31.6 61.0 %copy-start.1 = (f32[72,256]{1,0:T(8,128)}, f32[72,256]{1,0:T(8,128)S(1)}, u32[]{:S(2)}) copy-start(f32[72,256]{1,0:T(8,128)S(1)} %reduce_sum.37) | copy-start | bytes 221188
  32.2 4.9 %collective-permute-start.1 = (f32[104,128]{1,0:T(8,128)S(1)}, f32[104,128]{1,0:T(8,128)S(1)}, u32[]{:S(2)}, u32[]{:S(2)}) collective-permute-start(f32[104,128]{1,0:T(8,128)S(1)} %maximum_maximum_fusion), channel_id=1, source_target_pairs={{0,256},{8,264},{16,272},{24,280},{32,288},{40,296},{48,304},{56,3... | collective-permute-start | bytes 159752 | tf_op jit(solution)/shard_map/ppermute | solution.py:121
  82.3 10.5 %collective-permute-start.2 = (f32[296,128]{1,0:T(8,128)S(1)}, f32[296,128]{1,0:T(8,128)S(1)}, u32[]{:S(2)}, u32[]{:S(2)}) collective-permute-start(f32[296,128]{1,0:T(8,128)S(1)} %pad_maximum_fusion), channel_id=1, source_target_pairs={{0,8},{8,0},{16,24},{24,16},{32,40},{40,32},{48,56},{56,48},{64,72... | collective-permute-start | bytes 454664 | tf_op jit(solution)/shard_map/ppermute | solution.py:130
  92.8 11.3 %slice-start = ((f32[72,256]{1,0:T(8,128)}), f32[8,256]{1,0:T(8,128)S(1)}, s32[]{:S(2)}) async-start(f32[72,256]{1,0:T(8,128)} %copy-done.1), calls=%async_computation.3 | async-start | bytes 16384 | tf_op jit(solution)/shard_map/slice | solution.py:112
  93.0 11.1 %collective-permute-start.3 = (f32[2,256,128]{2,1,0:T(8,128)S(1)}, f32[2,256,128]{2,1,0:T(8,128)S(1)}, u32[]{:S(2)}, u32[]{:S(2)}) collective-permute-start(f32[2,256,128]{2,1,0:T(8,128)S(1)} %maximum_select_fusion.2), channel_id=1, source_target_pairs={{0,256},{8,264},{16,272},{24,280},{32,288},{40,296},{48,304},{56,3... | collective-permute-start | bytes 786440 | tf_op jit(solution)/shard_map/ppermute | solution.py:132
  102.6 3.0 %copy-start.2 = (f32[64,256]{1,0:T(8,128)S(1)}, f32[64,256]{1,0:T(8,128)}, u32[]{:S(2)}) copy-start(f32[64,256]{1,0:T(8,128)} %shard_map.64) | copy-start | bytes 196612
Sparse Core Ops, SparseCore 0:
  15.4 88.9 all-gather.2

commit v8 on v7

--- a/solution.py
+++ b/solution.py
@@ -48,7 +48,7 @@
     blocks, lines, sides, slots, nodes = loads.shape
     rows = high.shape[0]
     count = lines * slots
-    taken = 2
+    taken = 4
 
     def body(loads_ref, high_ref, low_ref, out_ref):
         tile = loads_ref[...].reshape(taken * count, nodes)
@@ -64,26 +64,49 @@
         ],
         out_specs=pl.BlockSpec((taken, count, rows), lambda side, block: (side * (blocks // taken) + block, 0, 0)),
         out_shape=jax.ShapeDtypeStruct((sides * blocks, count, rows), F32),
-        compiler_params=pltpu.CompilerParams(vmem_limit_bytes=56 * 1024 * 1024),
+        compiler_params=pltpu.CompilerParams(vmem_limit_bytes=48 * 1024 * 1024),
     )(loads, high, low)
 
 
-def solve(matrix, right):
-    size = matrix.shape[0]
+def solve(mine, other, reach, parts):
+    size, width = BR, parts.shape[1]
+    tail = mine.shape[0] - size // 2 - 8
+    lanes = 128
+    height = size // 2
 
-    def body(matrix_ref, right_ref, out_ref):
-        left, right = matrix_ref[...], right_ref[...]
-        index = lax.broadcasted_iota(jnp.int32, (size, 1), 0)
-        for k in range(size):
-            inverse = 1.0 / left[k:k + 1, k:k + 1]
-            left_row, right_row = left[k:k + 1] * inverse, right[k:k + 1] * inverse
-            column = left[:, k:k + 1]
-            here = index == k
-            left = jnp.where(here, left_row, left - column * left_row)
-            right = jnp.where(here, right_row, right - column * right_row)
-        out_ref[...] = right
+    def body(mine_ref, other_ref, reach_ref, parts_ref, out_ref, bound_ref):
+        sums = mine_ref[tail:] + other_ref[tail:]
+        left = jnp.concatenate([sums[:height, :size], sums[:height, size:]], axis=0)
+        left = jnp.concatenate([left, jnp.zeros((size, lanes - size), F32)], axis=1)
+        rows = lax.broadcasted_iota(jnp.int32, (size, lanes), 0)
+        diagonal = rows == lax.broadcasted_iota(jnp.int32, (size, lanes), 1)
+        left = left + jnp.where(diagonal, reach_ref[...], 0.0)
+        end_bound = jnp.sum(jnp.where(diagonal, sums[height:height + 1], 0.0), axis=1, keepdims=True)
+        parts = [left] + [parts_ref[:size, at:at + lanes] for at in range(0, width, lanes)]
+        own, other = jnp.zeros((size, lanes), F32), jnp.zeros((size, lanes), F32)
+        for k in range(0, size, 2):
+            first = jnp.broadcast_to(parts[0][:, k:k + 1], (size, lanes))
+            second = jnp.broadcast_to(parts[0][:, k + 1:k + 2], (size, lanes))
+            a, b, c, d = first[k:k + 1], second[k:k + 1], first[k + 1:k + 2], second[k + 1:k + 2]
+            inverse = 1.0 / (a * d - b * c)
+            upper, lower = rows == k, rows == k + 1
+            pivots = upper | lower
+            up = jnp.where(pivots, 0.0, (first * d - second * c) * inverse)
+            down = jnp.where(pivots, 0.0, (second * a - first * b) * inverse)
+            own = jnp.where(upper, d * inverse, jnp.where(lower, a * inverse, own))
+            other = jnp.where(upper, -b * inverse, jnp.where(lower, -c * inverse, other))
+            parts = [values - up * values[k:k + 1] - down * values[k + 1:k + 2] for values in parts]
+        even = rows % 2 == 0
+        for at, values in enumerate(parts[1:]):
+            following = jnp.concatenate([values[1:], values[:1]], axis=0)
+            previous = jnp.concatenate([values[-1:], values[:-1]], axis=0)
+            solved = own * values + other * jnp.where(even, following, previous)
+            here = slice(at * lanes, (at + 1) * lanes)
+            out_ref[:, here] = solved
+            bound_ref[:, here] = parts_ref[size:, here] + jnp.sum(jnp.abs(solved) * end_bound, axis=0, keepdims=True)
 
-    return pl.pallas_call(body, out_shape=jax.ShapeDtypeStruct(right.shape, F32))(matrix, right)
+    out_shape = (jax.ShapeDtypeStruct((size, width), F32), jax.ShapeDtypeStruct((8, width), F32))
+    return pl.pallas_call(body, out_shape=out_shape)(mine, other, reach, parts)
 
 
 def on_device(sensitivity, injections, from_node, to_node, switch_flags, impedance):
@@ -102,12 +125,13 @@
     part = nt(col_select.T, high) + nt(col_select.T, low)
     reach_of_rows = jnp.sum(jnp.abs(sensitivity), axis=1)
     part = jnp.concatenate([part, jnp.broadcast_to(reach_of_rows[None], (8, row_count))], axis=0)
-    part, other_loads = lax.optimization_barrier((part, other_loads))
+    copies = jnp.broadcast_to(part[None], (COLS,) + part.shape)
+    copies, other_loads = lax.optimization_barrier((copies, other_loads))
 
     pair = in_order(y, loads, other_loads)
     gathered = lax.all_gather(pair, "row", axis_index_groups=ALONG_Z_CORE, axis=0)
 
-    parts = lax.all_to_all(jnp.broadcast_to(part[None], (COLS,) + part.shape), "col", 0, 0, tiled=True)
+    parts = lax.all_to_all(copies, "col", 0, 0, tiled=True)
     parts = jnp.sum(parts, axis=0)
     columns_t, row_bound = parts[:BR], parts[BR:]
 
@@ -129,24 +153,25 @@
     mine = jnp.concatenate([ends, jnp.sum(line[:, BR:], axis=0)], axis=0)
     other = lax.ppermute(mine, "row", OTHER_CORE)
     ends = in_order(core, mine[: zs * BR], other[: zs * BR])
-    other_ends = lax.ppermute(ends, "row", OTHER_Y)
-    capacity = mine[zs * BR:] + other[zs * BR:]
-    end_bound = capacity[BR // 2:, :BR]
-    capacity = jnp.concatenate([capacity[: BR // 2, :BR], capacity[: BR // 2, BR:]], axis=0)
+    end_bound = mine[-8, :BR] + other[-8, :BR]
+    end_unit = (jnp.maximum(end_bound, 1e-30) / 8192.0)[:, None]
+    ends = ends.reshape(CORES, zs, BR, half)
+    other_ends = lax.ppermute((ends * (1.0 / end_unit)).astype(jnp.float16), "row", OTHER_Y)
 
     reach = impedance * (1.0 + 3.0 * switch_flags.astype(F32))
-    solved = solve(capacity + jnp.diag(reach), columns_t)
-    bound = row_bound + jnp.dot(end_bound, jnp.abs(solved), precision=HIGH, preferred_element_type=F32)
-    unit = jnp.maximum(bound[0], 1e-30) / 8192.0
-    ends = in_order(y, ends, other_ends).reshape(Y, CORES, zs, BR, half)
+    reach = jnp.concatenate([reach, jnp.zeros_like(reach)])[None]
+    solved, bound = solve(mine, other, reach, parts)
+    ends = in_order(y, ends, other_ends.astype(F32) * end_unit)
     ends = ends.transpose(3, 2, 1, 0, 4).reshape(BR, col_count)
     correction = lax.dot_general(
         solved, ends, (((0,), (0,)), ((), ())), precision=HIGH, preferred_element_type=F32
     )
-    after_high, after_low = split((sensitivity - correction) * (1.0 / unit)[:, None])
+    after_high, after_low = split(sensitivity - correction)
 
     packed = products(gathered.reshape(blocks, zs * CORES, Y, slots, col_count), after_high, after_low)
-    arrived = lax.all_to_all(packed.astype(jnp.float16), "col", 0, 0, tiled=True)
+
+    unit = jnp.maximum(bound[0], 1e-30) / 8192.0
+    arrived = lax.all_to_all((packed * (1.0 / unit)).astype(jnp.float16), "col", 0, 0, tiled=True)
     total = jnp.sum(arrived.astype(F32), axis=0) * unit[None]
     return total.T
 

time: 147 us -> 143 us (0.973)
  Pallas kernels: 15.7 us -> 12.9 us
    pallas_call x1, Pallas kernels: 8.78 us -> 6.97 us  [products(): pl.pallas_call(body, grid=(sides, blocks // taken), in_specs=[pl.BlockSpe...]
  transfers between devices with their start and end apart: 6 -> 6, of which waited for: 3 -> 3; matrix products, arithmetic and copies ran while one was open for 9% -> 8% of each run, Pallas kernels for 5% -> 4%
where the time goes in v8:
time: 143 us; the launch traced here: 142 us
  blocking collectives  63 us (44%)
  starting transfers between devices  25.3 us (18%)
  between operations  13.8 us (10%)
  Pallas kernels  12.9 us (9%)
  waiting for transfers between devices  12.1 us (8%)
  matrix products  7.5 us (5%)
  other arithmetic  4.19 us (3%)
  local copies, waits for them, and re-layouts  3.21 us (2%)
    all_gather x1, blocking collectives, on_device(): lax.all_gather(jnp.concatenate([block, cap_part + take[BR:]], axis=0), 'r...  43.7 us
    all_to_all x1, blocking collectives, on_device(): lax.all_to_all((packed * (1.0 / unit)).astype(jnp.float16), 'col', 0, 0,...  19.3 us
    ppermute x1, starting transfers between devices, on_device(): other = lax.ppermute(mine, 'row', OTHER_CORE)  9.99 us
    all_to_all x1, waiting for transfers between devices, on_device(): parts = lax.all_to_all(copies, 'col', 0, 0, tiled=True)  9.03 us
    pallas_call x1, Pallas kernels, products(): pl.pallas_call(body, grid=(sides, blocks // taken), in_specs=[pl.BlockSpe...  6.97 us
    all_to_all x1, starting transfers between devices, on_device(): parts = lax.all_to_all(copies, 'col', 0, 0, tiled=True)  6.37 us
    pallas_call x1, Pallas kernels, solve(): return pl.pallas_call(body, out_shape=out_shape)(mine, other, reach, parts)  5.92 us
    ppermute x1, starting transfers between devices, on_device(): other_loads = lax.ppermute(loads, 'row', OTHER_Y)  4.16 us
  transfers between devices with their start and end apart: 6, of which 3 were waited for; matrix products, arithmetic and copies ran while one was open for 8% of the time, Pallas kernels for 4%

profile of v8, /device:TPU:1, one launch (start us, length us, event | category | flops | bytes accessed | tf_op | source)
XLA Modules:
  0.0 142.0 jit_solution(338170003753509003)
XLA Ops:
  6.5 4.2 %collective-permute-start = (bf16[32,2048]{1,0:T(8,128)(2,1)}, bf16[32,2048]{1,0:T(8,128)(2,1)S(1)}, u32[]{:S(2)}, u32[]{:S(2)}) collective-permute-start(bf16[32,2048]{1,0:T(8,128)(2,1)} %bitcast.34), channel_id=1, source_target_pairs={{0,256},{8,264},{16,272},{24,280},{32,288},{40,296},{48,304},{56,3... | collective-permute-start | bytes 393224 | tf_op jit(solution)/shard_map/ppermute | solution.py:120
  10.7 2.5 %fusion.3 = f32[64,256]{1,0:T(8,128)S(1)} fusion(f32[256,2048]{1,0:T(8,128)} %param.6, s32[64]{0:T(128)} %param.9, s32[64]{0:T(128)} %param.8, s32[2048]{0:T(1024)S(1)} %iota_add_fusion), kind=kOutput, calls=%fused_computation.11 | convolution fusion | flops 68812800 | bytes 2171392 | tf_op jit(solution)/shard_map/dot_general | solution.py:44
  13.3 0.9 convolution_add_fusion
  14.2 0.2 abs_reduce_fusion
  14.5 0.9 broadcast_in_dim.7
  15.4 0.7 maximum_select_fusion.1
  16.1 6.4 %all-to-all-start = ((f32[8,72,256]{2,1,0:T(8,128)}), f32[8,72,256]{2,1,0:T(8,128)S(1)}, u32[]{:S(2)}, u32[]{:S(2)}) async-start(f32[8,72,256]{2,1,0:T(8,128)} %broadcast_in_dim.7), calls=%async_computation | async-start | bytes 1179648 | tf_op jit(solution)/shard_map/all_to_all | solution.py:134
  22.5 9.0 %all-to-all-done = f32[8,72,256]{2,1,0:T(8,128)S(1)} async-done(((f32[8,72,256]{2,1,0:T(8,128)}), f32[8,72,256]{2,1,0:T(8,128)S(1)}, u32[]{:S(2)}, u32[]{:S(2)}) %all-to-all-start) | async-done | bytes 589856 | tf_op jit(solution)/shard_map/all_to_all | solution.py:134
  31.6 0.3 fusion.16
  31.9 0.3 fusion.21
  32.2 2.1 %collective-permute-start.1 = (f32[104,128]{1,0:T(8,128)S(1)}, f32[104,128]{1,0:T(8,128)S(1)}, u32[]{:S(2)}, u32[]{:S(2)}) collective-permute-start(f32[104,128]{1,0:T(8,128)S(1)} %maximum_maximum_fusion), channel_id=1, source_target_pairs={{0,256},{8,264},{16,272},{24,280},{32,288},{40,296},{48,304},{56,3... | collective-permute-start | bytes 159752 | tf_op jit(solution)/shard_map/ppermute | solution.py:145
  34.4 2.7 %collective-permute-done.1 = f32[104,128]{1,0:T(8,128)S(1)} collective-permute-done((f32[104,128]{1,0:T(8,128)S(1)}, f32[104,128]{1,0:T(8,128)S(1)}, u32[]{:S(2)}, u32[]{:S(2)}) %collective-permute-start.1) | collective-permute-done | bytes 53280 | tf_op jit(solution)/shard_map/ppermute | solution.py:145
  37.2 43.7 %all-gather = f32[1664,128]{1,0:T(8,128)S(1)} all-gather(f32[104,128]{1,0:T(8,128)S(1)} %pad_maximum_fusion.2), channel_id=2, replica_groups={{0,16,32,48,64,80,96,112,128,144,160,176,192,208,224,240},{8,24,40,56,7..., dimensions={0}, use_global_device_ids=true | all-gather | bytes 905216 | tf_op jit(solution)/shard_map/all_gather | solution.py:148
  81.0 10.0 %collective-permute-start.2 = (f32[296,128]{1,0:T(8,128)S(1)}, f32[296,128]{1,0:T(8,128)S(1)}, u32[]{:S(2)}, u32[]{:S(2)}) collective-permute-start(f32[296,128]{1,0:T(8,128)S(1)} %pad_maximum_fusion.mine_ref), channel_id=1, source_target_pairs={{0,8},{8,0},{16,24},{24,16},{32,40},{40,32},{48,56},{56,48},{64,72... | collective-permute-start | bytes 454664 | tf_op jit(solution)/shard_map/ppermute | solution.py:154
  91.1 0.6 pad_bitcast_fusion.reach_ref
  91.7 0.3 collective-permute-done.2.other_ref
  92.0 0.1 copy.24
  92.2 0.5 fusion.15
  92.7 2.6 %collective-permute-start.3 = (f16[2,4,64,128]{3,0,1,2:T(2,128)(2,1)S(1)}, f16[2,4,64,128]{3,0,1,2:T(2,128)(2,1)S(1)}, u32[]{:S(2)}, u32[]{:S(2)}) collective-permute-start(f16[2,4,64,128]{3,0,1,2:T(2,128)(2,1)S(1)} %fusion.15), channel_id=1, source_target_pairs={{0,256},{8,264},{16,272},{24,280},{32,288},{40,296},{48,304},{56,3... | collective-permute-start | bytes 393224 | tf_op jit(solution)/shard_map/ppermute | solution.py:159
  95.4 5.9 %shard_map.64 = (f32[64,256]{1,0:T(8,128)}, f32[8,256]{1,0:T(8,128)}) custom-call(f32[296,128]{1,0:T(8,128)} %copy-done.2, f32[296,128]{1,0:T(8,128)} %copy-done.3, f32[1,128]{1,0:T(1,128)} %pad_bitcast_fusion.reach_ref, f32[72,256]{1,0:T(8,128)} %copy-done.1), custom_call_target="tpu_custom_call" | custom-call | tf_op jit(solution)/shard_map/pallas_call | solution.py:109
  101.3 0.7 broadcast_divide_fusion
  102.0 0.1 copy.21
  102.2 0.4 broadcast_select_fusion
  102.6 0.2 convert_multiply_fusion
  102.8 0.7 fusion.7
  103.5 0.4 reshape.189
  103.9 3.6 %fusion.1 = (bf16[256,2048]{1,0:T(8,128)(2,1)S(1)}, bf16[256,2048]{1,0:T(8,128)(2,1)S(1)}) fusion(f32[256,2048]{1,0:T(8,128)} %param.6, f32[64,256]{1,0:T(8,128)S(1)} %copy-done.5, f32[64,2048]{1,0:T(8,128)S(1)} %reshape.189), kind=kOutput, calls=%fused_computation.6 | convolution fusion | flops 405274624 | bytes 4784128 | tf_op jit(solution)/shard_map/dot_general | solution.py:166
  107.6 7.0 %shard_map.65 = f32[8,256,256]{2,1,0:T(8,128)S(1)} custom-call(bf16[4,8,2,32,2048]{4,3,2,1,0:T(8,128)(2,1)} %bitcast.25, bf16[256,2048]{1,0:T(8,128)(2,1)S(1)} %get-tuple-element.18.high_ref, bf16[256,2048]{1,0:T(8,128)(2,1)S(1)} %get-tuple-element.17.low_ref), custom_call_target="tpu_custom_call" | custom-call | tf_op jit(solution)/shard_map/pallas_call | solution.py:57
  114.5 0.3 multiply_convert_fusion
  114.8 19.3 %all_to_all.10 = f16[8,256,256]{2,1,0:T(8,128)(2,1)S(1)} all-to-all(f16[8,256,256]{2,1,0:T(8,128)(2,1)S(1)} %multiply_convert_fusion), channel_id=1, replica_groups=mesh['row'=64,'col'=8] {'col'}, dimensions={0} | all-to-all | bytes 2097152 | tf_op jit(solution)/shard_map/all_to_all | solution.py:174
  134.1 0.1 convert_reduce_fusion
  134.3 0.8 copy.26
  (45 shorter events, 0.6 us)
Async XLA Ops:
  6.5 6.7 %copy-start.6 = (s32[64]{0:T(128)S(1)}, s32[64]{0:T(128)}, u32[]{:S(2)}) copy-start(s32[64]{0:T(128)} %param.9) | copy-start | bytes 772
  6.5 6.7 %copy-start.7 = (s32[64]{0:T(128)S(1)}, s32[64]{0:T(128)}, u32[]{:S(2)}) copy-start(s32[64]{0:T(128)} %param.8) | copy-start | bytes 772
  6.5 6.7 %copy-start = (f32[256,2048]{1,0:T(8,128)S(1)}, f32[256,2048]{1,0:T(8,128)}, u32[]{:S(2)}) copy-start(f32[256,2048]{1,0:T(8,128)} %param.6) | copy-start | bytes 6291460
  6.5 101.0 %all-gather.3.cloned.1.call-start = ((), (), s32[]{:S(2)}) async-start(), calls=%async_computation.2 | async-start | bytes 8650752 | tf_op jit(solution)/shard_map/all_gather | solution.py:132
  6.5 7.9 %collective-permute-start = (bf16[32,2048]{1,0:T(8,128)(2,1)}, bf16[32,2048]{1,0:T(8,128)(2,1)S(1)}, u32[]{:S(2)}, u32[]{:S(2)}) collective-permute-start(bf16[32,2048]{1,0:T(8,128)(2,1)} %bitcast.34), channel_id=1, source_target_pairs={{0,256},{8,264},{16,272},{24,280},{32,288},{40,296},{48,304},{56,3... | collective-permute-start | bytes 393224 | tf_op jit(solution)/shard_map/ppermute | solution.py:120
  13.3 2.1 %copy-start.4 = (bf16[2048,32]{0,1:T(8,128)(2,1)S(1)}, bf16[2048,32]{0,1:T(8,128)(2,1)}, u32[]{:S(2)}) copy-start(bf16[2048,32]{0,1:T(8,128)(2,1)} %param.7) | copy-start | bytes 393220
  16.1 15.4 %all-to-all-start = ((f32[8,72,256]{2,1,0:T(8,128)}), f32[8,72,256]{2,1,0:T(8,128)S(1)}, u32[]{:S(2)}, u32[]{:S(2)}) async-start(f32[8,72,256]{2,1,0:T(8,128)} %broadcast_in_dim.7), calls=%async_computation | async-start | bytes 1179648 | tf_op jit(solution)/shard_map/all_to_all | solution.py:134
  22.5 68.5 %copy-start.8 = (f32[64]{0:T(128)S(1)}, f32[64]{0:T(128)}, u32[]{:S(2)}) copy-start(f32[64]{0:T(128)} %param.11) | copy-start | bytes 772
  22.5 68.5 %copy-start.9 = (s32[64]{0:T(128)S(1)}, s32[64]{0:T(128)}, u32[]{:S(2)}) copy-start(s32[64]{0:T(128)} %param.10) | copy-start | bytes 772
  31.6 60.5 %copy-start.1 = (f32[72,256]{1,0:T(8,128)}, f32[72,256]{1,0:T(8,128)S(1)}, u32[]{:S(2)}) copy-start(f32[72,256]{1,0:T(8,128)S(1)} %reduce_sum.37.parts_ref) | copy-start | bytes 221188
  32.2 4.9 %collective-permute-start.1 = (f32[104,128]{1,0:T(8,128)S(1)}, f32[104,128]{1,0:T(8,128)S(1)}, u32[]{:S(2)}, u32[]{:S(2)}) collective-permute-start(f32[104,128]{1,0:T(8,128)S(1)} %maximum_maximum_fusion), channel_id=1, source_target_pairs={{0,256},{8,264},{16,272},{24,280},{32,288},{40,296},{48,304},{56,3... | collective-permute-start | bytes 159752 | tf_op jit(solution)/shard_map/ppermute | solution.py:145
  81.0 14.3 %copy-start.2 = (f32[296,128]{1,0:T(8,128)}, f32[296,128]{1,0:T(8,128)S(1)}, u32[]{:S(2)}) copy-start(f32[296,128]{1,0:T(8,128)S(1)} %pad_maximum_fusion.mine_ref) | copy-start | bytes 454660
  81.0 11.0 %collective-permute-start.2 = (f32[296,128]{1,0:T(8,128)S(1)}, f32[296,128]{1,0:T(8,128)S(1)}, u32[]{:S(2)}, u32[]{:S(2)}) collective-permute-start(f32[296,128]{1,0:T(8,128)S(1)} %pad_maximum_fusion.mine_ref), channel_id=1, source_target_pairs={{0,8},{8,0},{16,24},{24,16},{32,40},{40,32},{48,56},{56,48},{64,72... | collective-permute-start | bytes 454664 | tf_op jit(solution)/shard_map/ppermute | solution.py:154
  92.0 3.3 %copy-start.3 = (f32[296,128]{1,0:T(8,128)}, f32[296,128]{1,0:T(8,128)S(1)}, u32[]{:S(2)}) copy-start(f32[296,128]{1,0:T(8,128)S(1)} %collective-permute-done.2.other_ref) | copy-start | bytes 454660
  92.7 9.9 %collective-permute-start.3 = (f16[2,4,64,128]{3,0,1,2:T(2,128)(2,1)S(1)}, f16[2,4,64,128]{3,0,1,2:T(2,128)(2,1)S(1)}, u32[]{:S(2)}, u32[]{:S(2)}) collective-permute-start(f16[2,4,64,128]{3,0,1,2:T(2,128)(2,1)S(1)} %fusion.15), channel_id=1, source_target_pairs={{0,256},{8,264},{16,272},{24,280},{32,288},{40,296},{48,304},{56,3... | collective-permute-start | bytes 393224 | tf_op jit(solution)/shard_map/ppermute | solution.py:159
  101.3 2.7 %copy-start.5 = (f32[64,256]{1,0:T(8,128)S(1)}, f32[64,256]{1,0:T(8,128)}, u32[]{:S(2)}) copy-start(f32[64,256]{1,0:T(8,128)} %get-tuple-element.11) | copy-start | bytes 196612
Sparse Core Ops, SparseCore 0:
  16.2 89.3 all-gather.2

commit v9 on v8

v9 whole, which is shorter than its diff:
```python
import jax
import jax.numpy as jnp
from jax import lax
from jax.experimental import pallas as pl
from jax.experimental.pallas import tpu as pltpu
from jax.sharding import PartitionSpec as P

HIGH = lax.Precision.HIGHEST
F32 = jnp.float32
BF16 = jnp.bfloat16

Y, Z, CORES = 2, 16, 2
COLS = 8
BR = 64


def row_of(y, z, core):
    return y * Z * CORES + z * CORES + core


ROWS = [(y, z, core) for y in range(Y) for z in range(Z) for core in range(CORES)]
OTHER_Y = [(row_of(y, z, k), row_of(1 - y, z, k)) for y, z, k in ROWS]
ALONG_Z_CORE = [[row_of(y, z, k) for z in range(Z) for k in range(CORES)] for y in range(Y)]
ALONG_Y = [[row_of(y, z, k) for y in range(Y)] for z in range(Z) for k in range(CORES)]
ALONG_Z = [[row_of(y, z, k) for z in range(Z)] for y in range(Y) for k in range(CORES)]
OTHER_CORE = [(row_of(y, z, k), row_of(y, z, 1 - k)) for y, z, k in ROWS]


def incidence_of(node_ids, from_node, to_node):
    plus = (node_ids[:, None] == from_node[None, :]).astype(F32)
    minus = (node_ids[:, None] == to_node[None, :]).astype(F32)
    return plus - minus


def split(values):
    high = lax.reduce_precision(values, 8, 7)
    return high.astype(BF16), (values - high).astype(BF16)


def in_order(position, mine, other):
    return jnp.where(position == 0, jnp.stack([mine, other]), jnp.stack([other, mine]))


def nt(left, right):
    return lax.dot_general(left, right, (((1,), (1,)), ((), ())), preferred_element_type=F32)


def differences(sensitivity, ends):
    rows, nodes = sensitivity.shape

    def body(values_ref, ends_ref, out_ref):
        values = values_ref[...]
        high = values.astype(BF16)
        low = (values - high.astype(F32)).astype(BF16)
        branch = lax.broadcasted_iota(jnp.int32, (BR, BR), 0)
        diagonal = branch == lax.broadcasted_iota(jnp.int32, (BR, BR), 1)
        ids = jnp.sum(jnp.where(diagonal, ends_ref[0:1], 0.0), axis=1, keepdims=True)
        other_ids = jnp.sum(jnp.where(diagonal, ends_ref[1:2], 0.0), axis=1, keepdims=True)
        node = lax.broadcasted_iota(jnp.int32, (BR, nodes), 1).astype(F32)
        select = jnp.where(node == ids, 1.0, jnp.where(node == other_ids, -1.0, 0.0)).astype(BF16)
        columns = nt(select, high) + nt(select, low)
        sums = nt(jnp.ones((8, nodes), BF16), jnp.abs(high))
        for copy in range(COLS):
            out_ref[copy, :BR] = columns
            out_ref[copy, BR:] = sums

    return pl.pallas_call(
        body,
        out_shape=jax.ShapeDtypeStruct((COLS, BR + 8, rows), F32),
        compiler_params=pltpu.CompilerParams(vmem_limit_bytes=20 * 1024 * 1024),
    )(sensitivity, ends)


def products(loads, sensitivity, solved, ends, other_ends, y):
    blocks, lines, sides, slots, nodes = loads.shape
    rows = sensitivity.shape[0]
    cores, places, _, half = ends.shape
    count = lines * slots
    taken = 4

    def split_here(values):
        high = values.astype(BF16)
        return high, (values - high.astype(F32)).astype(BF16)

    def body(y_ref, loads_ref, values_ref, solved_ref, ends_ref, other_ref, out_ref, high, low, ends_high, ends_low):
        @pl.when((pl.program_id(0) == 0) & (pl.program_id(1) == 0))
        def _():
            first = y_ref[0] == 0
            for place in range(places):
                for core in range(cores):
                    mine, other = ends_ref[core, place], other_ref[core, place]
                    at = (place * cores + core) * 2 * half
                    for piece in (jnp.where(first, mine, other), jnp.where(first, other, mine)):
                        ends_high[:, at:at + half], ends_low[:, at:at + half] = split_here(piece)
                        at += half
            solved_high, solved_low = split_here(solved_ref[...].T)
            for at in range(0, nodes, 512):
                here = slice(at, at + 512)
                drop = jnp.dot(solved_high, ends_high[:, here], preferred_element_type=F32)
                drop += jnp.dot(solved_high, ends_low[:, here], preferred_element_type=F32)
                drop += jnp.dot(solved_low, ends_high[:, here], preferred_element_type=F32)
                high[:, here], low[:, here] = split_here(values_ref[:, here] - drop)

        tile = loads_ref[...].reshape(taken * count, nodes)
        out_ref[...] = (nt(tile, high[...]) + nt(tile, low[...])).reshape(taken, count, rows)

    def whole(shape):
        return pl.BlockSpec(shape, lambda side, block: (0,) * len(shape))

    return pl.pallas_call(
        body,
        grid=(sides, blocks // taken),
        in_specs=[
            pl.BlockSpec(memory_space=pltpu.SMEM),
            pl.BlockSpec((taken, lines, 1, slots, nodes), lambda side, block: (block, 0, side, 0, 0)),
            whole(sensitivity.shape), whole(solved.shape), whole(ends.shape), whole(ends.shape),
        ],
        out_specs=pl.BlockSpec((taken, count, rows), lambda side, block: (side * (blocks // taken) + block, 0, 0)),
        out_shape=jax.ShapeDtypeStruct((sides * blocks, count, rows), F32),
        scratch_shapes=[pltpu.VMEM((rows, nodes), BF16)] * 2 + [pltpu.VMEM((BR, nodes), BF16)] * 2,
        compiler_params=pltpu.CompilerParams(vmem_limit_bytes=48 * 1024 * 1024),
    )(y.astype(jnp.int32).reshape(1), loads, sensitivity, solved, ends, other_ends)


def unit_of(bound):
    return jnp.maximum(bound, 1e-30) / 8192.0


def solve(mine, other, impedance, flags, parts):
    size, width = BR, parts.shape[1]
    tail = mine.shape[0] - size // 2 - 8
    lanes = 128
    height = size // 2

    def body(mine_ref, other_ref, impedance_ref, flags_ref, parts_ref, out_ref, unit_ref, inverse_ref):
        sums = mine_ref[tail:] + other_ref[tail:]
        left = jnp.concatenate([sums[:height, :size], sums[:height, size:]], axis=0)
        left = jnp.concatenate([left, jnp.zeros((size, lanes - size), F32)], axis=1)
        rows = lax.broadcasted_iota(jnp.int32, (size, lanes), 0)
        diagonal = rows == lax.broadcasted_iota(jnp.int32, (size, lanes), 1)
        reach = impedance_ref[...] * (1.0 + 3.0 * flags_ref[...].astype(F32))
        reach = jnp.concatenate([reach, jnp.zeros_like(reach)], axis=1)
        left = left + jnp.where(diagonal, reach, 0.0)
        end_bound = jnp.sum(jnp.where(diagonal, sums[height:height + 1], 0.0), axis=1, keepdims=True)
        parts = [left] + [parts_ref[:size, at:at + lanes] for at in range(0, width, lanes)]
        own, other = jnp.zeros((size, lanes), F32), jnp.zeros((size, lanes), F32)
        for k in range(0, size, 2):
            first = jnp.broadcast_to(parts[0][:, k:k + 1], (size, lanes))
            second = jnp.broadcast_to(parts[0][:, k + 1:k + 2], (size, lanes))
            a, b, c, d = first[k:k + 1], second[k:k + 1], first[k + 1:k + 2], second[k + 1:k + 2]
            inverse = 1.0 / (a * d - b * c)
            upper, lower = rows == k, rows == k + 1
            pivots = upper | lower
            up = jnp.where(pivots, 0.0, (first * d - second * c) * inverse)
            down = jnp.where(pivots, 0.0, (second * a - first * b) * inverse)
            own = jnp.where(upper, d * inverse, jnp.where(lower, a * inverse, own))
            other = jnp.where(upper, -b * inverse, jnp.where(lower, -c * inverse, other))
            parts = [values - up * values[k:k + 1] - down * values[k + 1:k + 2] for values in parts]
        even = rows % 2 == 0
        for at, values in enumerate(parts[1:]):
            following = jnp.concatenate([values[1:], values[:1]], axis=0)
            previous = jnp.concatenate([values[-1:], values[:-1]], axis=0)
            solved = own * values + other * jnp.where(even, following, previous)
            here = slice(at * lanes, (at + 1) * lanes)
            out_ref[:, here] = solved * unit_of(end_bound)
            bound = parts_ref[size:size + 1, here] + jnp.sum(jnp.abs(solved) * end_bound, axis=0, keepdims=True)
            unit_ref[:, here] = unit_of(bound)
            inverse_ref[:, here] = 1.0 / unit_of(bound)

    out_shape = tuple(jax.ShapeDtypeStruct((height, width), F32) for height in (size, 1, 1))
    return pl.pallas_call(body, out_shape=out_shape)(mine, other, impedance, flags, parts)


def on_device(sensitivity, injections, from_node, to_node, switch_flags, impedance):
    row_count, col_count = sensitivity.shape
    row = lax.axis_index("row")
    col = lax.axis_index("col")
    y, core = row // (Z * CORES), row % CORES
    slots = injections.shape[1]

    loads = injections.T
    pair = lax.all_gather(loads, "row", axis_index_groups=ALONG_Y, axis=0)

    row_select = incidence_of(row * row_count + jnp.arange(row_count, dtype=jnp.int32), from_node, to_node)
    copies = differences(sensitivity, (jnp.stack([from_node, to_node]) - col * col_count).astype(F32))

    gathered = lax.all_gather(pair, "row", axis_index_groups=ALONG_Z_CORE, axis=0)

    parts = lax.all_to_all(copies, "col", 0, 0, tiled=True)
    parts = jnp.sum(parts, axis=0)
    columns_t, row_bound = parts[:BR], parts[BR:]

    half = row_count // 2
    first, second = columns_t[:, :half], columns_t[:, half:]
    cap_part = jnp.dot(columns_t, row_select, precision=HIGH, preferred_element_type=F32)
    cap_part = jnp.concatenate([cap_part[: BR // 2], cap_part[BR // 2:]], axis=1)
    end_bound = jnp.dot(row_bound, jnp.abs(row_select), precision=HIGH, preferred_element_type=F32)
    cap_part = jnp.concatenate([cap_part, jnp.concatenate([end_bound, end_bound], axis=1)], axis=0)
    give = jnp.concatenate([jnp.where(y == 0, second, first), cap_part], axis=0)
    take = lax.ppermute(give, "row", OTHER_Y)
    blocks = COLS // Y
    block = jnp.where(col // blocks == y, jnp.where(y == 0, first, second), take[:BR])
    line = lax.all_gather(
        jnp.concatenate([block, cap_part + take[BR:]], axis=0), "row", axis_index_groups=ALONG_Z, axis=0
    )
    zs = Z // blocks
    ends = lax.dynamic_slice_in_dim(line[:, :BR], (col % blocks) * zs, zs, 0).reshape(zs * BR, half)
    mine = jnp.concatenate([ends, jnp.sum(line[:, BR:], axis=0)], axis=0)
    other = lax.ppermute(mine, "row", OTHER_CORE)
    ends = in_order(core, mine[: zs * BR], other[: zs * BR])
    end_bound = mine[-8, :BR] + other[-8, :BR]
    ends = ends.reshape(CORES, zs, BR, half) * (1.0 / unit_of(end_bound))[:, None]
    other_ends = lax.ppermute(ends.astype(jnp.float16), "row", OTHER_Y)

    solved, unit, inverse = solve(mine, other, impedance[None], switch_flags[None], parts)

    loads = gathered.reshape(blocks, zs * CORES, Y, slots, col_count)
    packed = products(loads, sensitivity, solved, ends, other_ends.astype(F32), y)

    arrived = lax.all_to_all((packed * inverse).astype(jnp.float16), "col", 0, 0, tiled=True)
    total = jnp.sum(arrived.astype(F32), axis=0) * unit
    return total.T


def solution(mesh):
    placed = (P("row", "col"), P("col", "row"), P(), P(), P(), P())
    return jax.shard_map(
        on_device, mesh=mesh, in_specs=placed, out_specs=P("row", "col"), check_vma=False
    )
```

time: 143 us -> 143 us (level)
  blocking collectives: 63 us -> 74.7 us
  matrix products: 7.5 us -> 0.58 us
  starting transfers between devices: 25.3 us -> 19 us
  Pallas kernels: 12.9 us -> 15.9 us
  other arithmetic: 4.19 us -> 1.5 us
    all_gather x0 -> x1, blocking collectives: none -> 7 us  [on_device(): pair = lax.all_gather(loads, 'row', axis_index_groups=ALONG_Y, axis=0)]
    dot_general x5 -> x2, matrix products: 7.5 us -> 0.58 us  [the longest x1 0.32 us: on_device(): jnp.dot(columns_t, row_select, precision=HIGH, preferred_element_type=F32)]
    ppermute x2 -> x1, starting transfers between devices: 6.81 us -> 1.92 us  [on_device(): other_ends = lax.ppermute(ends.astype(jnp.float16), 'row', OTHER_Y)]
    all_gather x1, blocking collectives: 43.7 us -> 46.3 us  [on_device(): lax.all_gather(jnp.concatenate([block, cap_part + take[BR:]], axis=0), 'r...]
    unnamed x20, local copies, waits for them, and re-layouts: 0.05 us -> 2.45 us
    all_to_all x1, blocking collectives: 19.3 us -> 21.5 us  [on_device(): lax.all_to_all((packed * inverse).astype(jnp.float16), 'col', 0, 0, tiled...]
    ppermute x1, starting transfers between devices: 9.99 us -> 7.96 us  [on_device(): other = lax.ppermute(mine, 'row', OTHER_CORE)]
    pallas_call x1 -> x2, Pallas kernels: 5.92 us -> 7.87 us  [the longest x1 5.95 us: solve(): pl.pallas_call(body, out_shape=out_shape)]
  transfers between devices with their start and end apart: 6 -> 5, of which waited for: 3 -> 3; matrix products, arithmetic and copies ran while one was open for 8% -> 1% of each run, Pallas kernels for 4% -> 6%
where the time goes in v9:
time: 143 us; the launch traced here: 142 us
  blocking collectives  74.7 us (52%)
  starting transfers between devices  19 us (13%)
  Pallas kernels  15.9 us (11%)
  between operations  13.7 us (10%)
  waiting for transfers between devices  13.4 us (9%)
  local copies, waits for them, and re-layouts  3.38 us (2%)
  other arithmetic  1.5 us (1%)
    all_gather x1, blocking collectives, on_device(): lax.all_gather(jnp.concatenate([block, cap_part + take[BR:]], axis=0), 'r...  46.3 us
    all_to_all x1, blocking collectives, on_device(): lax.all_to_all((packed * inverse).astype(jnp.float16), 'col', 0, 0, tiled...  21.5 us
    all_to_all x1, waiting for transfers between devices, on_device(): parts = lax.all_to_all(copies, 'col', 0, 0, tiled=True)  9.05 us
    pallas_call x1, Pallas kernels, products(): pl.pallas_call(body, grid=(sides, blocks // taken), in_specs=[pl.BlockSpe...  8.05 us
    ppermute x1, starting transfers between devices, on_device(): other = lax.ppermute(mine, 'row', OTHER_CORE)  7.96 us
    all_to_all x1, starting transfers between devices, on_device(): parts = lax.all_to_all(copies, 'col', 0, 0, tiled=True)  7.23 us
    all_gather x1, blocking collectives, on_device(): pair = lax.all_gather(loads, 'row', axis_index_groups=ALONG_Y, axis=0)  7 us
    pallas_call x1, Pallas kernels, solve(): pl.pallas_call(body, out_shape=out_shape)  5.95 us
  transfers between devices with their start and end apart: 5, of which 3 were waited for; matrix products, arithmetic and copies ran while one was open for 1% of the time, Pallas kernels for 6%

profile of v9, /device:TPU:1, one launch (start us, length us, event | category | flops | bytes accessed | tf_op | source)
XLA Modules:
  0.0 142.2 jit_solution(13618779859123472675)
XLA Ops:
  6.5 0.0 all-gather.5.cloned.1.call-start
  6.5 7.0 %all-gather = bf16[64,2048]{1,0:T(8,128)(2,1)} all-gather(bf16[32,2048]{1,0:T(8,128)(2,1)} %bitcast.25), channel_id=2, replica_groups={{0,256},{8,264},{16,272},{24,280},{32,288},{40,296},{48,304},{56,312},{..., dimensions={0}, use_global_device_ids=true | all-gather | bytes 393216 | tf_op jit(solution)/shard_map/all_gather | solution.py:182
  13.5 0.0 all-gather.5.cloned.1.call-update
  13.6 0.7 fusion.16.ends_ref
  14.3 1.6 %copy-done = f32[256,2048]{1,0:T(8,128)S(1)} copy-done((f32[256,2048]{1,0:T(8,128)S(1)}, f32[256,2048]{1,0:T(8,128)}, u32[]{:S(2)}) %copy-start) | copy-done | bytes 2097176
  15.8 1.9 %shard_map.64 = f32[8,72,256]{2,1,0:T(8,128)} custom-call(f32[256,2048]{1,0:T(8,128)S(1)} %copy-done, f32[2,64]{1,0:T(2,128)S(1)} %fusion.16.ends_ref), custom_call_target="tpu_custom_call" | custom-call | tf_op jit(solution)/shard_map/pallas_call | solution.py:67
  17.8 7.2 %all-to-all-start = ((f32[8,72,256]{2,1,0:T(8,128)}), f32[8,72,256]{2,1,0:T(8,128)S(1)}, u32[]{:S(2)}, u32[]{:S(2)}) async-start(f32[8,72,256]{2,1,0:T(8,128)} %shard_map.64), calls=%async_computation | async-start | bytes 1179648 | tf_op jit(solution)/shard_map/all_to_all | solution.py:189
  25.0 9.1 %all-to-all-done = f32[8,72,256]{2,1,0:T(8,128)S(1)} async-done(((f32[8,72,256]{2,1,0:T(8,128)}), f32[8,72,256]{2,1,0:T(8,128)S(1)}, u32[]{:S(2)}, u32[]{:S(2)}) %all-to-all-start) | async-done | bytes 589856 | tf_op jit(solution)/shard_map/all_to_all | solution.py:189
  34.1 0.3 fusion.1
  34.4 0.3 fusion.3
  34.7 0.1 maximum_maximum_fusion
  34.8 1.9 %collective-permute-start = (f32[104,128]{1,0:T(8,128)S(1)}, f32[104,128]{1,0:T(8,128)S(1)}, u32[]{:S(2)}, u32[]{:S(2)}) collective-permute-start(f32[104,128]{1,0:T(8,128)S(1)} %maximum_maximum_fusion), channel_id=1, source_target_pairs={{0,256},{8,264},{16,272},{24,280},{32,288},{40,296},{48,304},{56,3... | collective-permute-start | bytes 159752 | tf_op jit(solution)/shard_map/ppermute | solution.py:200
  36.8 3.3 %collective-permute-done = f32[104,128]{1,0:T(8,128)S(1)} collective-permute-done((f32[104,128]{1,0:T(8,128)S(1)}, f32[104,128]{1,0:T(8,128)S(1)}, u32[]{:S(2)}, u32[]{:S(2)}) %collective-permute-start) | collective-permute-done | bytes 53280 | tf_op jit(solution)/shard_map/ppermute | solution.py:200
  40.1 0.1 slice_add_fusion
  40.2 46.3 %all-gather.2 = f32[1664,128]{1,0:T(8,128)S(1)} all-gather(f32[104,128]{1,0:T(8,128)S(1)} %pad_maximum_fusion.1), channel_id=4, replica_groups={{0,16,32,48,64,80,96,112,128,144,160,176,192,208,224,240},{8,24,40,56,7..., dimensions={0}, use_global_device_ids=true | all-gather | bytes 905216 | tf_op jit(solution)/shard_map/all_gather | solution.py:203
  86.6 0.0 copy-start.4
  86.6 8.0 %collective-permute-start.1 = (f32[296,128]{1,0:T(8,128)S(1)}, f32[296,128]{1,0:T(8,128)S(1)}, u32[]{:S(2)}, u32[]{:S(2)}) collective-permute-start(f32[296,128]{1,0:T(8,128)S(1)} %pad_maximum_fusion.mine_ref), channel_id=1, source_target_pairs={{0,8},{8,0},{16,24},{24,16},{32,40},{40,32},{48,56},{56,48},{64,72... | collective-permute-start | bytes 454664 | tf_op jit(solution)/shard_map/ppermute | solution.py:209
  94.6 1.0 collective-permute-done.1.other_ref
  95.6 0.1 fusion.18
  95.7 1.9 %collective-permute-start.2 = (f16[2,4,64,128]{3,2,1,0:T(8,128)(2,1)S(1)}, f16[2,4,64,128]{3,2,1,0:T(8,128)(2,1)S(1)}, u32[]{:S(2)}, u32[]{:S(2)}) collective-permute-start(f16[2,4,64,128]{3,2,1,0:T(8,128)(2,1)S(1)} %get-tuple-element.11), channel_id=1, source_target_pairs={{0,256},{8,264},{16,272},{24,280},{32,288},{40,296},{48,304},{56,3... | collective-permute-start | bytes 393224 | tf_op jit(solution)/shard_map/ppermute | solution.py:213
  97.7 6.0 %shard_map.65 = (f32[64,256]{1,0:T(8,128)}, f32[1,256]{1,0:T(1,128)}, f32[1,256]{1,0:T(1,128)}) custom-call(f32[296,128]{1,0:T(8,128)} %copy-done.4, f32[296,128]{1,0:T(8,128)} %copy-done.5, f32[1,64]{1,0:T(1,128)} %bitcast.28, s32[1,64]{1,0:T(1,128)} %bitcast.29, f32[72,256]{1,0:T(8,128)} %copy-done.3), custom_call_target="tpu_custom_call" | custom-call | tf_op jit(solution)/shard_map/pallas_call | solution.py:171
  103.6 0.0 collective-permute-done.2
  103.6 0.0 all-gather.5.cloned.1.call-done
  103.7 0.0 copy-done.1
  103.7 0.0 copy-start.2
  103.7 0.8 copy-done.2
  104.5 8.0 %shard_map.66 = f32[8,256,256]{2,1,0:T(8,128)S(1)} custom-call(s32[1]{0:T(128)} %bitcast.y_ref, bf16[4,8,2,32,2048]{4,3,2,1,0:T(8,128)(2,1)} %bitcast.19, f32[256,2048]{1,0:T(8,128)S(1)} %copy-done.1, f32[64,256]{1,0:T(8,128)S(1)} %copy-done.2, f32[2,4,64,128]{3,2,1,0:T(8,128)S(1)} %get-tuple-element.12.ends_ref, ...), custom_call_target="tpu_custom_call" | custom-call | tf_op jit(solution)/shard_map/pallas_call | solution.py:110
  112.6 0.0 copy-done.7
  112.6 0.3 multiply_convert_fusion
  112.9 21.5 %all_to_all.10 = f16[8,256,256]{2,1,0:T(8,128)(2,1)S(1)} all-to-all(f16[8,256,256]{2,1,0:T(8,128)(2,1)S(1)} %multiply_convert_fusion), channel_id=1, replica_groups=mesh['row'=64,'col'=8] {'col'}, dimensions={0} | all-to-all | bytes 2097152 | tf_op jit(solution)/shard_map/all_to_all | solution.py:220
  134.3 0.1 convert_reduce_fusion
  134.5 0.8 copy.7
  (29 shorter events, 0.3 us)
Async XLA Ops:
  6.5 97.1 %all-gather.5.cloned.1.call-start = ((), (), s32[]{:S(2)}) async-start(), calls=%async_computation.2 | async-start | bytes 8650752 | tf_op jit(solution)/shard_map/all_gather | solution.py:187
  14.3 1.6 %copy-start = (f32[256,2048]{1,0:T(8,128)S(1)}, f32[256,2048]{1,0:T(8,128)}, u32[]{:S(2)}) copy-start(f32[256,2048]{1,0:T(8,128)} %values_ref.3) | copy-start | bytes 6291460
  15.8 18.2 %copy-start.8 = (s32[64]{0:T(128)S(1)}, s32[64]{0:T(128)}, u32[]{:S(2)}) copy-start(s32[64]{0:T(128)} %param.9) | copy-start | bytes 772
  15.8 18.3 %copy-start.9 = (s32[64]{0:T(128)S(1)}, s32[64]{0:T(128)}, u32[]{:S(2)}) copy-start(s32[64]{0:T(128)} %param.8) | copy-start | bytes 772
  17.8 16.3 %all-to-all-start = ((f32[8,72,256]{2,1,0:T(8,128)}), f32[8,72,256]{2,1,0:T(8,128)S(1)}, u32[]{:S(2)}, u32[]{:S(2)}) async-start(f32[8,72,256]{2,1,0:T(8,128)} %shard_map.64), calls=%async_computation | async-start | bytes 1179648 | tf_op jit(solution)/shard_map/all_to_all | solution.py:189
  34.1 61.5 %copy-start.3 = (f32[72,256]{1,0:T(8,128)}, f32[72,256]{1,0:T(8,128)S(1)}, u32[]{:S(2)}) copy-start(f32[72,256]{1,0:T(8,128)S(1)} %reduce_sum.27.parts_ref) | copy-start | bytes 221188
  34.8 5.3 %collective-permute-start = (f32[104,128]{1,0:T(8,128)S(1)}, f32[104,128]{1,0:T(8,128)S(1)}, u32[]{:S(2)}, u32[]{:S(2)}) collective-permute-start(f32[104,128]{1,0:T(8,128)S(1)} %maximum_maximum_fusion), channel_id=1, source_target_pairs={{0,256},{8,264},{16,272},{24,280},{32,288},{40,296},{48,304},{56,3... | collective-permute-start | bytes 159752 | tf_op jit(solution)/shard_map/ppermute | solution.py:200
  86.5 17.2 %copy-start.1 = (f32[256,2048]{1,0:T(8,128)S(1)}, f32[256,2048]{1,0:T(8,128)}, u32[]{:S(2)}) copy-start(f32[256,2048]{1,0:T(8,128)} %values_ref.3) | copy-start | bytes 6291460
  86.6 11.1 %copy-start.4 = (f32[296,128]{1,0:T(8,128)}, f32[296,128]{1,0:T(8,128)S(1)}, u32[]{:S(2)}) copy-start(f32[296,128]{1,0:T(8,128)S(1)} %pad_maximum_fusion.mine_ref) | copy-start | bytes 454660
  86.6 9.0 %collective-permute-start.1 = (f32[296,128]{1,0:T(8,128)S(1)}, f32[296,128]{1,0:T(8,128)S(1)}, u32[]{:S(2)}, u32[]{:S(2)}) collective-permute-start(f32[296,128]{1,0:T(8,128)S(1)} %pad_maximum_fusion.mine_ref), channel_id=1, source_target_pairs={{0,8},{8,0},{16,24},{24,16},{32,40},{40,32},{48,56},{56,48},{64,72... | collective-permute-start | bytes 454664 | tf_op jit(solution)/shard_map/ppermute | solution.py:209
  95.6 2.1 %copy-start.5 = (f32[296,128]{1,0:T(8,128)}, f32[296,128]{1,0:T(8,128)S(1)}, u32[]{:S(2)}) copy-start(f32[296,128]{1,0:T(8,128)S(1)} %collective-permute-done.1.other_ref) | copy-start | bytes 454660
  95.7 7.9 %collective-permute-start.2 = (f16[2,4,64,128]{3,2,1,0:T(8,128)(2,1)S(1)}, f16[2,4,64,128]{3,2,1,0:T(8,128)(2,1)S(1)}, u32[]{:S(2)}, u32[]{:S(2)}) collective-permute-start(f16[2,4,64,128]{3,2,1,0:T(8,128)(2,1)S(1)} %get-tuple-element.11), channel_id=1, source_target_pairs={{0,256},{8,264},{16,272},{24,280},{32,288},{40,296},{48,304},{56,3... | collective-permute-start | bytes 393224 | tf_op jit(solution)/shard_map/ppermute | solution.py:213
  103.7 0.8 copy-start.2
  104.5 8.1 %copy-start.7 = (f32[1,256]{1,0:T(1,128)S(1)}, f32[1,256]{1,0:T(1,128)}, u32[]{:S(2)}) copy-start(f32[1,256]{1,0:T(1,128)} %get-tuple-element.9) | copy-start | bytes 3076
  112.9 21.6 %copy-start.6 = (f32[1,256]{1,0:T(1,128)S(1)}, f32[1,256]{1,0:T(1,128)}, u32[]{:S(2)}) copy-start(f32[1,256]{1,0:T(1,128)} %get-tuple-element.10) | copy-start | bytes 3076
Sparse Core Ops, SparseCore 0:
  13.7 89.4 all-gather.4

commit v10 on v9

--- a/solution.py
+++ b/solution.py
@@ -71,7 +71,7 @@
     )(sensitivity, ends)
 
 
-def products(loads, sensitivity, solved, ends, other_ends, y):
+def products(loads, sensitivity, solved, ends, other_ends, unit, y):
     blocks, lines, sides, slots, nodes = loads.shape
     rows = sensitivity.shape[0]
     cores, places, _, half = ends.shape
@@ -82,7 +82,7 @@
         high = values.astype(BF16)
         return high, (values - high.astype(F32)).astype(BF16)
 
-    def body(y_ref, loads_ref, values_ref, solved_ref, ends_ref, other_ref, out_ref, high, low, ends_high, ends_low):
+    def body(y_ref, loads_ref, values_ref, solved_ref, ends_ref, other_ref, unit_ref, out_ref, units_ref, both, inverse, ends_high, ends_low):
         @pl.when((pl.program_id(0) == 0) & (pl.program_id(1) == 0))
         def _():
             first = y_ref[0] == 0
@@ -99,10 +99,15 @@
                 drop = jnp.dot(solved_high, ends_high[:, here], preferred_element_type=F32)
                 drop += jnp.dot(solved_high, ends_low[:, here], preferred_element_type=F32)
                 drop += jnp.dot(solved_low, ends_high[:, here], preferred_element_type=F32)
-                high[:, here], low[:, here] = split_here(values_ref[:, here] - drop)
+                both[:rows, here], both[rows:, here] = split_here(values_ref[:, here] - drop)
+            units_ref[...] = jnp.broadcast_to(unit_ref[...], (count, rows)).T
+            inverse[...] = 1.0 / units_ref[...]
 
         tile = loads_ref[...].reshape(taken * count, nodes)
-        out_ref[...] = (nt(tile, high[...]) + nt(tile, low[...])).reshape(taken, count, rows)
+        sums = nt(both[...], tile)
+        sums = sums[:rows] + sums[rows:]
+        for block in range(taken):
+            out_ref[block] = sums[:, block * count:(block + 1) * count] * inverse[...]
 
     def whole(shape):
         return pl.BlockSpec(shape, lambda side, block: (0,) * len(shape))
@@ -113,13 +118,21 @@
         in_specs=[
             pl.BlockSpec(memory_space=pltpu.SMEM),
             pl.BlockSpec((taken, lines, 1, slots, nodes), lambda side, block: (block, 0, side, 0, 0)),
-            whole(sensitivity.shape), whole(solved.shape), whole(ends.shape), whole(ends.shape),
+            whole(sensitivity.shape), whole(solved.shape), whole(ends.shape), whole(ends.shape), whole(unit.shape),
         ],
-        out_specs=pl.BlockSpec((taken, count, rows), lambda side, block: (side * (blocks // taken) + block, 0, 0)),
-        out_shape=jax.ShapeDtypeStruct((sides * blocks, count, rows), F32),
-        scratch_shapes=[pltpu.VMEM((rows, nodes), BF16)] * 2 + [pltpu.VMEM((BR, nodes), BF16)] * 2,
+        out_specs=(
+            pl.BlockSpec((taken, rows, count), lambda side, block: (side * (blocks // taken) + block, 0, 0)),
+            whole((rows, count)),
+        ),
+        out_shape=(
+            jax.ShapeDtypeStruct((sides * blocks, rows, count), F32), jax.ShapeDtypeStruct((rows, count), F32)
+        ),
+        scratch_shapes=[
+            pltpu.VMEM((2 * rows, nodes), BF16), pltpu.VMEM((rows, count), F32),
+            pltpu.VMEM((BR, nodes), BF16), pltpu.VMEM((BR, nodes), BF16),
+        ],
         compiler_params=pltpu.CompilerParams(vmem_limit_bytes=48 * 1024 * 1024),
-    )(y.astype(jnp.int32).reshape(1), loads, sensitivity, solved, ends, other_ends)
+    )(y.astype(jnp.int32).reshape(1), loads, sensitivity, solved, ends, other_ends, unit)
 
 
 def unit_of(bound):
@@ -132,7 +145,7 @@
     lanes = 128
     height = size // 2
 
-    def body(mine_ref, other_ref, impedance_ref, flags_ref, parts_ref, out_ref, unit_ref, inverse_ref):
+    def body(mine_ref, other_ref, impedance_ref, flags_ref, parts_ref, out_ref, unit_ref):
         sums = mine_ref[tail:] + other_ref[tail:]
         left = jnp.concatenate([sums[:height, :size], sums[:height, size:]], axis=0)
         left = jnp.concatenate([left, jnp.zeros((size, lanes - size), F32)], axis=1)
@@ -165,10 +178,10 @@
             out_ref[:, here] = solved * unit_of(end_bound)
             bound = parts_ref[size:size + 1, here] + jnp.sum(jnp.abs(solved) * end_bound, axis=0, keepdims=True)
             unit_ref[:, here] = unit_of(bound)
-            inverse_ref[:, here] = 1.0 / unit_of(bound)
-
-    out_shape = tuple(jax.ShapeDtypeStruct((height, width), F32) for height in (size, 1, 1))
-    return pl.pallas_call(body, out_shape=out_shape)(mine, other, impedance, flags, parts)
+
+    out_shape = tuple(jax.ShapeDtypeStruct((height, width), F32) for height in (size, 1))
+    params = pltpu.CompilerParams(vmem_limit_bytes=8 * 1024 * 1024)
+    return pl.pallas_call(body, out_shape=out_shape, compiler_params=params)(mine, other, impedance, flags, parts)
 
 
 def on_device(sensitivity, injections, from_node, to_node, switch_flags, impedance):
@@ -212,14 +225,14 @@
     ends = ends.reshape(CORES, zs, BR, half) * (1.0 / unit_of(end_bound))[:, None]
     other_ends = lax.ppermute(ends.astype(jnp.float16), "row", OTHER_Y)
 
-    solved, unit, inverse = solve(mine, other, impedance[None], switch_flags[None], parts)
+    solved, unit = solve(mine, other, impedance[None], switch_flags[None], parts)
 
     loads = gathered.reshape(blocks, zs * CORES, Y, slots, col_count)
-    packed = products(loads, sensitivity, solved, ends, other_ends.astype(F32), y)
-
-    arrived = lax.all_to_all((packed * inverse).astype(jnp.float16), "col", 0, 0, tiled=True)
-    total = jnp.sum(arrived.astype(F32), axis=0) * unit
-    return total.T
+    packed, units = products(loads, sensitivity, solved, ends, other_ends.astype(F32), unit, y)
+
+    arrived = lax.all_to_all(packed.astype(jnp.float16), "col", 0, 0, tiled=True)
+    total = jnp.sum(arrived.astype(F32), axis=0) * units
+    return total
 
 
 def solution(mesh):

time: 143 us -> 142 us (level)
  waiting for transfers between devices: 13.4 us -> 15.3 us
  Pallas kernels: 15.9 us -> 14.2 us
  local copies, waits for them, and re-layouts: 3.38 us -> 1.71 us
    pallas_call x1, Pallas kernels: 5.95 us -> 4.28 us  [solve(): pl.pallas_call(body, out_shape=out_shape, compiler_params=params)]
    all_gather x1, waiting for transfers between devices: 0.02 us -> 1.63 us  [on_device(): lax.all_gather(pair, 'row', axis_index_groups=ALONG_Z_CORE, axis=0)]
    all_gather x1, blocking collectives: 46.3 us -> 44.7 us  [on_device(): lax.all_gather(jnp.concatenate([block, cap_part + take[BR:]], axis=0), 'r...]
  transfers between devices with their start and end apart: 5 -> 5, of which waited for: 3 -> 5; matrix products, arithmetic and copies ran while one was open for 1% -> 1% of each run, Pallas kernels for 6% -> 4%
where the time goes in v10:
time: 142 us; the launch traced here: 141 us
  blocking collectives  73.3 us (52%)
  starting transfers between devices  20.3 us (14%)
  waiting for transfers between devices  15.3 us (11%)
  Pallas kernels  14.2 us (10%)
  between operations  13.6 us (10%)
  other arithmetic  2.13 us (2%)
  local copies, waits for them, and re-layouts  1.71 us (1%)
    all_gather x1, blocking collectives, on_device(): lax.all_gather(jnp.concatenate([block, cap_part + take[BR:]], axis=0), 'r...  44.7 us
    all_to_all x1, blocking collectives, on_device(): lax.all_to_all(packed.astype(jnp.float16), 'col', 0, 0, tiled=True)  21.6 us
    ppermute x1, starting transfers between devices, on_device(): other = lax.ppermute(mine, 'row', OTHER_CORE)  9.21 us
    all_to_all x1, waiting for transfers between devices, on_device(): parts = lax.all_to_all(copies, 'col', 0, 0, tiled=True)  9.05 us
    pallas_call x1, Pallas kernels, products(): pl.pallas_call(body, grid=(sides, blocks // taken), in_specs=[pl.BlockSpe...  8.03 us
    all_to_all x1, starting transfers between devices, on_device(): parts = lax.all_to_all(copies, 'col', 0, 0, tiled=True)  7.22 us
    all_gather x1, blocking collectives, on_device(): pair = lax.all_gather(loads, 'row', axis_index_groups=ALONG_Y, axis=0)  7 us
    pallas_call x1, Pallas kernels, solve(): pl.pallas_call(body, out_shape=out_shape, compiler_params=params)  4.28 us
  transfers between devices with their start and end apart: 5, of which 5 were waited for; matrix products, arithmetic and copies ran while one was open for 1% of the time, Pallas kernels for 4%

profile of v10, /device:TPU:1, one launch (start us, length us, event | category | flops | bytes accessed | tf_op | source)
XLA Modules:
  0.0 141.2 jit_solution(12932517846768227020)
XLA Ops:
  6.5 0.0 all-gather.5.cloned.1.call-start
  6.5 7.0 %all-gather = bf16[64,2048]{1,0:T(8,128)(2,1)} all-gather(bf16[32,2048]{1,0:T(8,128)(2,1)} %bitcast.23), channel_id=2, replica_groups={{0,256},{8,264},{16,272},{24,280},{32,288},{40,296},{48,304},{56,312},{..., dimensions={0}, use_global_device_ids=true | all-gather | bytes 393216 | tf_op jit(solution)/shard_map/all_gather | solution.py:195
  13.5 0.0 all-gather.5.cloned.1.call-update
  13.6 0.7 fusion.16.ends_ref
  14.3 1.6 %copy-done = f32[256,2048]{1,0:T(8,128)S(1)} copy-done((f32[256,2048]{1,0:T(8,128)S(1)}, f32[256,2048]{1,0:T(8,128)}, u32[]{:S(2)}) %copy-start) | copy-done | bytes 2097176
  15.8 1.9 %shard_map.64 = f32[8,72,256]{2,1,0:T(8,128)} custom-call(f32[256,2048]{1,0:T(8,128)S(1)} %copy-done, f32[2,64]{1,0:T(2,128)S(1)} %fusion.16.ends_ref), custom_call_target="tpu_custom_call" | custom-call | tf_op jit(solution)/shard_map/pallas_call | solution.py:67
  17.8 7.2 %all-to-all-start = ((f32[8,72,256]{2,1,0:T(8,128)}), f32[8,72,256]{2,1,0:T(8,128)S(1)}, u32[]{:S(2)}, u32[]{:S(2)}) async-start(f32[8,72,256]{2,1,0:T(8,128)} %shard_map.64), calls=%async_computation | async-start | bytes 1179648 | tf_op jit(solution)/shard_map/all_to_all | solution.py:202
  25.0 9.1 %all-to-all-done = f32[8,72,256]{2,1,0:T(8,128)S(1)} async-done(((f32[8,72,256]{2,1,0:T(8,128)}), f32[8,72,256]{2,1,0:T(8,128)S(1)}, u32[]{:S(2)}, u32[]{:S(2)}) %all-to-all-start) | async-done | bytes 589856 | tf_op jit(solution)/shard_map/all_to_all | solution.py:202
  34.1 0.0 copy-done.4
  34.1 0.3 fusion.1
  34.4 0.3 fusion.3
  34.7 0.1 maximum_maximum_fusion
  34.8 1.9 %collective-permute-start = (f32[104,128]{1,0:T(8,128)S(1)}, f32[104,128]{1,0:T(8,128)S(1)}, u32[]{:S(2)}, u32[]{:S(2)}) collective-permute-start(f32[104,128]{1,0:T(8,128)S(1)} %maximum_maximum_fusion), channel_id=1, source_target_pairs={{0,256},{8,264},{16,272},{24,280},{32,288},{40,296},{48,304},{56,3... | collective-permute-start | bytes 159752 | tf_op jit(solution)/shard_map/ppermute | solution.py:213
  36.7 3.3 %collective-permute-done = f32[104,128]{1,0:T(8,128)S(1)} collective-permute-done((f32[104,128]{1,0:T(8,128)S(1)}, f32[104,128]{1,0:T(8,128)S(1)}, u32[]{:S(2)}, u32[]{:S(2)}) %collective-permute-start) | collective-permute-done | bytes 53280 | tf_op jit(solution)/shard_map/ppermute | solution.py:213
  40.1 0.1 slice_add_fusion
  40.2 0.0 copy-start.2
  40.2 0.0 copy-start.3
  40.2 44.7 %all-gather.2 = f32[1664,128]{1,0:T(8,128)S(1)} all-gather(f32[104,128]{1,0:T(8,128)S(1)} %pad_maximum_fusion.1), channel_id=4, replica_groups={{0,16,32,48,64,80,96,112,128,144,160,176,192,208,224,240},{8,24,40,56,7..., dimensions={0}, use_global_device_ids=true | all-gather | bytes 905216 | tf_op jit(solution)/shard_map/all_gather | solution.py:216
  85.0 9.2 %collective-permute-start.1 = (f32[296,128]{1,0:T(8,128)S(1)}, f32[296,128]{1,0:T(8,128)S(1)}, u32[]{:S(2)}, u32[]{:S(2)}) collective-permute-start(f32[296,128]{1,0:T(8,128)S(1)} %pad_maximum_fusion.mine_ref), channel_id=1, source_target_pairs={{0,8},{8,0},{16,24},{24,16},{32,40},{40,32},{48,56},{56,48},{64,72... | collective-permute-start | bytes 454664 | tf_op jit(solution)/shard_map/ppermute | solution.py:222
  94.3 1.0 collective-permute-done.1.other_ref
  95.3 0.1 fusion.18
  95.4 1.9 %collective-permute-start.2 = (f16[2,4,64,128]{3,2,1,0:T(8,128)(2,1)S(1)}, f16[2,4,64,128]{3,2,1,0:T(8,128)(2,1)S(1)}, u32[]{:S(2)}, u32[]{:S(2)}) collective-permute-start(f16[2,4,64,128]{3,2,1,0:T(8,128)(2,1)S(1)} %get-tuple-element.13), channel_id=1, source_target_pairs={{0,256},{8,264},{16,272},{24,280},{32,288},{40,296},{48,304},{56,3... | collective-permute-start | bytes 393224 | tf_op jit(solution)/shard_map/ppermute | solution.py:226
  97.3 0.0 copy-done.2
  97.3 0.0 copy-done.3
  97.3 4.3 %shard_map.65 = (f32[64,256]{1,0:T(8,128)S(1)}, f32[1,256]{1,0:T(1,128)S(1)}) custom-call(f32[296,128]{1,0:T(8,128)S(1)} %pad_maximum_fusion.mine_ref, f32[296,128]{1,0:T(8,128)S(1)} %collective-permute-done.1.other_ref, f32[1,64]{1,0:T(1,128)S(1)} %bitcast.15, s32[1,64]{1,0:T(1,128)S(1)} %bitcast.16, f32[72,256]{1,0:T(8,128)S(1)} %reduce_sum.27.parts_ref), custom_call_target="tpu_custom_call" | custom-call | tf_op jit(solution)/shard_map/pallas_call | solution.py:184
  101.6 0.4 collective-permute-done.2
  102.0 1.6 %all-gather.5.cloned.1.call-done = bf16[64,32,2048]{2,1,0:T(8,128)(2,1)} async-done(((bf16[2,32,2048]{2,1,0:T(8,128)(2,1)}), bf16[64,32,2048]{2,1,0:T(8,128)(2,1)}) %all-gather.5.cloned.1.call-update) | async-done | bytes 8388624 | tf_op jit(solution)/shard_map/all_gather | solution.py:200
  103.6 8.0 %shard_map.66 = (f32[8,256,256]{2,1,0:T(8,128)S(1)}, f32[256,256]{1,0:T(8,128)S(1)}) custom-call(s32[1]{0:T(128)} %bitcast.y_ref, bf16[4,8,2,32,2048]{4,3,2,1,0:T(8,128)(2,1)} %bitcast.17, f32[256,2048]{1,0:T(8,128)S(1)} %copy-done.1, f32[64,256]{1,0:T(8,128)S(1)} %get-tuple-element.9.solved_ref, f32[2,4,64,128]{3,2,1,0:T(8,128)S(1)} %get-tuple-element.14.ends_ref, ...), custom_call_target="tpu_custom_call" | custom-call | tf_op jit(solution)/shard_map/pallas_call | solution.py:115
  111.7 0.2 convert_element_type.26
  111.9 21.6 %all_to_all.10 = f16[8,256,256]{2,1,0:T(8,128)(2,1)S(1)} all-to-all(f16[8,256,256]{2,1,0:T(8,128)(2,1)S(1)} %convert_element_type.26), channel_id=1, replica_groups=mesh['row'=64,'col'=8] {'col'}, dimensions={0} | all-to-all | bytes 2097152 | tf_op jit(solution)/shard_map/all_to_all | solution.py:233
  133.4 0.1 convert_reduce_fusion
  133.6 0.7 mul.25
  (20 shorter events, 0.2 us)
Async XLA Ops:
  6.5 97.1 %all-gather.5.cloned.1.call-start = ((), (), s32[]{:S(2)}) async-start(), calls=%async_computation.2 | async-start | bytes 8650752 | tf_op jit(solution)/shard_map/all_gather | solution.py:200
  14.3 1.6 %copy-start = (f32[256,2048]{1,0:T(8,128)S(1)}, f32[256,2048]{1,0:T(8,128)}, u32[]{:S(2)}) copy-start(f32[256,2048]{1,0:T(8,128)} %values_ref.3) | copy-start | bytes 6291460
  15.8 18.2 %copy-start.4 = (s32[64]{0:T(128)S(1)}, s32[64]{0:T(128)}, u32[]{:S(2)}) copy-start(s32[64]{0:T(128)} %param.9) | copy-start | bytes 772
  15.8 18.3 %copy-start.5 = (s32[64]{0:T(128)S(1)}, s32[64]{0:T(128)}, u32[]{:S(2)}) copy-start(s32[64]{0:T(128)} %param.8) | copy-start | bytes 772
  17.8 16.3 %all-to-all-start = ((f32[8,72,256]{2,1,0:T(8,128)}), f32[8,72,256]{2,1,0:T(8,128)S(1)}, u32[]{:S(2)}, u32[]{:S(2)}) async-start(f32[8,72,256]{2,1,0:T(8,128)} %shard_map.64), calls=%async_computation | async-start | bytes 1179648 | tf_op jit(solution)/shard_map/all_to_all | solution.py:202
  34.8 5.3 %collective-permute-start = (f32[104,128]{1,0:T(8,128)S(1)}, f32[104,128]{1,0:T(8,128)S(1)}, u32[]{:S(2)}, u32[]{:S(2)}) collective-permute-start(f32[104,128]{1,0:T(8,128)S(1)} %maximum_maximum_fusion), channel_id=1, source_target_pairs={{0,256},{8,264},{16,272},{24,280},{32,288},{40,296},{48,304},{56,3... | collective-permute-start | bytes 159752 | tf_op jit(solution)/shard_map/ppermute | solution.py:213
  40.2 57.2 %copy-start.2 = (f32[64]{0:T(128)S(1)}, f32[64]{0:T(128)}, u32[]{:S(2)}) copy-start(f32[64]{0:T(128)} %param.11) | copy-start | bytes 772
  40.2 57.2 %copy-start.3 = (s32[64]{0:T(128)S(1)}, s32[64]{0:T(128)}, u32[]{:S(2)}) copy-start(s32[64]{0:T(128)} %param.10) | copy-start | bytes 772
  84.9 18.7 %copy-start.1 = (f32[256,2048]{1,0:T(8,128)S(1)}, f32[256,2048]{1,0:T(8,128)}, u32[]{:S(2)}) copy-start(f32[256,2048]{1,0:T(8,128)} %values_ref.3) | copy-start | bytes 6291460
  85.0 10.2 %collective-permute-start.1 = (f32[296,128]{1,0:T(8,128)S(1)}, f32[296,128]{1,0:T(8,128)S(1)}, u32[]{:S(2)}, u32[]{:S(2)}) collective-permute-start(f32[296,128]{1,0:T(8,128)S(1)} %pad_maximum_fusion.mine_ref), channel_id=1, source_target_pairs={{0,8},{8,0},{16,24},{24,16},{32,40},{40,32},{48,56},{56,48},{64,72... | collective-permute-start | bytes 454664 | tf_op jit(solution)/shard_map/ppermute | solution.py:222
  95.4 6.6 %collective-permute-start.2 = (f16[2,4,64,128]{3,2,1,0:T(8,128)(2,1)S(1)}, f16[2,4,64,128]{3,2,1,0:T(8,128)(2,1)S(1)}, u32[]{:S(2)}, u32[]{:S(2)}) collective-permute-start(f16[2,4,64,128]{3,2,1,0:T(8,128)(2,1)S(1)} %get-tuple-element.13), channel_id=1, source_target_pairs={{0,256},{8,264},{16,272},{24,280},{32,288},{40,296},{48,304},{56,3... | collective-permute-start | bytes 393224 | tf_op jit(solution)/shard_map/ppermute | solution.py:226
Sparse Core Ops, SparseCore 0:
  13.7 89.9 all-gather.4

commit v11 on v10

--- a/solution.py
+++ b/solution.py
@@ -109,8 +109,7 @@
         for block in range(taken):
             out_ref[block] = sums[:, block * count:(block + 1) * count] * inverse[...]
 
-    def whole(shape):
-        return pl.BlockSpec(shape, lambda side, block: (0,) * len(shape))
+    whole = pl.BlockSpec(memory_space=pltpu.VMEM)
 
     return pl.pallas_call(
         body,
@@ -118,11 +117,11 @@
         in_specs=[
             pl.BlockSpec(memory_space=pltpu.SMEM),
             pl.BlockSpec((taken, lines, 1, slots, nodes), lambda side, block: (block, 0, side, 0, 0)),
-            whole(sensitivity.shape), whole(solved.shape), whole(ends.shape), whole(ends.shape), whole(unit.shape),
+            whole, whole, whole, whole, whole,
         ],
         out_specs=(
             pl.BlockSpec((taken, rows, count), lambda side, block: (side * (blocks // taken) + block, 0, 0)),
-            whole((rows, count)),
+            whole,
         ),
         out_shape=(
             jax.ShapeDtypeStruct((sides * blocks, rows, count), F32), jax.ShapeDtypeStruct((rows, count), F32)

time: 142 us -> 142 us (level)
  no operation moved by 1% of the time
where the time goes in v11:
time: 142 us; the launch traced here: 141 us
  blocking collectives  73.3 us (52%)
  starting transfers between devices  20.3 us (14%)
  waiting for transfers between devices  15.3 us (11%)
  Pallas kernels  14.2 us (10%)
  between operations  13.6 us (10%)
  other arithmetic  2.13 us (2%)
  local copies, waits for them, and re-layouts  1.71 us (1%)
    all_gather x1, blocking collectives, on_device(): lax.all_gather(jnp.concatenate([block, cap_part + take[BR:]], axis=0), 'r...  44.7 us
    all_to_all x1, blocking collectives, on_device(): lax.all_to_all(packed.astype(jnp.float16), 'col', 0, 0, tiled=True)  21.6 us
    ppermute x1, starting transfers between devices, on_device(): other = lax.ppermute(mine, 'row', OTHER_CORE)  9.21 us
    all_to_all x1, waiting for transfers between devices, on_device(): parts = lax.all_to_all(copies, 'col', 0, 0, tiled=True)  9.05 us
    pallas_call x1, Pallas kernels, products(): pl.pallas_call(body, grid=(sides, blocks // taken), in_specs=[pl.BlockSpe...  8.03 us
    all_to_all x1, starting transfers between devices, on_device(): parts = lax.all_to_all(copies, 'col', 0, 0, tiled=True)  7.22 us
    all_gather x1, blocking collectives, on_device(): pair = lax.all_gather(loads, 'row', axis_index_groups=ALONG_Y, axis=0)  7 us
    pallas_call x1, Pallas kernels, solve(): pl.pallas_call(body, out_shape=out_shape, compiler_params=params)  4.28 us
  transfers between devices with their start and end apart: 5, of which 5 were waited for; matrix products, arithmetic and copies ran while one was open for 1% of the time, Pallas kernels for 4%

profile of v11, /device:TPU:1, one launch (start us, length us, event | category | flops | bytes accessed | tf_op | source)
XLA Modules:
  0.0 141.2 jit_solution(12932517846768227020)
XLA Ops:
  6.5 0.0 all-gather.5.cloned.1.call-start
  6.5 7.0 %all-gather = bf16[64,2048]{1,0:T(8,128)(2,1)} all-gather(bf16[32,2048]{1,0:T(8,128)(2,1)} %bitcast.23), channel_id=2, replica_groups={{0,256},{8,264},{16,272},{24,280},{32,288},{40,296},{48,304},{56,312},{..., dimensions={0}, use_global_device_ids=true | all-gather | bytes 393216 | tf_op jit(solution)/shard_map/all_gather | solution.py:194
  13.5 0.0 all-gather.5.cloned.1.call-update
  13.6 0.7 fusion.16.ends_ref
  14.3 1.6 %copy-done = f32[256,2048]{1,0:T(8,128)S(1)} copy-done((f32[256,2048]{1,0:T(8,128)S(1)}, f32[256,2048]{1,0:T(8,128)}, u32[]{:S(2)}) %copy-start) | copy-done | bytes 2097176
  15.8 1.9 %shard_map.64 = f32[8,72,256]{2,1,0:T(8,128)} custom-call(f32[256,2048]{1,0:T(8,128)S(1)} %copy-done, f32[2,64]{1,0:T(2,128)S(1)} %fusion.16.ends_ref), custom_call_target="tpu_custom_call" | custom-call | tf_op jit(solution)/shard_map/pallas_call | solution.py:67
  17.8 7.2 %all-to-all-start = ((f32[8,72,256]{2,1,0:T(8,128)}), f32[8,72,256]{2,1,0:T(8,128)S(1)}, u32[]{:S(2)}, u32[]{:S(2)}) async-start(f32[8,72,256]{2,1,0:T(8,128)} %shard_map.64), calls=%async_computation | async-start | bytes 1179648 | tf_op jit(solution)/shard_map/all_to_all | solution.py:201
  25.0 9.1 %all-to-all-done = f32[8,72,256]{2,1,0:T(8,128)S(1)} async-done(((f32[8,72,256]{2,1,0:T(8,128)}), f32[8,72,256]{2,1,0:T(8,128)S(1)}, u32[]{:S(2)}, u32[]{:S(2)}) %all-to-all-start) | async-done | bytes 589856 | tf_op jit(solution)/shard_map/all_to_all | solution.py:201
  34.1 0.0 copy-done.4
  34.1 0.3 fusion.1
  34.4 0.3 fusion.3
  34.7 0.1 maximum_maximum_fusion
  34.8 1.9 %collective-permute-start = (f32[104,128]{1,0:T(8,128)S(1)}, f32[104,128]{1,0:T(8,128)S(1)}, u32[]{:S(2)}, u32[]{:S(2)}) collective-permute-start(f32[104,128]{1,0:T(8,128)S(1)} %maximum_maximum_fusion), channel_id=1, source_target_pairs={{0,256},{8,264},{16,272},{24,280},{32,288},{40,296},{48,304},{56,3... | collective-permute-start | bytes 159752 | tf_op jit(solution)/shard_map/ppermute | solution.py:212
  36.7 3.3 %collective-permute-done = f32[104,128]{1,0:T(8,128)S(1)} collective-permute-done((f32[104,128]{1,0:T(8,128)S(1)}, f32[104,128]{1,0:T(8,128)S(1)}, u32[]{:S(2)}, u32[]{:S(2)}) %collective-permute-start) | collective-permute-done | bytes 53280 | tf_op jit(solution)/shard_map/ppermute | solution.py:212
  40.1 0.1 slice_add_fusion
  40.2 0.0 copy-start.2
  40.2 0.0 copy-start.3
  40.2 44.7 %all-gather.2 = f32[1664,128]{1,0:T(8,128)S(1)} all-gather(f32[104,128]{1,0:T(8,128)S(1)} %pad_maximum_fusion.1), channel_id=4, replica_groups={{0,16,32,48,64,80,96,112,128,144,160,176,192,208,224,240},{8,24,40,56,7..., dimensions={0}, use_global_device_ids=true | all-gather | bytes 905216 | tf_op jit(solution)/shard_map/all_gather | solution.py:215
  85.0 9.2 %collective-permute-start.1 = (f32[296,128]{1,0:T(8,128)S(1)}, f32[296,128]{1,0:T(8,128)S(1)}, u32[]{:S(2)}, u32[]{:S(2)}) collective-permute-start(f32[296,128]{1,0:T(8,128)S(1)} %pad_maximum_fusion.mine_ref), channel_id=1, source_target_pairs={{0,8},{8,0},{16,24},{24,16},{32,40},{40,32},{48,56},{56,48},{64,72... | collective-permute-start | bytes 454664 | tf_op jit(solution)/shard_map/ppermute | solution.py:221
  94.3 1.0 collective-permute-done.1.other_ref
  95.3 0.1 fusion.18
  95.4 1.9 %collective-permute-start.2 = (f16[2,4,64,128]{3,2,1,0:T(8,128)(2,1)S(1)}, f16[2,4,64,128]{3,2,1,0:T(8,128)(2,1)S(1)}, u32[]{:S(2)}, u32[]{:S(2)}) collective-permute-start(f16[2,4,64,128]{3,2,1,0:T(8,128)(2,1)S(1)} %get-tuple-element.13), channel_id=1, source_target_pairs={{0,256},{8,264},{16,272},{24,280},{32,288},{40,296},{48,304},{56,3... | collective-permute-start | bytes 393224 | tf_op jit(solution)/shard_map/ppermute | solution.py:225
  97.3 0.0 copy-done.2
  97.3 0.0 copy-done.3
  97.3 4.3 %shard_map.65 = (f32[64,256]{1,0:T(8,128)S(1)}, f32[1,256]{1,0:T(1,128)S(1)}) custom-call(f32[296,128]{1,0:T(8,128)S(1)} %pad_maximum_fusion.mine_ref, f32[296,128]{1,0:T(8,128)S(1)} %collective-permute-done.1.other_ref, f32[1,64]{1,0:T(1,128)S(1)} %bitcast.15, s32[1,64]{1,0:T(1,128)S(1)} %bitcast.16, f32[72,256]{1,0:T(8,128)S(1)} %reduce_sum.27.parts_ref), custom_call_target="tpu_custom_call" | custom-call | tf_op jit(solution)/shard_map/pallas_call | solution.py:183
  101.6 0.4 collective-permute-done.2
  102.0 1.6 %all-gather.5.cloned.1.call-done = bf16[64,32,2048]{2,1,0:T(8,128)(2,1)} async-done(((bf16[2,32,2048]{2,1,0:T(8,128)(2,1)}), bf16[64,32,2048]{2,1,0:T(8,128)(2,1)}) %all-gather.5.cloned.1.call-update) | async-done | bytes 8388624 | tf_op jit(solution)/shard_map/all_gather | solution.py:199
  103.6 8.0 %shard_map.66 = (f32[8,256,256]{2,1,0:T(8,128)S(1)}, f32[256,256]{1,0:T(8,128)S(1)}) custom-call(s32[1]{0:T(128)} %bitcast.y_ref, bf16[4,8,2,32,2048]{4,3,2,1,0:T(8,128)(2,1)} %bitcast.17, f32[256,2048]{1,0:T(8,128)S(1)} %copy-done.1, f32[64,256]{1,0:T(8,128)S(1)} %get-tuple-element.9.solved_ref, f32[2,4,64,128]{3,2,1,0:T(8,128)S(1)} %get-tuple-element.14.ends_ref, ...), custom_call_target="tpu_custom_call" | custom-call | tf_op jit(solution)/shard_map/pallas_call | solution.py:114
  111.7 0.2 convert_element_type.26
  111.9 21.6 %all_to_all.10 = f16[8,256,256]{2,1,0:T(8,128)(2,1)S(1)} all-to-all(f16[8,256,256]{2,1,0:T(8,128)(2,1)S(1)} %convert_element_type.26), channel_id=1, replica_groups=mesh['row'=64,'col'=8] {'col'}, dimensions={0} | all-to-all | bytes 2097152 | tf_op jit(solution)/shard_map/all_to_all | solution.py:232
  133.4 0.1 convert_reduce_fusion
  133.6 0.7 mul.25
  (20 shorter events, 0.2 us)
Async XLA Ops:
  6.5 97.1 %all-gather.5.cloned.1.call-start = ((), (), s32[]{:S(2)}) async-start(), calls=%async_computation.2 | async-start | bytes 8650752 | tf_op jit(solution)/shard_map/all_gather | solution.py:199
  14.3 1.6 %copy-start = (f32[256,2048]{1,0:T(8,128)S(1)}, f32[256,2048]{1,0:T(8,128)}, u32[]{:S(2)}) copy-start(f32[256,2048]{1,0:T(8,128)} %values_ref.3) | copy-start | bytes 6291460
  15.8 18.2 %copy-start.4 = (s32[64]{0:T(128)S(1)}, s32[64]{0:T(128)}, u32[]{:S(2)}) copy-start(s32[64]{0:T(128)} %param.9) | copy-start | bytes 772
  15.8 18.3 %copy-start.5 = (s32[64]{0:T(128)S(1)}, s32[64]{0:T(128)}, u32[]{:S(2)}) copy-start(s32[64]{0:T(128)} %param.8) | copy-start | bytes 772
  17.8 16.3 %all-to-all-start = ((f32[8,72,256]{2,1,0:T(8,128)}), f32[8,72,256]{2,1,0:T(8,128)S(1)}, u32[]{:S(2)}, u32[]{:S(2)}) async-start(f32[8,72,256]{2,1,0:T(8,128)} %shard_map.64), calls=%async_computation | async-start | bytes 1179648 | tf_op jit(solution)/shard_map/all_to_all | solution.py:201
  34.8 5.3 %collective-permute-start = (f32[104,128]{1,0:T(8,128)S(1)}, f32[104,128]{1,0:T(8,128)S(1)}, u32[]{:S(2)}, u32[]{:S(2)}) collective-permute-start(f32[104,128]{1,0:T(8,128)S(1)} %maximum_maximum_fusion), channel_id=1, source_target_pairs={{0,256},{8,264},{16,272},{24,280},{32,288},{40,296},{48,304},{56,3... | collective-permute-start | bytes 159752 | tf_op jit(solution)/shard_map/ppermute | solution.py:212
  40.2 57.2 %copy-start.2 = (f32[64]{0:T(128)S(1)}, f32[64]{0:T(128)}, u32[]{:S(2)}) copy-start(f32[64]{0:T(128)} %param.11) | copy-start | bytes 772
  40.2 57.2 %copy-start.3 = (s32[64]{0:T(128)S(1)}, s32[64]{0:T(128)}, u32[]{:S(2)}) copy-start(s32[64]{0:T(128)} %param.10) | copy-start | bytes 772
  84.9 18.7 %copy-start.1 = (f32[256,2048]{1,0:T(8,128)S(1)}, f32[256,2048]{1,0:T(8,128)}, u32[]{:S(2)}) copy-start(f32[256,2048]{1,0:T(8,128)} %values_ref.3) | copy-start | bytes 6291460
  85.0 10.2 %collective-permute-start.1 = (f32[296,128]{1,0:T(8,128)S(1)}, f32[296,128]{1,0:T(8,128)S(1)}, u32[]{:S(2)}, u32[]{:S(2)}) collective-permute-start(f32[296,128]{1,0:T(8,128)S(1)} %pad_maximum_fusion.mine_ref), channel_id=1, source_target_pairs={{0,8},{8,0},{16,24},{24,16},{32,40},{40,32},{48,56},{56,48},{64,72... | collective-permute-start | bytes 454664 | tf_op jit(solution)/shard_map/ppermute | solution.py:221
  95.4 6.6 %collective-permute-start.2 = (f16[2,4,64,128]{3,2,1,0:T(8,128)(2,1)S(1)}, f16[2,4,64,128]{3,2,1,0:T(8,128)(2,1)S(1)}, u32[]{:S(2)}, u32[]{:S(2)}) collective-permute-start(f16[2,4,64,128]{3,2,1,0:T(8,128)(2,1)S(1)} %get-tuple-element.13), channel_id=1, source_target_pairs={{0,256},{8,264},{16,272},{24,280},{32,288},{40,296},{48,304},{56,3... | collective-permute-start | bytes 393224 | tf_op jit(solution)/shard_map/ppermute | solution.py:225
Sparse Core Ops, SparseCore 0:
  13.7 89.9 all-gather.4

commit v12 on v11

--- a/solution.py
+++ b/solution.py
@@ -82,7 +82,7 @@
         high = values.astype(BF16)
         return high, (values - high.astype(F32)).astype(BF16)
 
-    def body(y_ref, loads_ref, values_ref, solved_ref, ends_ref, other_ref, unit_ref, out_ref, units_ref, both, inverse, ends_high, ends_low):
+    def body(y_ref, loads_ref, values_ref, solved_ref, ends_ref, other_ref, unit_ref, out_ref, units_ref, both, inverse, stacked):
         @pl.when((pl.program_id(0) == 0) & (pl.program_id(1) == 0))
         def _():
             first = y_ref[0] == 0
@@ -91,14 +91,16 @@
                     mine, other = ends_ref[core, place], other_ref[core, place]
                     at = (place * cores + core) * 2 * half
                     for piece in (jnp.where(first, mine, other), jnp.where(first, other, mine)):
-                        ends_high[:, at:at + half], ends_low[:, at:at + half] = split_here(piece)
+                        high, low = split_here(piece)
+                        stacked[:BR, at:at + half] = high
+                        stacked[BR:2 * BR, at:at + half] = low
+                        stacked[2 * BR:, at:at + half] = high
                         at += half
             solved_high, solved_low = split_here(solved_ref[...].T)
+            solved_parts = jnp.concatenate([solved_high, solved_high, solved_low], axis=1)
             for at in range(0, nodes, 512):
                 here = slice(at, at + 512)
-                drop = jnp.dot(solved_high, ends_high[:, here], preferred_element_type=F32)
-                drop += jnp.dot(solved_high, ends_low[:, here], preferred_element_type=F32)
-                drop += jnp.dot(solved_low, ends_high[:, here], preferred_element_type=F32)
+                drop = jnp.dot(solved_parts, stacked[:, here], preferred_element_type=F32)
                 both[:rows, here], both[rows:, here] = split_here(values_ref[:, here] - drop)
             units_ref[...] = jnp.broadcast_to(unit_ref[...], (count, rows)).T
             inverse[...] = 1.0 / units_ref[...]
@@ -128,7 +130,7 @@
         ),
         scratch_shapes=[
             pltpu.VMEM((2 * rows, nodes), BF16), pltpu.VMEM((rows, count), F32),
-            pltpu.VMEM((BR, nodes), BF16), pltpu.VMEM((BR, nodes), BF16),
+            pltpu.VMEM((3 * BR, nodes), BF16),
         ],
         compiler_params=pltpu.CompilerParams(vmem_limit_bytes=48 * 1024 * 1024),
     )(y.astype(jnp.int32).reshape(1), loads, sensitivity, solved, ends, other_ends, unit)

time: 142 us -> 141 us (level)
  no operation moved by 1% of the time
where the time goes in v12:
time: 141 us
  blocking collectives  73.3 us (52%)
  starting transfers between devices  20.3 us (14%)
  waiting for transfers between devices  15.3 us (11%)
  Pallas kernels  13.9 us (10%)
  between operations  13.6 us (10%)
  other arithmetic  2.13 us (2%)
  local copies, waits for them, and re-layouts  1.71 us (1%)
    all_gather x1, blocking collectives, on_device(): lax.all_gather(jnp.concatenate([block, cap_part + take[BR:]], axis=0), 'r...  44.7 us
    all_to_all x1, blocking collectives, on_device(): lax.all_to_all(packed.astype(jnp.float16), 'col', 0, 0, tiled=True)  21.6 us
    ppermute x1, starting transfers between devices, on_device(): other = lax.ppermute(mine, 'row', OTHER_CORE)  9.21 us
    all_to_all x1, waiting for transfers between devices, on_device(): parts = lax.all_to_all(copies, 'col', 0, 0, tiled=True)  9.05 us
    pallas_call x1, Pallas kernels, products(): pl.pallas_call(body, grid=(sides, blocks // taken), in_specs=[pl.BlockSpe...  7.68 us
    all_to_all x1, starting transfers between devices, on_device(): parts = lax.all_to_all(copies, 'col', 0, 0, tiled=True)  7.22 us
    all_gather x1, blocking collectives, on_device(): pair = lax.all_gather(loads, 'row', axis_index_groups=ALONG_Y, axis=0)  7 us
    pallas_call x1, Pallas kernels, solve(): pl.pallas_call(body, out_shape=out_shape, compiler_params=params)  4.28 us
  transfers between devices with their start and end apart: 5, of which 5 were waited for; matrix products, arithmetic and copies ran while one was open for 1% of the time, Pallas kernels for 4%

profile of v12, /device:TPU:1, one launch (start us, length us, event | category | flops | bytes accessed | tf_op | source)
XLA Modules:
  0.0 140.8 jit_solution(17526739047567128041)
XLA Ops:
  6.5 0.0 all-gather.5.cloned.1.call-start
  6.5 7.0 %all-gather = bf16[64,2048]{1,0:T(8,128)(2,1)} all-gather(bf16[32,2048]{1,0:T(8,128)(2,1)} %bitcast.23), channel_id=2, replica_groups={{0,256},{8,264},{16,272},{24,280},{32,288},{40,296},{48,304},{56,312},{..., dimensions={0}, use_global_device_ids=true | all-gather | bytes 393216 | tf_op jit(solution)/shard_map/all_gather | solution.py:196
  13.5 0.0 all-gather.5.cloned.1.call-update
  13.6 0.7 fusion.16.ends_ref
  14.3 1.6 %copy-done = f32[256,2048]{1,0:T(8,128)S(1)} copy-done((f32[256,2048]{1,0:T(8,128)S(1)}, f32[256,2048]{1,0:T(8,128)}, u32[]{:S(2)}) %copy-start) | copy-done | bytes 2097176
  15.8 1.9 %shard_map.64 = f32[8,72,256]{2,1,0:T(8,128)} custom-call(f32[256,2048]{1,0:T(8,128)S(1)} %copy-done, f32[2,64]{1,0:T(2,128)S(1)} %fusion.16.ends_ref), custom_call_target="tpu_custom_call" | custom-call | tf_op jit(solution)/shard_map/pallas_call | solution.py:67
  17.8 7.2 %all-to-all-start = ((f32[8,72,256]{2,1,0:T(8,128)}), f32[8,72,256]{2,1,0:T(8,128)S(1)}, u32[]{:S(2)}, u32[]{:S(2)}) async-start(f32[8,72,256]{2,1,0:T(8,128)} %shard_map.64), calls=%async_computation | async-start | bytes 1179648 | tf_op jit(solution)/shard_map/all_to_all | solution.py:203
  25.0 9.1 %all-to-all-done = f32[8,72,256]{2,1,0:T(8,128)S(1)} async-done(((f32[8,72,256]{2,1,0:T(8,128)}), f32[8,72,256]{2,1,0:T(8,128)S(1)}, u32[]{:S(2)}, u32[]{:S(2)}) %all-to-all-start) | async-done | bytes 589856 | tf_op jit(solution)/shard_map/all_to_all | solution.py:203
  34.1 0.0 copy-done.4
  34.1 0.3 fusion.1
  34.4 0.3 fusion.3
  34.7 0.1 maximum_maximum_fusion
  34.8 1.9 %collective-permute-start = (f32[104,128]{1,0:T(8,128)S(1)}, f32[104,128]{1,0:T(8,128)S(1)}, u32[]{:S(2)}, u32[]{:S(2)}) collective-permute-start(f32[104,128]{1,0:T(8,128)S(1)} %maximum_maximum_fusion), channel_id=1, source_target_pairs={{0,256},{8,264},{16,272},{24,280},{32,288},{40,296},{48,304},{56,3... | collective-permute-start | bytes 159752 | tf_op jit(solution)/shard_map/ppermute | solution.py:214
  36.7 3.3 %collective-permute-done = f32[104,128]{1,0:T(8,128)S(1)} collective-permute-done((f32[104,128]{1,0:T(8,128)S(1)}, f32[104,128]{1,0:T(8,128)S(1)}, u32[]{:S(2)}, u32[]{:S(2)}) %collective-permute-start) | collective-permute-done | bytes 53280 | tf_op jit(solution)/shard_map/ppermute | solution.py:214
  40.1 0.1 slice_add_fusion
  40.2 0.0 copy-start.2
  40.2 0.0 copy-start.3
  40.2 44.7 %all-gather.2 = f32[1664,128]{1,0:T(8,128)S(1)} all-gather(f32[104,128]{1,0:T(8,128)S(1)} %pad_maximum_fusion.1), channel_id=4, replica_groups={{0,16,32,48,64,80,96,112,128,144,160,176,192,208,224,240},{8,24,40,56,7..., dimensions={0}, use_global_device_ids=true | all-gather | bytes 905216 | tf_op jit(solution)/shard_map/all_gather | solution.py:217
  85.0 9.2 %collective-permute-start.1 = (f32[296,128]{1,0:T(8,128)S(1)}, f32[296,128]{1,0:T(8,128)S(1)}, u32[]{:S(2)}, u32[]{:S(2)}) collective-permute-start(f32[296,128]{1,0:T(8,128)S(1)} %pad_maximum_fusion.mine_ref), channel_id=1, source_target_pairs={{0,8},{8,0},{16,24},{24,16},{32,40},{40,32},{48,56},{56,48},{64,72... | collective-permute-start | bytes 454664 | tf_op jit(solution)/shard_map/ppermute | solution.py:223
  94.3 1.0 collective-permute-done.1.other_ref
  95.3 0.1 fusion.18
  95.4 1.9 %collective-permute-start.2 = (f16[2,4,64,128]{3,2,1,0:T(8,128)(2,1)S(1)}, f16[2,4,64,128]{3,2,1,0:T(8,128)(2,1)S(1)}, u32[]{:S(2)}, u32[]{:S(2)}) collective-permute-start(f16[2,4,64,128]{3,2,1,0:T(8,128)(2,1)S(1)} %get-tuple-element.13), channel_id=1, source_target_pairs={{0,256},{8,264},{16,272},{24,280},{32,288},{40,296},{48,304},{56,3... | collective-permute-start | bytes 393224 | tf_op jit(solution)/shard_map/ppermute | solution.py:227
  97.3 0.0 copy-done.2
  97.3 0.0 copy-done.3
  97.3 4.3 %shard_map.65 = (f32[64,256]{1,0:T(8,128)S(1)}, f32[1,256]{1,0:T(1,128)S(1)}) custom-call(f32[296,128]{1,0:T(8,128)S(1)} %pad_maximum_fusion.mine_ref, f32[296,128]{1,0:T(8,128)S(1)} %collective-permute-done.1.other_ref, f32[1,64]{1,0:T(1,128)S(1)} %bitcast.15, s32[1,64]{1,0:T(1,128)S(1)} %bitcast.16, f32[72,256]{1,0:T(8,128)S(1)} %reduce_sum.27.parts_ref), custom_call_target="tpu_custom_call" | custom-call | tf_op jit(solution)/shard_map/pallas_call | solution.py:185
  101.6 0.4 collective-permute-done.2
  102.0 1.6 %all-gather.5.cloned.1.call-done = bf16[64,32,2048]{2,1,0:T(8,128)(2,1)} async-done(((bf16[2,32,2048]{2,1,0:T(8,128)(2,1)}), bf16[64,32,2048]{2,1,0:T(8,128)(2,1)}) %all-gather.5.cloned.1.call-update) | async-done | bytes 8388624 | tf_op jit(solution)/shard_map/all_gather | solution.py:201
  103.6 7.7 %shard_map.66 = (f32[8,256,256]{2,1,0:T(8,128)S(1)}, f32[256,256]{1,0:T(8,128)S(1)}) custom-call(s32[1]{0:T(128)} %bitcast.y_ref, bf16[4,8,2,32,2048]{4,3,2,1,0:T(8,128)(2,1)} %bitcast.17, f32[256,2048]{1,0:T(8,128)S(1)} %copy-done.1, f32[64,256]{1,0:T(8,128)S(1)} %get-tuple-element.9.solved_ref, f32[2,4,64,128]{3,2,1,0:T(8,128)S(1)} %get-tuple-element.14.ends_ref, ...), custom_call_target="tpu_custom_call" | custom-call | tf_op jit(solution)/shard_map/pallas_call | solution.py:116
  111.3 0.2 convert_element_type.26
  111.5 21.6 %all_to_all.10 = f16[8,256,256]{2,1,0:T(8,128)(2,1)S(1)} all-to-all(f16[8,256,256]{2,1,0:T(8,128)(2,1)S(1)} %convert_element_type.26), channel_id=1, replica_groups=mesh['row'=64,'col'=8] {'col'}, dimensions={0} | all-to-all | bytes 2097152 | tf_op jit(solution)/shard_map/all_to_all | solution.py:234
  133.1 0.1 convert_reduce_fusion
  133.2 0.7 mul.25
  (20 shorter events, 0.2 us)
Async XLA Ops:
  6.5 97.1 %all-gather.5.cloned.1.call-start = ((), (), s32[]{:S(2)}) async-start(), calls=%async_computation.2 | async-start | bytes 8650752 | tf_op jit(solution)/shard_map/all_gather | solution.py:201
  14.3 1.6 %copy-start = (f32[256,2048]{1,0:T(8,128)S(1)}, f32[256,2048]{1,0:T(8,128)}, u32[]{:S(2)}) copy-start(f32[256,2048]{1,0:T(8,128)} %values_ref.3) | copy-start | bytes 6291460
  15.8 18.2 %copy-start.4 = (s32[64]{0:T(128)S(1)}, s32[64]{0:T(128)}, u32[]{:S(2)}) copy-start(s32[64]{0:T(128)} %param.9) | copy-start | bytes 772
  15.8 18.3 %copy-start.5 = (s32[64]{0:T(128)S(1)}, s32[64]{0:T(128)}, u32[]{:S(2)}) copy-start(s32[64]{0:T(128)} %param.8) | copy-start | bytes 772
  17.8 16.3 %all-to-all-start = ((f32[8,72,256]{2,1,0:T(8,128)}), f32[8,72,256]{2,1,0:T(8,128)S(1)}, u32[]{:S(2)}, u32[]{:S(2)}) async-start(f32[8,72,256]{2,1,0:T(8,128)} %shard_map.64), calls=%async_computation | async-start | bytes 1179648 | tf_op jit(solution)/shard_map/all_to_all | solution.py:203
  34.8 5.3 %collective-permute-start = (f32[104,128]{1,0:T(8,128)S(1)}, f32[104,128]{1,0:T(8,128)S(1)}, u32[]{:S(2)}, u32[]{:S(2)}) collective-permute-start(f32[104,128]{1,0:T(8,128)S(1)} %maximum_maximum_fusion), channel_id=1, source_target_pairs={{0,256},{8,264},{16,272},{24,280},{32,288},{40,296},{48,304},{56,3... | collective-permute-start | bytes 159752 | tf_op jit(solution)/shard_map/ppermute | solution.py:214
  40.2 57.2 %copy-start.2 = (f32[64]{0:T(128)S(1)}, f32[64]{0:T(128)}, u32[]{:S(2)}) copy-start(f32[64]{0:T(128)} %param.11) | copy-start | bytes 772
  40.2 57.2 %copy-start.3 = (s32[64]{0:T(128)S(1)}, s32[64]{0:T(128)}, u32[]{:S(2)}) copy-start(s32[64]{0:T(128)} %param.10) | copy-start | bytes 772
  84.9 18.7 %copy-start.1 = (f32[256,2048]{1,0:T(8,128)S(1)}, f32[256,2048]{1,0:T(8,128)}, u32[]{:S(2)}) copy-start(f32[256,2048]{1,0:T(8,128)} %values_ref.3) | copy-start | bytes 6291460
  85.0 10.2 %collective-permute-start.1 = (f32[296,128]{1,0:T(8,128)S(1)}, f32[296,128]{1,0:T(8,128)S(1)}, u32[]{:S(2)}, u32[]{:S(2)}) collective-permute-start(f32[296,128]{1,0:T(8,128)S(1)} %pad_maximum_fusion.mine_ref), channel_id=1, source_target_pairs={{0,8},{8,0},{16,24},{24,16},{32,40},{40,32},{48,56},{56,48},{64,72... | collective-permute-start | bytes 454664 | tf_op jit(solution)/shard_map/ppermute | solution.py:223
  95.4 6.6 %collective-permute-start.2 = (f16[2,4,64,128]{3,2,1,0:T(8,128)(2,1)S(1)}, f16[2,4,64,128]{3,2,1,0:T(8,128)(2,1)S(1)}, u32[]{:S(2)}, u32[]{:S(2)}) collective-permute-start(f16[2,4,64,128]{3,2,1,0:T(8,128)(2,1)S(1)} %get-tuple-element.13), channel_id=1, source_target_pairs={{0,256},{8,264},{16,272},{24,280},{32,288},{40,296},{48,304},{56,3... | collective-permute-start | bytes 393224 | tf_op jit(solution)/shard_map/ppermute | solution.py:227
Sparse Core Ops, SparseCore 0:
  13.7 89.9 all-gather.4
